TPU v7x, 512 devices: a whole 4x8x8 slice. The times are simulated.
512 devices in a mesh: seq: 64 (over y, z), chan: 8 (over x, core).
Axes of the slice: x: 4, y: 8, z: 8, core: 2. Of those that a mesh axis runs over, the one named last changes fastest.
Arguments:
- tokens: bfloat16 [16384, 8192], P('seq', 'chan'), may hold values from -6 to 6
- in_weight: bfloat16 [8192, 3, 2048], P('seq', None, 'chan')
- rate: float32 [2048, 16], P('chan'), as said below
- residue: float32 [2048, 16], P('chan')
- skip_gain: float32 [2048], P('chan'), may hold values from 0.5 to 1.5
Outputs:
- mixed: bfloat16 [16384, 2048], P('seq', 'chan')
- state_unit: float32 [2048, 16], P(('chan', 'seq'))
- state_scale: float32 [2048], P(('chan', 'seq'))
Inputs may be any that keep to these rules, and one draw needn't show every extreme that they name: rate is positive and below 1/25.
All inputs are finite; a program needn't handle non-finite values. Where the computation divides by a largest or mean magnitude, that divisor is 1e-20 or more.
Results may differ from a plain program's by a relative error of at most 0.0096.
Values may be sent and summed in bfloat16 or wider, within the bound.
No kernel may reach another device: no remote copies, remote signals or barrier semaphores. Data moves between devices by JAX's collectives and lax.ppermute only.
A program may use at most 64 MiB of HBM per device.

v0:
```python
import jax
import jax.numpy as jnp
from jax import lax
from jax.sharding import PartitionSpec as P

HIGHEST_MODE = lax.Precision.HIGHEST


def carried_in(array, axis, combine, identity):
    size, place = (lax.axis_size(axis), lax.axis_index(axis))
    everything = jax.tree.map(lambda part: lax.all_gather(part, axis), array)
    start = jax.tree.map(
        lambda part, zero: jnp.broadcast_to(jnp.asarray(zero, part.dtype), part.shape),
        array,
        identity,
    )

    def hop(k, before):
        reached = k < place
        new = combine(before, jax.tree.map(lambda part: part[k], everything))
        return jax.tree.map(lambda a, b: jnp.where(reached, a, b), new, before)

    return lax.fori_loop(0, size, hop, start)


def combine_state(earlier, later):
    return (earlier[0] * later[1] + later[0], earlier[1] * later[1])


def shards(tokens, in_weight, rate, residue, skip_gain):
    local_rows = tokens.shape[0]
    width = rate.shape[0]
    poles_here = rate.shape[1]
    weights_all = lax.all_gather(in_weight, "seq", axis=0, tiled=True)
    projected = jnp.einsum(
        "td,dgc->tgc",
        lax.all_gather(tokens, "chan", axis=1, tiled=True),
        weights_all,
        preferred_element_type=jnp.float32,
    )
    projected = projected.astype(jnp.bfloat16)
    query = projected[:, 0].astype(jnp.float32)
    drive = projected[:, 1].astype(jnp.float32) * projected[:, 2].astype(jnp.float32)
    block = 128
    count = local_rows // block
    group = 64
    groups = width // group
    steps_in = jnp.arange(block, dtype=jnp.float32)
    rate_col = rate[:, :, None]
    left = residue[:, :, None] * jnp.exp(-rate_col * steps_in)
    right = jnp.exp(rate_col * steps_in)
    lower = (steps_in[:, None] >= steps_in[None, :]).astype(jnp.float32)
    drive_cols = drive.T.reshape(groups, group, count, block)
    left_groups = left.reshape(groups, group, poles_here, block)
    right_groups = right.reshape(groups, group, poles_here, block)

    def inner_group(operands):
        left_part, right_part, drive_part = operands
        toeplitz = (
            jnp.einsum("cnt,cns->cts", left_part, right_part, precision=HIGHEST_MODE) * lower[None]
        )
        return jnp.einsum("cts,cbs->cbt", toeplitz, drive_part, precision=HIGHEST_MODE)

    inner = lax.map(inner_group, (left_groups, right_groups, drive_cols))
    inner = inner.reshape(width, local_rows).T
    blocked = drive.reshape(count, block, width)
    end_decay = jnp.exp(-rate_col * (block - 1 - steps_in))
    block_states = jnp.einsum("cns,bsc->bcn", end_decay, blocked, precision=HIGHEST_MODE)
    later_idx = jnp.arange(count + 1, dtype=jnp.float32)[:, None]
    earlier_idx = jnp.arange(count, dtype=jnp.float32)[None, :]
    gap = jnp.maximum(later_idx - 1.0 - earlier_idx, 0.0)
    valid = (earlier_idx < later_idx).astype(jnp.float32)
    jump = jnp.exp(-rate[None, None] * block * gap[:, :, None, None]) * valid[:, :, None, None]
    prefix_local = jnp.einsum("abcn,bcn->acn", jump, block_states, precision=HIGHEST_MODE)
    own = prefix_local[count]
    span = jnp.exp(-rate * local_rows)
    zeros_state = jnp.zeros_like(own)
    ones_state = jnp.ones_like(own)
    incoming, _ = carried_in((own, span), "seq", combine_state, (zeros_state, ones_state))
    start_decay = jnp.exp(-rate[None] * block * jnp.arange(count, dtype=jnp.float32)[:, None, None])
    entering = prefix_local[:count] + start_decay * incoming[None]
    after = residue[:, :, None] * jnp.exp(-rate_col * (steps_in + 1.0))
    carried = jnp.einsum("cni,bcn->bic", after, entering, precision=HIGHEST_MODE)
    conv = inner + carried.reshape(local_rows, width)
    mixed = (query * (conv + skip_gain[None, :] * drive)).astype(jnp.bfloat16)
    position = lax.axis_index("seq")
    devices = lax.axis_size("seq")
    remaining = (local_rows * devices - (position + 1) * local_rows).astype(jnp.float32)
    term = own * jnp.exp(-rate * remaining)
    state = lax.psum_scatter(term, "seq", scatter_dimension=0, tiled=True)
    top = jnp.maximum(jnp.max(jnp.abs(state), axis=1), 1.0)
    return (mixed, state / top[:, None], top / 127.0)


def solution(mesh):
    in_specs = (
        P("seq", "chan"),
        P("seq", None, "chan"),
        P("chan", None),
        P("chan", None),
        P("chan"),
    )
    out_specs = (P("seq", "chan"), P(("chan", "seq"), None), P(("chan", "seq")))
    return jax.shard_map(shards, mesh=mesh, in_specs=in_specs, out_specs=out_specs, check_vma=False)
```

profile of v0, /device:TPU:6, one launch (start us, length us, event | category | flops | bytes accessed | tf_op | source)
XLA Modules:
  0.0 596.5 jit_solution(6088122542587803011)
XLA Ops:
  9.7 40.6 %all-gather.6.cloned.1.call-done = bf16[256,8192]{1,0:T(8,128)(2,1)} async-done(((bf16[256,1024]{1,0:T(8,128)(2,1)}), bf16[256,8192]{1,0:T(8,128)(2,1)}) %all-gather.6.cloned.1.call-update) | async-done | bytes 4194320 | tf_op jit(solution)/shard_map/all_gather | solution.py:37
  50.3 124.6 %all-gather.8.cloned.1.call-done = bf16[8192,3,256]{2,0,1:T(8,128)(2,1)} async-done(((bf16[128,3,256]{2,0,1:T(8,128)(2,1)}), bf16[8192,3,256]{2,0,1:T(8,128)(2,1)}) %all-gather.8.cloned.1.call-update) | async-done | bytes 12582928 | tf_op jit(solution)/shard_map/all_gather | solution.py:34
  174.9 9.2 %fusion.33 = bf16[256,3,256]{2,0,1:T(8,128)(2,1)S(1)} fusion(bf16[8192,3,256]{2,0,1:T(8,128)(2,1)} %all-gather.8.cloned.1.call-done, bf16[256,8192]{1,0:T(8,128)(2,1)} %all-gather.6.cloned.1.call-done), kind=kOutput, calls=%fused_computation.33 | convolution fusion | flops 3221422080 | bytes 17170432 | tf_op jit(solution)/shard_map/td,dgc->tgc/dot_general | solution.py:35
  184.4 3.4 fusion.36
  189.2 1.3 dynamic-slice
  191.2 3.0 multiply_exponential_fusion
  195.1 60.3 %while.25 = (s32[]{:T(128)}, f32[4,64,2,128]{3,2,1,0:T(2,128)}, f32[4,64,2,128]{3,2,1,0:T(2,128)S(1)}, f32[4,64,16,128]{3,2,1,0:T(8,128)}, f32[4,64,16,128]{3,2,1,0:T(8,128)S(1)}, /*index=5*/s32[]{:T(128)}) while((s32[]{:T(128)}, f32[4,64,2,128]{3,2,1,0:T(2,128)}, f32[4,64,2,128]{3,2,1,0:T(2,128)S(1)}, ...), condition=%wide.region_1.2_spmd.clone, body=%wide.region_0.1_spmd.clone.sunk | while | flops 227573760 | bytes 9701453 | solution.py:64
  195.3 7.8 %fusion.66 = f32[64,128,128]{2,1,0:T(8,128)S(1)} fusion(f32[4,64,16,128]{3,2,1,0:T(8,128)S(1)} %get-tuple-element.310, s32[]{:T(128)S(6)} %copy.79, f32[4,64,16,128]{3,2,1,0:T(8,128)} %get-tuple-element.309), kind=kOutput, calls=%fused_computation.6.clone.1 | convolution fusion | flops 201326592 | bytes 5243904 | tf_op jit(solution)/shard_map/while/body/eval_jaxpr/cnt,cns->cts/dot_general | solution.py:60
  203.1 7.2 %fusion.68 = f32[4,64,2,128]{3,2,1,0:T(2,128)} fusion(f32[4,64,2,128]{3,2,1,0:T(2,128)} %get-tuple-element.301, s32[]{:T(128)S(6)} %copy.79, f32[64,128,128]{2,1,0:T(8,128)S(1)} %fusion.66, f32[128,128]{1,0:T(8,128)S(1)} %fusion.67, f32[4,64,2,128]{3,2,1,0:T(2,128)S(1)} %get-tuple-element.308), kind=kOutput, calls=%fused_computation.5.clone.1 | convolution fusion | flops 26214400 | bytes 4391936 | tf_op jit(solution)/shard_map/while/body/eval_jaxpr/cts,cbs->cbt/dot_general | solution.py:62
  210.3 7.8 %fusion.66 = f32[64,128,128]{2,1,0:T(8,128)S(1)} fusion(f32[4,64,16,128]{3,2,1,0:T(8,128)S(1)} %get-tuple-element.310, s32[]{:T(128)S(6)} %copy.79, f32[4,64,16,128]{3,2,1,0:T(8,128)} %get-tuple-element.309), kind=kOutput, calls=%fused_computation.6.clone.1 | convolution fusion | flops 201326592 | bytes 5243904 | tf_op jit(solution)/shard_map/while/body/eval_jaxpr/cnt,cns->cts/dot_general | solution.py:60
  218.1 7.3 %fusion.68 = f32[4,64,2,128]{3,2,1,0:T(2,128)} fusion(f32[4,64,2,128]{3,2,1,0:T(2,128)} %get-tuple-element.301, s32[]{:T(128)S(6)} %copy.79, f32[64,128,128]{2,1,0:T(8,128)S(1)} %fusion.66, f32[128,128]{1,0:T(8,128)S(1)} %fusion.67, f32[4,64,2,128]{3,2,1,0:T(2,128)S(1)} %get-tuple-element.308), kind=kOutput, calls=%fused_computation.5.clone.1 | convolution fusion | flops 26214400 | bytes 4391936 | tf_op jit(solution)/shard_map/while/body/eval_jaxpr/cts,cbs->cbt/dot_general | solution.py:62
  225.4 7.8 %fusion.66 = f32[64,128,128]{2,1,0:T(8,128)S(1)} fusion(f32[4,64,16,128]{3,2,1,0:T(8,128)S(1)} %get-tuple-element.310, s32[]{:T(128)S(6)} %copy.79, f32[4,64,16,128]{3,2,1,0:T(8,128)} %get-tuple-element.309), kind=kOutput, calls=%fused_computation.6.clone.1 | convolution fusion | flops 201326592 | bytes 5243904 | tf_op jit(solution)/shard_map/while/body/eval_jaxpr/cnt,cns->cts/dot_general | solution.py:60
  233.2 7.2 %fusion.68 = f32[4,64,2,128]{3,2,1,0:T(2,128)} fusion(f32[4,64,2,128]{3,2,1,0:T(2,128)} %get-tuple-element.301, s32[]{:T(128)S(6)} %copy.79, f32[64,128,128]{2,1,0:T(8,128)S(1)} %fusion.66, f32[128,128]{1,0:T(8,128)S(1)} %fusion.67, f32[4,64,2,128]{3,2,1,0:T(2,128)S(1)} %get-tuple-element.308), kind=kOutput, calls=%fused_computation.5.clone.1 | convolution fusion | flops 26214400 | bytes 4391936 | tf_op jit(solution)/shard_map/while/body/eval_jaxpr/cts,cbs->cbt/dot_general | solution.py:62
  240.4 7.8 %fusion.66 = f32[64,128,128]{2,1,0:T(8,128)S(1)} fusion(f32[4,64,16,128]{3,2,1,0:T(8,128)S(1)} %get-tuple-element.310, s32[]{:T(128)S(6)} %copy.79, f32[4,64,16,128]{3,2,1,0:T(8,128)} %get-tuple-element.309), kind=kOutput, calls=%fused_computation.6.clone.1 | convolution fusion | flops 201326592 | bytes 5243904 | tf_op jit(solution)/shard_map/while/body/eval_jaxpr/cnt,cns->cts/dot_general | solution.py:60
  248.2 7.3 %fusion.68 = f32[4,64,2,128]{3,2,1,0:T(2,128)} fusion(f32[4,64,2,128]{3,2,1,0:T(2,128)} %get-tuple-element.301, s32[]{:T(128)S(6)} %copy.79, f32[64,128,128]{2,1,0:T(8,128)S(1)} %fusion.66, f32[128,128]{1,0:T(8,128)S(1)} %fusion.67, f32[4,64,2,128]{3,2,1,0:T(2,128)S(1)} %get-tuple-element.308), kind=kOutput, calls=%fused_computation.5.clone.1 | convolution fusion | flops 26214400 | bytes 4391936 | tf_op jit(solution)/shard_map/while/body/eval_jaxpr/cts,cbs->cbt/dot_general | solution.py:62
  255.5 1.0 copy.67
  256.7 278.0 %all-reduce = f32[256,16]{1,0:T(8,128)S(1)} all-reduce(f32[256,16]{1,0:T(8,128)S(1)} %copy.42), channel_id=3, replica_groups=mesh['seq'=64,'chan'=8] {'seq'}, use_global_device_ids=true, to_apply=%region_4.5.clone | all-reduce | flops 4096 | bytes 32768
  535.9 1.5 copy.58
  537.5 48.5 %while.26 = (s32[]{:T(128)}, f32[256,16]{0,1:T(8,128)S(1)}, s32[]{:T(128)}, f32[64,256,16]{1,0,2:T(8,128)S(1)}, f32[64,256,16]{1,2,0:T(8,128)}, /*index=5*/s32[]{:T(128)}, s32[]{:T(128)}) while((s32[]{:T(128)}, f32[256,16]{0,1:T(8,128)S(1)}, s32[]{:T(128)}, f32[64,256,16]{1,0,2:T(8,128)S(1)}, f32[64,256,16]{1,2,0:T(8,128)}, ...), condition=%wide.region_3.4_spmd.clone, body=%wide.region_2.3_spmd.clone.sunk | while | flops 16388 | bytes 98417 | solution.py:23
  537.5 0.7 fusion.69
  538.3 0.7 fusion.69
  539.1 0.7 fusion.69
  539.8 0.7 fusion.69
  540.6 0.7 fusion.69
  541.3 0.7 fusion.69
  542.1 0.7 fusion.69
  542.8 0.7 fusion.69
  544.4 0.7 fusion.69
  558.8 0.7 fusion.69
  573.2 0.7 fusion.69
  586.2 2.8 fusion.39
  589.2 0.7 fusion.47
  (166 shorter events, 46.5 us)
Async XLA Ops:
  7.2 43.2 %all-gather.6.cloned.1.call-start = ((), (), s32[]{:S(2)}) async-start(), calls=%async_computation | async-start | bytes 4718592 | tf_op jit(solution)/shard_map/all_gather | solution.py:37
  7.9 167.0 %all-gather.8.cloned.1.call-start = ((), (), s32[]{:S(2)}) async-start(), calls=%async_computation.1 | async-start | bytes 12779520 | tf_op jit(solution)/shard_map/all_gather | solution.py:34
  8.6 527.3 %all-gather.12.cloned.1.call-start = ((), (), s32[]{:S(2)}) async-start(), calls=%async_computation.3 | async-start | bytes 1064960 | tf_op jit(solution)/shard_map/all_gather | solution.py:11
  184.2 4.0 copy-start
  184.4 4.7 copy-start.1
  188.9 348.5 %all-gather.10.cloned.1.call-start = ((), (), s32[]{:S(2)}) async-start(), calls=%async_computation.2 | async-start | bytes 1064960 | tf_op jit(solution)/shard_map/all_gather | solution.py:11
  586.2 3.0 copy-start.2
Sparse Core Ops, SparseCore 0:
  10.1 40.1 all-gather.5
  53.4 121.4 all-gather.7
  189.1 77.7 all-gather.11
  269.8 77.5 all-gather.9
where the time goes:
time: 603 us; the launch traced here: 596 us
  blocking collectives  278 us (46%)
  waiting for transfers between devices  167 us (28%)
  matrix products  75.6 us (13%)
  other arithmetic  53.5 us (9%)
  between operations  14.6 us (2%)
  local copies, waits for them, and re-layouts  6.92 us (1%)
    unnamed x1, blocking collectives  278 us
    all_gather x1, waiting for transfers between devices, shards(): weights_all = lax.all_gather(in_weight, 'seq', axis=0, tiled=True)  125 us
    select_n x64, other arithmetic, hop(): return jax.tree.map(lambda a, b: jnp.where(reached, a, b), new, before)  46.6 us
    all_gather x1, waiting for transfers between devices, shards(): lax.all_gather(tokens, 'chan', axis=1, tiled=True)  40.6 us
    dot_general x4, matrix products, inner_group(): jnp.einsum('cnt,cns->cts', left_part, right_part, precision=HIGHEST_MODE)  31 us
    dot_general x4, matrix products, inner_group(): jnp.einsum('cts,cbs->cbt', toeplitz, drive_part, precision=HIGHEST_MODE)  29 us
  transfers between devices with their start and end apart: 4, of which 2 were waited for; matrix products, arithmetic and copies ran while one was open for 12% of the time, Pallas kernels for 0%

commit v1 on v0

v1 whole, which is shorter than its diff:
```python
import functools

import jax
import jax.numpy as jnp
from jax import lax
from jax.experimental import pallas as pl
from jax.experimental.pallas import tpu as pltpu
from jax.sharding import Mesh
from jax.sharding import PartitionSpec as P

Y, Z, X, K = 8, 8, 4, 2
SUB = 8
EXACT = lax.Precision.HIGHEST


def shifted(array, axis, step):
    size = lax.axis_size(axis)
    return lax.ppermute(array, axis, [(i, (i + step) % size) for i in range(size)])


def to_all(array, axis):
    copies = jnp.broadcast_to(array[None], (lax.axis_size(axis),) + array.shape)
    return lax.all_to_all(copies, axis, 0, 0, tiled=True)


def project_kernel(order_ref, tokens_ref, weight_ref, rate_ref, query_ref, drive_ref, before_ref, own_ref, total, ends):
    step = pl.program_id(0)
    rows = tokens_ref.shape[1]
    width = query_ref.shape[1]
    poles = rate_ref.shape[0]
    depth = tokens_ref.shape[2]

    @pl.when(step == 0)
    def _():
        total[...] = jnp.zeros_like(total)

    for stream in range(3):
        block = weight_ref[:, stream].reshape(depth, width)
        total[stream] += jnp.dot(tokens_ref[0], block, preferred_element_type=jnp.float32)

    @pl.when(step == pl.num_programs(0) - 1)
    def _():
        query_ref[...] = total[0].astype(jnp.bfloat16)
        key = total[1].astype(jnp.bfloat16).astype(jnp.float32)
        value = total[2].astype(jnp.bfloat16).astype(jnp.float32)
        span = rows // SUB
        for half in range(width // 128):
            here = slice(half * 128, half * 128 + 128)
            drive_ref[half] = key[:, here] * value[:, here]
            keep = [jnp.broadcast_to(jnp.exp(-rate_ref[n : n + 1, here]), (SUB, 128)) for n in range(poles)]

            def advance(i, states):
                drive = drive_ref[half, pl.ds(i, SUB, stride=span), :]
                return [s * a + drive for s, a in zip(states, keep)]

            states = lax.fori_loop(0, span, advance, [jnp.zeros((SUB, 128), jnp.float32)] * poles, unroll=8)
            for n in range(poles):
                ends[half, n * SUB : (n + 1) * SUB, :] = states[n]
            across = jnp.exp(-rate_ref[:, here] * span)
            before = jnp.zeros((poles, 128), jnp.float32)
            for b in range(SUB):
                before_ref[half, pl.ds(b, poles, stride=SUB), :] = before
                before = before * across + ends[half, pl.ds(b, poles, stride=SUB), :]
            own_ref[:, here] = before


def finish_kernel(place_ref, query_ref, drive_ref, before_ref, rows_in_ref, far_ref, rate_ref, residue_ref, skip_ref, mixed_ref, unit_ref, scale_ref, conv):
    rows, width = query_ref.shape
    poles = rate_ref.shape[0]
    span = rows // SUB
    y, z = place_ref[0], place_ref[1]
    rate = rate_ref[...]
    plane = rate * (rows * Z)
    incoming = jnp.zeros_like(rate)
    last = jnp.zeros_like(rate)
    hop = jnp.exp(-plane)
    for other in range(Y):
        incoming = jnp.where(other < y, incoming * hop + far_ref[other], incoming)
        last = last * hop + far_ref[other]
    incoming = rows_in_ref[...] + incoming * jnp.exp(-rate * (rows * z).astype(jnp.float32))

    block = lax.broadcasted_iota(jnp.int32, (SUB, 128), 0).astype(jnp.float32) * span
    for half in range(width // 128):
        here = slice(half * 128, half * 128 + 128)
        keep = [jnp.broadcast_to(jnp.exp(-rate[n : n + 1, here]), (SUB, 128)) for n in range(poles)]
        gain = [jnp.broadcast_to(residue_ref[n : n + 1, here], (SUB, 128)) for n in range(poles)]
        skip = jnp.broadcast_to(skip_ref[:, here], (SUB, 128))
        states = [
            before_ref[half, n * SUB : (n + 1) * SUB, :] + incoming[n : n + 1, here] * jnp.exp(-rate[n : n + 1, here] * block)
            for n in range(poles)
        ]

        def advance(i, states):
            drive = drive_ref[half, pl.ds(i, SUB, stride=span), :]
            states = [s * a + drive for s, a in zip(states, keep)]
            terms = [s * g for s, g in zip(states, gain)] + [skip * drive]
            while len(terms) > 1:
                terms = [sum(terms[j : j + 2][1:], terms[j]) for j in range(0, len(terms), 2)]
            conv[half, pl.ds(i, SUB, stride=span), :] = terms[0]
            return states

        lax.fori_loop(0, span, advance, states, unroll=8)
        mixed_ref[:, here] = (query_ref[:, here].astype(jnp.float32) * conv[half]).astype(jnp.bfloat16)

    owned = (y * Z + z) * 4
    pick = lax.broadcasted_iota(jnp.int32, (8, width), 1) == lax.broadcasted_iota(jnp.int32, (8, width), 0) + owned
    pick = pick.astype(jnp.float32)
    contract = (((1,), (1,)), ((), ()))
    state = lax.dot_general(pick, last, contract, precision=EXACT, preferred_element_type=jnp.float32)
    flipped = lax.dot_general(last, pick, contract, precision=EXACT, preferred_element_type=jnp.float32)
    top = jnp.maximum(jnp.max(jnp.abs(state), axis=1, keepdims=True), 1.0)
    unit_ref[...] = (state / top)[:4]
    scale_ref[...] = (jnp.maximum(jnp.max(jnp.abs(flipped), axis=0, keepdims=True), 1.0) / 127.0)[:, :4]


def vmem():
    return pl.BlockSpec(memory_space=pltpu.VMEM)


def smem():
    return pl.BlockSpec(memory_space=pltpu.SMEM)


def shards(tokens, in_weight, rate, residue, skip_gain):
    rows, depth = tokens.shape
    width, poles = rate.shape
    y, z, x, k = (lax.axis_index(a) for a in ("y", "z", "x", "k"))

    weights = lax.all_gather(in_weight.transpose(1, 0, 2), ("y", "z"), axis=0)

    pair = jnp.stack([tokens, shifted(tokens, "k", 1)])
    ahead = shifted(pair, "x", 1)
    behind = shifted(pair, "x", -1)
    across = [shifted(pair[:1], "x", 2), shifted(pair[1:], "x", -2)]
    pieces = jnp.concatenate([pair, ahead, behind] + across)
    order = jnp.stack([2 * ((x + d) % X) + (k + e) % K for d in (0, X - 1, 1, 2) for e in (0, 1)])

    rate_rows = rate.T
    residue_rows = residue.T
    chunks = X * K
    per = weights.shape[0] // chunks
    drive_shape = (width // 128, rows, 128)
    before_shape = (width // 128, poles * SUB, 128)
    f32 = functools.partial(jax.ShapeDtypeStruct, dtype=jnp.float32)
    whole = lambda shape: pl.BlockSpec(shape, lambda i, order: (0,) * len(shape))
    query, drive, before, own = pl.pallas_call(
        project_kernel,
        grid_spec=pltpu.PrefetchScalarGridSpec(
            num_scalar_prefetch=1,
            grid=(chunks,),
            in_specs=[
                pl.BlockSpec((1, rows, depth), lambda i, order: (i, 0, 0)),
                pl.BlockSpec((per,) + weights.shape[1:], lambda i, order: (order[i], 0, 0, 0)),
                whole((poles, width)),
            ],
            out_specs=[whole((rows, width)), whole(drive_shape), whole(before_shape), whole((poles, width))],
            scratch_shapes=[pltpu.VMEM((3, rows, width), jnp.float32), pltpu.VMEM(before_shape, jnp.float32)],
        ),
        out_shape=[
            jax.ShapeDtypeStruct((rows, width), jnp.bfloat16),
            f32(drive_shape),
            f32(before_shape),
            f32((poles, width)),
        ],
        compiler_params=pltpu.CompilerParams(vmem_limit_bytes=40 * 2**20),
        name="project",
    )(order, pieces, weights, rate_rows)

    near = to_all(own, "z")
    at = jnp.arange(Z, dtype=jnp.float32)[:, None, None]
    gap = z.astype(jnp.float32) - 1.0 - at
    row_rate = rate_rows[None] * rows
    rows_in = jnp.sum(jnp.where(gap >= 0, jnp.exp(-row_rate * jnp.maximum(gap, 0.0)), 0.0) * near, axis=0)
    row_sum = jnp.sum(jnp.exp(-row_rate * (Z - 1.0 - at)) * near, axis=0)
    far = to_all(row_sum, "y")

    mixed, unit, scale = pl.pallas_call(
        finish_kernel,
        in_specs=[smem()] + [vmem()] * 8,
        out_specs=[vmem()] * 3,
        scratch_shapes=[pltpu.VMEM(drive_shape, jnp.float32)],
        out_shape=[jax.ShapeDtypeStruct((rows, width), jnp.bfloat16), f32((4, poles)), f32((1, 4))],
        compiler_params=pltpu.CompilerParams(vmem_limit_bytes=40 * 2**20),
        name="finish",
    )(jnp.stack([y, z]), query, drive, before, rows_in, far, rate_rows, residue_rows, skip_gain[None])
    return mixed, unit, scale.reshape(4)


def solution(mesh):
    fine = Mesh(mesh.devices.reshape(Y, Z, X, K), ("y", "z", "x", "k"))
    seq, chan = ("y", "z"), ("x", "k")
    in_specs = (P(seq, chan), P(seq, None, chan), P(chan, None), P(chan, None), P(chan))
    out_specs = (P(seq, chan), P(chan + seq, None), P(chan + seq))
    return jax.shard_map(shards, mesh=fine, in_specs=in_specs, out_specs=out_specs, check_vma=False)
```

time: 603 us -> 188 us (0.31)
  blocking collectives: 278 us -> 0 us
  matrix products: 75.6 us -> 0 us
  other arithmetic: 53.5 us -> 1.93 us
  waiting for transfers between devices: 167 us -> 121 us
  starting transfers between devices: 0.16 us -> 29.9 us
  Pallas kernels: 0 us -> 12.4 us
    unnamed x1 -> x0, blocking collectives: 278 us -> none
    all_gather x4 -> x1, waiting for transfers between devices: 165 us -> 61.8 us  [shards(): weights = lax.all_gather(in_weight.transpose(1, 0, 2), ('y', 'z'), axis=0)]
    dot_general x11 -> x0, matrix products: 75.6 us -> none  [the longest x4 31 us: inner_group(): jnp.einsum('cnt,cns->cts', left_part, right_part, precision=HIGHEST_MODE)]
    select_n x64 -> x0, other arithmetic: 46.6 us -> none  [hop(): return jax.tree.map(lambda a, b: jnp.where(reached, a, b), new, before)]
    ppermute x0 -> x5, waiting for transfers between devices: none -> 40.1 us  [shifted(): lax.ppermute(array, axis, [(i, (i + step) % size) for i in range(size)])]
    ppermute x0 -> x5, starting transfers between devices: none -> 19 us  [shifted(): lax.ppermute(array, axis, [(i, (i + step) % size) for i in range(size)])]
    all_to_all x0 -> x2, waiting for transfers between devices: none -> 18.1 us  [to_all(): return lax.all_to_all(copies, axis, 0, 0, tiled=True)]
    pallas_call x0 -> x2, Pallas kernels: none -> 12.4 us  [the longest x1 10.1 us: shards(): pl.pallas_call(project_kernel, grid_spec=pltpu.PrefetchScalarGridSpec(num...]
  transfers between devices with their start and end apart: 4 -> 8, of which waited for: 2 -> 6; matrix products, arithmetic and copies ran while one was open for 12% -> 2% of each run, Pallas kernels for 0% -> 0%
where the time goes in v1:
time: 188 us; the launch traced here: 187 us
  waiting for transfers between devices  121 us (64%)
  starting transfers between devices  29.9 us (16%)
  between operations  14.2 us (8%)
  Pallas kernels  12.4 us (7%)
  local copies, waits for them, and re-layouts  8.1 us (4%)
  other arithmetic  1.93 us (1%)
    all_gather x1, waiting for transfers between devices, shards(): weights = lax.all_gather(in_weight.transpose(1, 0, 2), ('y', 'z'), axis=0)  61.8 us
    ppermute x5, waiting for transfers between devices, shifted(): lax.ppermute(array, axis, [(i, (i + step) % size) for i in range(size)])  40.1 us
    ppermute x5, starting transfers between devices, shifted(): lax.ppermute(array, axis, [(i, (i + step) % size) for i in range(size)])  19 us
    all_to_all x2, waiting for transfers between devices, to_all(): return lax.all_to_all(copies, axis, 0, 0, tiled=True)  18.1 us
    all_to_all x2, starting transfers between devices, to_all(): return lax.all_to_all(copies, axis, 0, 0, tiled=True)  10.9 us
    pallas_call x1, Pallas kernels, shards(): pl.pallas_call(project_kernel, grid_spec=pltpu.PrefetchScalarGridSpec(num...  10.1 us
    unnamed x19, local copies, waits for them, and re-layouts  6.65 us
  transfers between devices with their start and end apart: 8, of which 6 were waited for; matrix products, arithmetic and copies ran while one was open for 2% of the time, Pallas kernels for 0%

profile of v1, /device:TPU:6, one launch (start us, length us, event | category | flops | bytes accessed | tf_op | source)
XLA Modules:
  0.0 187.2 jit_solution(15430409440195815130)
XLA Ops:
  7.2 0.0 all-gather.3.cloned.1.call-start
  7.2 0.7 all-gather.3.cloned.1.call-update
  7.9 1.9 %collective-permute-start = (bf16[256,1024]{1,0:T(8,128)(2,1)}, bf16[256,1024]{1,0:T(8,128)(2,1)S(1)}, u32[]{:S(2)}, u32[]{:S(2)}) collective-permute-start(bf16[256,1024]{1,0:T(8,128)(2,1)} %param.5), channel_id=1, source_target_pairs={{0,1},{1,0},{2,3},{3,2},{4,5},{5,4},{6,7},{7,6},{8,9},{9,8},{10,11... | collective-permute-start | bytes 1572872 | tf_op jit(solution)/shard_map/ppermute | solution.py:18
  9.8 2.1 %collective-permute-done = bf16[256,1024]{1,0:T(8,128)(2,1)S(1)} collective-permute-done((bf16[256,1024]{1,0:T(8,128)(2,1)}, bf16[256,1024]{1,0:T(8,128)(2,1)S(1)}, u32[]{:S(2)}, u32[]{:S(2)}) %collective-permute-start) | collective-permute-done | bytes 524320 | tf_op jit(solution)/shard_map/ppermute | solution.py:18
  11.9 1.1 pad_maximum_fusion
  13.1 7.8 %collective-permute-start.1 = (bf16[2,256,1024]{2,1,0:T(8,128)(2,1)S(1)}, bf16[2,256,1024]{2,1,0:T(8,128)(2,1)}, u32[]{:S(2)}, u32[]{:S(2)}) collective-permute-start(bf16[2,256,1024]{2,1,0:T(8,128)(2,1)S(1)} %pad_maximum_fusion), channel_id=1, source_target_pairs={{0,2},{2,4},{4,6},{6,0},{1,3},{3,5},{5,7},{7,1},{8,10},{10,12},{12... | collective-permute-start | bytes 3145736 | tf_op jit(solution)/shard_map/ppermute | solution.py:18
  20.8 1.9 %collective-permute-start.2 = (bf16[2,256,1024]{2,1,0:T(8,128)(2,1)S(1)}, bf16[2,256,1024]{2,1,0:T(8,128)(2,1)S(1)}, u32[]{:S(2)}, u32[]{:S(2)}) collective-permute-start(bf16[2,256,1024]{2,1,0:T(8,128)(2,1)S(1)} %pad_maximum_fusion), channel_id=1, source_target_pairs={{0,6},{2,0},{4,2},{6,4},{1,7},{3,1},{5,3},{7,5},{8,14},{10,8},{12,... | collective-permute-start | bytes 3145736 | tf_op jit(solution)/shard_map/ppermute | solution.py:18
  22.8 3.4 %collective-permute-start.3 = (bf16[1,256,1024]{2,1,0:T(8,128)(2,1)}, bf16[1,256,1024]{2,1,0:T(8,128)(2,1)S(1)}, u32[]{:S(2)}, u32[]{:S(2)}) collective-permute-start(bf16[1,256,1024]{2,1,0:T(8,128)(2,1)} %bitcast.27), channel_id=1, source_target_pairs={{0,4},{2,6},{4,0},{6,2},{1,5},{3,7},{5,1},{7,3},{8,12},{10,14},{12... | collective-permute-start | bytes 1572872 | tf_op jit(solution)/shard_map/ppermute | solution.py:18
  26.2 0.1 stack.56.order_ref
  26.3 0.6 iota_subtract_fusion
  26.9 1.1 constant_dynamic-update-slice_fusion.5
  28.0 4.0 %collective-permute-start.4 = (bf16[1,256,1024]{2,1,0:T(8,128)(2,1)S(1)}, bf16[1,256,1024]{2,1,0:T(8,128)(2,1)S(1)}, u32[]{:S(2)}, u32[]{:S(2)}) collective-permute-start(bf16[1,256,1024]{2,1,0:T(8,128)(2,1)S(1)} %bitcast.29), channel_id=1, source_target_pairs={{0,4},{2,6},{4,0},{6,2},{1,5},{3,7},{5,1},{7,3},{8,12},{10,14},{12... | collective-permute-start | bytes 1572872 | tf_op jit(solution)/shard_map/ppermute | solution.py:18
  32.0 34.0 %collective-permute-done.1 = bf16[2,256,1024]{2,1,0:T(8,128)(2,1)} collective-permute-done((bf16[2,256,1024]{2,1,0:T(8,128)(2,1)S(1)}, bf16[2,256,1024]{2,1,0:T(8,128)(2,1)}, u32[]{:S(2)}, u32[]{:S(2)}) %collective-permute-start.1) | collective-permute-done | bytes 1048608 | tf_op jit(solution)/shard_map/ppermute | solution.py:18
  66.0 1.3 constant_dynamic-update-slice_fusion.3
  67.3 4.0 %collective-permute-done.2 = bf16[2,256,1024]{2,1,0:T(8,128)(2,1)S(1)} collective-permute-done((bf16[2,256,1024]{2,1,0:T(8,128)(2,1)S(1)}, bf16[2,256,1024]{2,1,0:T(8,128)(2,1)S(1)}, u32[]{:S(2)}, u32[]{:S(2)}) %collective-permute-start.2) | collective-permute-done | bytes 1048608 | tf_op jit(solution)/shard_map/ppermute | solution.py:18
  71.3 0.1 constant_dynamic-update-slice_fusion.2
  71.4 0.0 collective-permute-done.3
  71.4 0.0 collective-permute-done.4
  71.5 1.9 %copy-done = bf16[8,256,1024]{2,1,0:T(8,128)(2,1)} copy-done((bf16[8,256,1024]{2,1,0:T(8,128)(2,1)}, bf16[8,256,1024]{2,1,0:T(8,128)(2,1)S(1)}, u32[]{:S(2)}) %copy-start) | copy-done | bytes 4194328
  73.4 61.8 %all-gather.3.cloned.1.call-done = bf16[192,128,256]{2,1,0:T(8,128)(2,1)} async-done(((bf16[3,128,256]{2,1,0:T(8,128)(2,1)}), bf16[192,128,256]{2,1,0:T(8,128)(2,1)}) %all-gather.3.cloned.1.call-update) | async-done | bytes 12582928 | tf_op jit(solution)/shard_map/all_gather | solution.py:129
  135.3 2.2 %copy-done.1 = bf16[8,256,1024]{2,1,0:T(8,128)(2,1)S(1)} copy-done((bf16[8,256,1024]{2,1,0:T(8,128)(2,1)S(1)}, bf16[8,256,1024]{2,1,0:T(8,128)(2,1)}, u32[]{:S(2)}) %copy-start.1) | copy-done | bytes 4194328
  137.4 10.1 %project.1 = (bf16[256,256]{1,0:T(8,128)(2,1)S(1)}, f32[2,256,128]{2,1,0:T(8,128)S(1)}, f32[2,128,128]{2,1,0:T(8,128)S(1)}, f32[16,256]{1,0:T(8,128)S(1)}) custom-call(s32[8]{0:T(128)S(1)} %stack.56.order_ref, bf16[8,256,1024]{2,1,0:T(8,128)(2,1)S(1)} %copy-done.1, bf16[64,3,128,256]{3,2,1,0:T(8,128)(2,1)} %bitcast.25, f32[16,256]{1,0:T(8,128)S(1)} %bitcast.21), custom_call_target="tpu_custom_call" | custom-call | tf_op jit(solution)/shard_map/project/pallas_call | solution.py:146
  147.5 0.7 broadcast_in_dim.31
  148.2 6.3 %all-to-all-start = ((f32[8,16,256]{2,1,0:T(8,128)}), f32[8,16,256]{2,1,0:T(8,128)S(1)}, u32[]{:S(2)}, u32[]{:S(2)}) async-start(f32[8,16,256]{2,1,0:T(8,128)} %broadcast_in_dim.31), calls=%async_computation | async-start | bytes 262144 | tf_op jit(solution)/shard_map/all_to_all | solution.py:23
  154.5 9.1 %all-to-all-done = f32[8,16,256]{2,1,0:T(8,128)S(1)} async-done(((f32[8,16,256]{2,1,0:T(8,128)}), f32[8,16,256]{2,1,0:T(8,128)S(1)}, u32[]{:S(2)}, u32[]{:S(2)}) %all-to-all-start) | async-done | bytes 131104 | tf_op jit(solution)/shard_map/all_to_all | solution.py:23
  163.6 0.0 copy-done.5
  163.6 0.1 multiply_reduce_fusion
  163.7 0.7 broadcast_in_dim.32
  164.4 4.6 %all-to-all-start.1 = ((f32[8,16,256]{2,1,0:T(8,128)}), f32[8,16,256]{2,1,0:T(8,128)S(1)}, u32[]{:S(2)}, u32[]{:S(2)}) async-start(f32[8,16,256]{2,1,0:T(8,128)} %broadcast_in_dim.32), calls=%async_computation.1 | async-start | bytes 262144 | tf_op jit(solution)/shard_map/all_to_all | solution.py:23
  169.0 0.1 pad_add_fusion.place_ref
  169.1 9.0 %all-to-all-done.1.far_ref = f32[8,16,256]{2,1,0:T(8,128)S(1)} async-done(((f32[8,16,256]{2,1,0:T(8,128)}), f32[8,16,256]{2,1,0:T(8,128)S(1)}, u32[]{:S(2)}, u32[]{:S(2)}) %all-to-all-start.1) | async-done | bytes 131104 | tf_op jit(solution)/shard_map/all_to_all | solution.py:23
  178.1 2.3 %finish.1 = (bf16[256,256]{1,0:T(8,128)(2,1)}, f32[4,16]{1,0:T(4,128)}, f32[1,4]{1,0:T(1,128)}) custom-call(s32[2]{0:T(128)S(1)} %pad_add_fusion.place_ref, bf16[256,256]{1,0:T(8,128)(2,1)S(1)} %get-tuple-element.10.query_ref, f32[2,256,128]{2,1,0:T(8,128)S(1)} %get-tuple-element.11.drive_ref, f32[2,128,128]{2,1,0:T(8,128)S(1)} %get-tuple-element.12.before_ref, ...), custom_call_target="tpu_custom_call" | custom-call | tf_op jit(solution)/shard_map/finish/pallas_call | solution.py:177
  (16 shorter events, 0.1 us)
Async XLA Ops:
  7.2 128.1 %all-gather.3.cloned.1.call-start = ((), (), s32[]{:S(2)}) async-start(), calls=%async_computation.2 | async-start | bytes 12779520 | tf_op jit(solution)/shard_map/all_gather | solution.py:129
  7.9 4.0 %collective-permute-start = (bf16[256,1024]{1,0:T(8,128)(2,1)}, bf16[256,1024]{1,0:T(8,128)(2,1)S(1)}, u32[]{:S(2)}, u32[]{:S(2)}) collective-permute-start(bf16[256,1024]{1,0:T(8,128)(2,1)} %param.5), channel_id=1, source_target_pairs={{0,1},{1,0},{2,3},{3,2},{4,5},{5,4},{6,7},{7,6},{8,9},{9,8},{10,11... | collective-permute-start | bytes 1572872 | tf_op jit(solution)/shard_map/ppermute | solution.py:18
  13.1 52.9 %collective-permute-start.1 = (bf16[2,256,1024]{2,1,0:T(8,128)(2,1)S(1)}, bf16[2,256,1024]{2,1,0:T(8,128)(2,1)}, u32[]{:S(2)}, u32[]{:S(2)}) collective-permute-start(bf16[2,256,1024]{2,1,0:T(8,128)(2,1)S(1)} %pad_maximum_fusion), channel_id=1, source_target_pairs={{0,2},{2,4},{4,6},{6,0},{1,3},{3,5},{5,7},{7,1},{8,10},{10,12},{12... | collective-permute-start | bytes 3145736 | tf_op jit(solution)/shard_map/ppermute | solution.py:18
  20.8 50.5 %collective-permute-start.2 = (bf16[2,256,1024]{2,1,0:T(8,128)(2,1)S(1)}, bf16[2,256,1024]{2,1,0:T(8,128)(2,1)S(1)}, u32[]{:S(2)}, u32[]{:S(2)}) collective-permute-start(bf16[2,256,1024]{2,1,0:T(8,128)(2,1)S(1)} %pad_maximum_fusion), channel_id=1, source_target_pairs={{0,6},{2,0},{4,2},{6,4},{1,7},{3,1},{5,3},{7,5},{8,14},{10,8},{12,... | collective-permute-start | bytes 3145736 | tf_op jit(solution)/shard_map/ppermute | solution.py:18
  22.8 48.6 %collective-permute-start.3 = (bf16[1,256,1024]{2,1,0:T(8,128)(2,1)}, bf16[1,256,1024]{2,1,0:T(8,128)(2,1)S(1)}, u32[]{:S(2)}, u32[]{:S(2)}) collective-permute-start(bf16[1,256,1024]{2,1,0:T(8,128)(2,1)} %bitcast.27), channel_id=1, source_target_pairs={{0,4},{2,6},{4,0},{6,2},{1,5},{3,7},{5,1},{7,3},{8,12},{10,14},{12... | collective-permute-start | bytes 1572872 | tf_op jit(solution)/shard_map/ppermute | solution.py:18
  26.9 108.4 %copy-start.2 = (f32[256,16]{0,1:T(8,128)S(1)}, f32[256,16]{0,1:T(8,128)}, u32[]{:S(2)}) copy-start(f32[256,16]{0,1:T(8,128)} %param.7) | copy-start | bytes 49156
  28.0 43.5 %collective-permute-start.4 = (bf16[1,256,1024]{2,1,0:T(8,128)(2,1)S(1)}, bf16[1,256,1024]{2,1,0:T(8,128)(2,1)S(1)}, u32[]{:S(2)}, u32[]{:S(2)}) collective-permute-start(bf16[1,256,1024]{2,1,0:T(8,128)(2,1)S(1)} %bitcast.29), channel_id=1, source_target_pairs={{0,4},{2,6},{4,0},{6,2},{1,5},{3,7},{5,1},{7,3},{8,12},{10,14},{12... | collective-permute-start | bytes 1572872 | tf_op jit(solution)/shard_map/ppermute | solution.py:18
  71.5 1.9 %copy-start = (bf16[8,256,1024]{2,1,0:T(8,128)(2,1)}, bf16[8,256,1024]{2,1,0:T(8,128)(2,1)S(1)}, u32[]{:S(2)}) copy-start(bf16[8,256,1024]{2,1,0:T(8,128)(2,1)S(1)} %constant_dynamic-update-slice_fusion.tokens_ref) | copy-start | bytes 12582916
  135.2 2.2 %copy-start.1 = (bf16[8,256,1024]{2,1,0:T(8,128)(2,1)S(1)}, bf16[8,256,1024]{2,1,0:T(8,128)(2,1)}, u32[]{:S(2)}) copy-start(bf16[8,256,1024]{2,1,0:T(8,128)(2,1)} %copy-done) | copy-start | bytes 12582916
  137.4 26.1 %copy-start.5 = (f32[8]{0:T(128)S(1)}, f32[8]{0:T(128)}, u32[]{:S(2)}) copy-start(f32[8]{0:T(128)} %get-tuple-element.19) | copy-start | bytes 100
  137.4 26.1 %copy-start.6 = (f32[8]{0:T(128)S(1)}, f32[8]{0:T(128)}, u32[]{:S(2)}) copy-start(f32[8]{0:T(128)} %get-tuple-element.20) | copy-start | bytes 100
  137.4 40.7 %copy-start.3 = (f32[256,16]{0,1:T(8,128)S(1)}, f32[256,16]{0,1:T(8,128)}, u32[]{:S(2)}) copy-start(f32[256,16]{0,1:T(8,128)} %param.8) | copy-start | bytes 49156
  137.4 40.7 %copy-start.4 = (f32[256]{0:T(256)S(1)}, f32[256]{0:T(256)}, u32[]{:S(2)}) copy-start(f32[256]{0:T(256)} %param.9) | copy-start | bytes 3076
  148.2 15.4 %all-to-all-start = ((f32[8,16,256]{2,1,0:T(8,128)}), f32[8,16,256]{2,1,0:T(8,128)S(1)}, u32[]{:S(2)}, u32[]{:S(2)}) async-start(f32[8,16,256]{2,1,0:T(8,128)} %broadcast_in_dim.31), calls=%async_computation | async-start | bytes 262144 | tf_op jit(solution)/shard_map/all_to_all | solution.py:23
  164.4 13.7 %all-to-all-start.1 = ((f32[8,16,256]{2,1,0:T(8,128)}), f32[8,16,256]{2,1,0:T(8,128)S(1)}, u32[]{:S(2)}, u32[]{:S(2)}) async-start(f32[8,16,256]{2,1,0:T(8,128)} %broadcast_in_dim.32), calls=%async_computation.1 | async-start | bytes 262144 | tf_op jit(solution)/shard_map/all_to_all | solution.py:23
Sparse Core Ops, SparseCore 0:
  11.1 124.1 all-gather.2

commit v2 on v1

v2 whole, which is shorter than its diff:
```python
import functools

import jax
import jax.numpy as jnp
from jax import lax
from jax.experimental import pallas as pl
from jax.experimental.pallas import tpu as pltpu
from jax.sharding import Mesh
from jax.sharding import PartitionSpec as P

Y, Z, X, K = 8, 8, 4, 2
LINE = 8
AXES = ("y", "z", "x", "k")
SUB = 8
LANES = 128
EXACT = lax.Precision.HIGHEST


def number(y, z, x, k):
    return ((y * Z + z) * X + x) * K + k


def lines(first):
    groups = []
    for k in range(K):
        along_z = (k == 0) == first
        for x in range(X):
            for o in range(LINE):
                groups.append([number(o, i, x, k) if along_z else number(i, o, x, k) for i in range(LINE)])
    return groups


def shifted(array, axis, step):
    size = lax.axis_size(axis)
    return lax.ppermute(array, axis, [(i, (i + step) % size) for i in range(size)])


def to_all(array, axis):
    copies = jnp.broadcast_to(array[None], (lax.axis_size(axis),) + array.shape)
    return lax.all_to_all(copies, axis, 0, 0, tiled=True)


def collect_kernel(meta_ref, *refs):
    k = meta_ref[8]
    tokens_ref = refs[-1]
    place = 0
    for ref in refs[:-1]:
        for i in range(0, ref.shape[0], LINE):
            piece = meta_ref[place]
            place += 1
            for block in range(LINE):
                chunk, part = jnp.where(k == 0, piece, block), jnp.where(k == 0, block, piece)
                tokens_ref[chunk, part] = ref[i + block]


def project(features_ref, weights_ref, left, right, total, left_sems, right_sems):
    streams, _, width = total.shape
    copies = []
    for chunk in range(LINE):
        copies.append(
            (
                pltpu.make_async_copy(features_ref.at[chunk], left.at[chunk], left_sems.at[chunk]),
                pltpu.make_async_copy(weights_ref.at[chunk], right.at[chunk], right_sems.at[chunk]),
            )
        )
    for pair in copies:
        for copy in pair:
            copy.start()
    for chunk, pair in enumerate(copies):
        for copy in pair:
            copy.wait()
        rows = jnp.concatenate([left[chunk, part] for part in range(LINE)], axis=1)
        for stream in range(streams):
            block = right[chunk, :, stream].reshape(-1, width)
            product = jnp.dot(rows, block, preferred_element_type=jnp.float32)
            total[stream] = product if chunk == 0 else total[stream] + product


def drive_kernel(features_ref, weights_ref, filter_ref, local_ref, own_ref, ends, total, *scratch):
    poles, width = own_ref.shape
    halves, rows = width // LANES, total.shape[1]
    span = rows // SUB
    project(features_ref, weights_ref, *scratch[:2], total, *scratch[2:])
    key = total[0].astype(jnp.bfloat16).astype(jnp.float32)
    value = total[1].astype(jnp.bfloat16).astype(jnp.float32)
    for half in range(halves):
        here = slice(half * LANES, half * LANES + LANES)
        local_ref[half, :rows] = key[:, here] * value[:, here]
    for half in range(halves):
        here = slice(half * LANES, half * LANES + LANES)
        keep = [jnp.broadcast_to(jnp.exp(-filter_ref[n : n + 1, here]), (SUB, LANES)) for n in range(poles)]

        def advance(i, states):
            drive = local_ref[half, pl.ds(i, SUB, stride=span), :]
            return [s * a + drive for s, a in zip(states, keep)]

        states = lax.fori_loop(0, span, advance, [jnp.zeros((SUB, LANES), jnp.float32)] * poles, unroll=8)
        for n in range(poles):
            ends[half, n * SUB : (n + 1) * SUB, :] = states[n]
        across = jnp.exp(-filter_ref[:poles, here] * span)
        before = jnp.zeros((poles, LANES), jnp.float32)
        for b in range(SUB):
            local_ref[half, pl.ds(rows + b, poles, stride=SUB), :] = before
            before = before * across + ends[half, pl.ds(b, poles, stride=SUB), :]
        own_ref[:, here] = before


def convolve_kernel(meta_ref, local_ref, rows_in_ref, far_ref, filter_ref, conv_ref, unit_ref, scale_ref):
    halves, rows, _ = conv_ref.shape
    poles, width = rows_in_ref.shape
    span = rows // SUB
    y, z = meta_ref[9], meta_ref[10]
    rate = filter_ref[:poles]
    incoming = jnp.zeros_like(rate)
    last = jnp.zeros_like(rate)
    hop = jnp.exp(-rate * (rows * Z))
    for other in range(Y):
        incoming = jnp.where(other < y, incoming * hop + far_ref[other], incoming)
        last = last * hop + far_ref[other]
    incoming = rows_in_ref[...] + incoming * jnp.exp(-rate * (rows * z).astype(jnp.float32))

    block = lax.broadcasted_iota(jnp.int32, (SUB, LANES), 0).astype(jnp.float32) * span
    for half in range(halves):
        here = slice(half * LANES, half * LANES + LANES)
        keep = [jnp.broadcast_to(jnp.exp(-rate[n : n + 1, here]), (SUB, LANES)) for n in range(poles)]
        gain = [jnp.broadcast_to(filter_ref[poles + n : poles + n + 1, here], (SUB, LANES)) for n in range(poles)]
        skip = jnp.broadcast_to(filter_ref[2 * poles : 2 * poles + 1, here], (SUB, LANES))
        states = [
            local_ref[half, rows + n * SUB : rows + (n + 1) * SUB, :] + incoming[n : n + 1, here] * jnp.exp(-rate[n : n + 1, here] * block)
            for n in range(poles)
        ]

        def advance(i, states):
            drive = local_ref[half, pl.ds(i, SUB, stride=span), :]
            states = [s * a + drive for s, a in zip(states, keep)]
            terms = [s * g for s, g in zip(states, gain)]
            while len(terms) > 1:
                terms = [a + b for a, b in zip(terms[::2], terms[1::2])]
            conv_ref[half, pl.ds(i, SUB, stride=span), :] = terms[0] + skip * drive
            return states

        lax.fori_loop(0, span, advance, states, unroll=8)

    owned = (y * Z + z) * 4
    pick = lax.broadcasted_iota(jnp.int32, (8, width), 1) == lax.broadcasted_iota(jnp.int32, (8, width), 0) + owned
    pick = pick.astype(jnp.float32)
    contract = (((1,), (1,)), ((), ()))
    state = lax.dot_general(pick, last, contract, precision=EXACT, preferred_element_type=jnp.float32)
    flipped = lax.dot_general(last, pick, contract, precision=EXACT, preferred_element_type=jnp.float32)
    top = jnp.maximum(jnp.max(jnp.abs(state), axis=1, keepdims=True), 1.0)
    unit_ref[...] = (state / top)[:4]
    scale_ref[...] = (jnp.maximum(jnp.max(jnp.abs(flipped), axis=0, keepdims=True), 1.0) / 127.0)[:, :4]


def mix_kernel(features_ref, weights_ref, conv_ref, mixed_ref, total, *scratch):
    project(features_ref, weights_ref, *scratch[:2], total, *scratch[2:])
    query = total[0].astype(jnp.bfloat16).astype(jnp.float32)
    for half in range(conv_ref.shape[0]):
        here = slice(half * LANES, half * LANES + LANES)
        mixed_ref[:, here] = (query[:, here] * conv_ref[half]).astype(jnp.bfloat16)


def vmem():
    return pl.BlockSpec(memory_space=pltpu.VMEM)


def in_hbm(array):
    return pltpu.with_memory_space_constraint(array, pltpu.HBM)


def smem():
    return pl.BlockSpec(memory_space=pltpu.SMEM)


def shards(tokens, in_weight, rate, residue, skip_gain):
    rows, depth = tokens.shape
    width, poles = rate.shape
    y, z, x, k = (lax.axis_index(a) for a in AXES)
    f32 = functools.partial(jax.ShapeDtypeStruct, dtype=jnp.float32)
    bf16 = functools.partial(jax.ShapeDtypeStruct, dtype=jnp.bfloat16)

    def near_line(array):
        copies = jnp.broadcast_to(array[None], (LINE,) + array.shape)
        return lax.all_to_all(copies, AXES, 0, 0, tiled=True, axis_index_groups=lines(True))

    def far_line(array):
        return lax.all_gather(array, AXES, axis=0, axis_index_groups=lines(False))

    near_weights = near_line(in_weight.transpose(1, 0, 2))
    drive_weights = far_line(near_weights[:, 1:])

    blocks = tokens.reshape(rows, LINE, LANES).transpose(1, 0, 2) + near_weights[0, 0, 0, 0] * 0
    other = shifted(blocks, "k", 1)
    across = [shifted(blocks[: LINE // 2], "x", 2), shifted(blocks[LINE // 2 :], "x", -2)]
    arrived = [shifted(blocks, "x", 1), shifted(blocks, "x", -1)] + across
    remote = jnp.concatenate(arrived)
    pieces = [blocks, other, remote, shifted(remote, "k", 1)]
    chan = [2 * x + k, 2 * x + 1 - k] + [2 * ((x + d) % X) + e for e in (k, 1 - k) for d in (X - 1, 1, 2)]
    meta = jnp.stack(chan + [k, y, z]).astype(jnp.int32)
    features = pl.pallas_call(
        collect_kernel,
        in_specs=[smem()] + [vmem()] * 4,
        out_specs=vmem(),
        out_shape=bf16((LINE,) + blocks.shape),
        compiler_params=pltpu.CompilerParams(vmem_limit_bytes=16 * 2**20),
        name="collect",
    )(meta, *pieces)

    query_weights = far_line(near_weights[:, :1])

    def project_scratch(gathered):
        return [
            pltpu.VMEM((gathered.shape[2], rows, width), jnp.float32),
            pltpu.VMEM(features.shape, jnp.bfloat16),
            pltpu.VMEM(gathered.shape, jnp.bfloat16),
            pltpu.SemaphoreType.DMA((LINE,)),
            pltpu.SemaphoreType.DMA((LINE,)),
        ]

    rate_rows = rate.T
    filters = jnp.concatenate([rate_rows, residue.T, skip_gain[None]])
    params = pltpu.CompilerParams(vmem_limit_bytes=20 * 2**20)
    hbm = pl.BlockSpec(memory_space=pltpu.HBM)
    drive_shape = (width // LANES, rows, LANES)
    local_shape = (width // LANES, rows + poles * SUB, LANES)
    local, own = pl.pallas_call(
        drive_kernel,
        in_specs=[hbm, hbm, vmem()],
        out_specs=[vmem()] * 2,
        out_shape=[f32(local_shape), f32((poles, width))],
        scratch_shapes=[pltpu.VMEM((width // LANES, poles * SUB, LANES), jnp.float32)] + project_scratch(drive_weights),
        compiler_params=params,
        name="drive",
    )(in_hbm(features), in_hbm(drive_weights), filters)

    near = to_all(own, "z")
    at = jnp.arange(Z, dtype=jnp.float32)[:, None, None]
    gap = z.astype(jnp.float32) - 1.0 - at
    row_rate = rate_rows[None] * rows
    rows_in = jnp.sum(jnp.where(gap >= 0, jnp.exp(-row_rate * jnp.maximum(gap, 0.0)), 0.0) * near, axis=0)
    row_sum = jnp.sum(jnp.exp(-row_rate * (Z - 1.0 - at)) * near, axis=0)
    far = to_all(row_sum, "y")

    conv, unit, scale = pl.pallas_call(
        convolve_kernel,
        in_specs=[smem()] + [vmem()] * 4,
        out_specs=[vmem()] * 3,
        out_shape=[f32(drive_shape), f32((4, poles)), f32((1, 4))],
        compiler_params=params,
        name="convolve",
    )(meta, local, rows_in, far, filters)
    mixed = pl.pallas_call(
        mix_kernel,
        in_specs=[hbm, hbm, vmem()],
        out_specs=vmem(),
        out_shape=bf16((rows, width)),
        scratch_shapes=project_scratch(query_weights),
        compiler_params=params,
        name="mix",
    )(in_hbm(features), in_hbm(query_weights), conv)
    return mixed, unit, scale.reshape(4)


def solution(mesh):
    fine = Mesh(mesh.devices.reshape(Y, Z, X, K), AXES)
    seq, chan = ("y", "z"), ("x", "k")
    in_specs = (P(seq, chan), P(seq, None, chan), P(chan, None), P(chan, None), P(chan))
    out_specs = (P(seq, chan), P(chan + seq, None), P(chan + seq))
    return jax.shard_map(shards, mesh=fine, in_specs=in_specs, out_specs=out_specs, check_vma=False)
```

time: 188 us -> 158 us (0.84)
  waiting for transfers between devices: 121 us -> 46.7 us
  blocking collectives: 0 us -> 48.6 us
  starting transfers between devices: 29.9 us -> 25.1 us
  Pallas kernels: 12.4 us -> 14.4 us
    all_to_all x0 -> x2, blocking collectives: none -> 48.6 us  [the longest x1 34.6 us: near_line(): lax.all_to_all(copies, AXES, 0, 0, tiled=True, axis_index_groups=lines(Tr...]
    all_gather x1 -> x2, waiting for transfers between devices: 61.8 us -> 23.4 us  [far_line(): return lax.all_gather(array, AXES, axis=0, axis_index_groups=lines(False))]
    ppermute x5 -> x6, waiting for transfers between devices: 40.1 us -> 13.5 us  [shifted(): lax.ppermute(array, axis, [(i, (i + step) % size) for i in range(size)])]
    all_to_all x2 -> x1, waiting for transfers between devices: 18.1 us -> 9.72 us  [to_all(): return lax.all_to_all(copies, axis, 0, 0, tiled=True)]
    unnamed x19 -> x14, local copies, waits for them, and re-layouts: 6.65 us -> 2.44 us
    all_to_all x2 -> x1, starting transfers between devices: 10.9 us -> 7.38 us  [to_all(): return lax.all_to_all(copies, axis, 0, 0, tiled=True)]
    slice x0 -> x4, local copies, waits for them, and re-layouts: none -> 2.46 us  [the longest x1 1.05 us: shards(): drive_weights = far_line(near_weights[:, 1:])]
    pallas_call x2 -> x4, Pallas kernels: 12.4 us -> 14.4 us  [the longest x1 5.63 us: shards(): pl.pallas_call(drive_kernel, in_specs=[hbm, hbm, vmem()], out_specs=[vmem...]
  transfers between devices with their start and end apart: 8 -> 9, of which waited for: 6 -> 6; matrix products, arithmetic and copies ran while one was open for 2% -> 2% of each run, Pallas kernels for 0% -> 6%
where the time goes in v2:
time: 158 us; the launch traced here: 157 us
  blocking collectives  48.6 us (31%)
  waiting for transfers between devices  46.7 us (30%)
  starting transfers between devices  25.1 us (16%)
  between operations  15 us (9%)
  Pallas kernels  14.4 us (9%)
  local copies, waits for them, and re-layouts  7.06 us (4%)
    all_to_all x1, blocking collectives, near_line(): lax.all_to_all(copies, AXES, 0, 0, tiled=True, axis_index_groups=lines(Tr...  34.6 us
    all_gather x2, waiting for transfers between devices, far_line(): return lax.all_gather(array, AXES, axis=0, axis_index_groups=lines(False))  23.4 us
    ppermute x6, starting transfers between devices, shifted(): lax.ppermute(array, axis, [(i, (i + step) % size) for i in range(size)])  17.6 us
    all_to_all x1, blocking collectives, to_all(): return lax.all_to_all(copies, axis, 0, 0, tiled=True)  14 us
    ppermute x6, waiting for transfers between devices, shifted(): lax.ppermute(array, axis, [(i, (i + step) % size) for i in range(size)])  13.5 us
    all_to_all x1, waiting for transfers between devices, to_all(): return lax.all_to_all(copies, axis, 0, 0, tiled=True)  9.72 us
    all_to_all x1, starting transfers between devices, to_all(): return lax.all_to_all(copies, axis, 0, 0, tiled=True)  7.38 us
    pallas_call x1, Pallas kernels, shards(): pl.pallas_call(drive_kernel, in_specs=[hbm, hbm, vmem()], out_specs=[vmem...  5.63 us
  transfers between devices with their start and end apart: 9, of which 6 were waited for; matrix products, arithmetic and copies ran while one was open for 2% of the time, Pallas kernels for 6%

profile of v2, /device:TPU:6, one launch (start us, length us, event | category | flops | bytes accessed | tf_op | source)
XLA Modules:
  0.0 157.0 jit_solution(16629739135918406080)
XLA Ops:
  7.2 1.1 broadcast_in_dim.20
  8.3 34.6 %all_to_all.15 = bf16[8,3,128,256]{3,2,1,0:T(8,128)(2,1)S(1)} all-to-all(bf16[8,3,128,256]{3,2,1,0:T(8,128)(2,1)S(1)} %broadcast_in_dim.20), channel_id=1, replica_groups={{0,8,16,24,32,40,48,56},{64,72,80,88,96,104,112,120},{128,136,144,152,1..., dimensions={0} | all-to-all | bytes 3145728 | tf_op jit(solution)/shard_map/all_to_all | solution.py:184
  42.9 1.1 slice.24
  44.0 0.0 all-gather.5.cloned.1.call-start
  44.1 0.9 slice.23
  45.0 0.2 copy-done.1
  45.1 0.2 copy.16
  45.3 0.5 slice.20
  46.5 0.3 copy.17
  46.8 2.4 %collective-permute-start.1 = (bf16[8,256,128]{2,1,0:T(8,128)(2,1)S(1)}, bf16[8,256,128]{2,1,0:T(8,128)(2,1)S(1)}, u32[]{:S(2)}, u32[]{:S(2)}) collective-permute-start(bf16[8,256,128]{2,1,0:T(8,128)(2,1)S(1)} %bitcast.22), channel_id=1, source_target_pairs={{0,2},{2,4},{4,6},{6,0},{1,3},{3,5},{5,7},{7,1},{8,10},{10,12},{12... | collective-permute-start | bytes 1572872 | tf_op jit(solution)/shard_map/ppermute | solution.py:35
  49.2 3.5 %collective-permute-start.2 = (bf16[8,256,128]{2,1,0:T(8,128)(2,1)S(1)}, bf16[8,256,128]{2,1,0:T(8,128)(2,1)S(1)}, u32[]{:S(2)}, u32[]{:S(2)}) collective-permute-start(bf16[8,256,128]{2,1,0:T(8,128)(2,1)S(1)} %bitcast.23), channel_id=1, source_target_pairs={{0,6},{2,0},{4,2},{6,4},{1,7},{3,1},{5,3},{7,5},{8,14},{10,8},{12,... | collective-permute-start | bytes 1572872 | tf_op jit(solution)/shard_map/ppermute | solution.py:35
  52.7 3.3 %collective-permute-start.3 = (bf16[4,256,128]{2,1,0:T(8,128)(2,1)S(1)}, bf16[4,256,128]{2,1,0:T(8,128)(2,1)S(1)}, u32[]{:S(2)}, u32[]{:S(2)}) collective-permute-start(bf16[4,256,128]{2,1,0:T(8,128)(2,1)S(1)} %get-tuple-element.16), channel_id=1, source_target_pairs={{0,4},{2,6},{4,0},{6,2},{1,5},{3,7},{5,1},{7,3},{8,12},{10,14},{12... | collective-permute-start | bytes 786440 | tf_op jit(solution)/shard_map/ppermute | solution.py:35
  56.1 4.2 %collective-permute-start.4 = (bf16[4,256,128]{2,1,0:T(8,128)(2,1)S(1)}, bf16[4,256,128]{2,1,0:T(8,128)(2,1)S(1)}, u32[]{:S(2)}, u32[]{:S(2)}) collective-permute-start(bf16[4,256,128]{2,1,0:T(8,128)(2,1)S(1)} %get-tuple-element.15), channel_id=1, source_target_pairs={{0,4},{2,6},{4,0},{6,2},{1,5},{3,7},{5,1},{7,3},{8,12},{10,14},{12... | collective-permute-start | bytes 786440 | tf_op jit(solution)/shard_map/ppermute | solution.py:35
  60.3 3.2 %collective-permute-done.1 = bf16[8,256,128]{2,1,0:T(8,128)(2,1)S(1)} collective-permute-done((bf16[8,256,128]{2,1,0:T(8,128)(2,1)S(1)}, bf16[8,256,128]{2,1,0:T(8,128)(2,1)S(1)}, u32[]{:S(2)}, u32[]{:S(2)}) %collective-permute-start.1) | collective-permute-done | bytes 524320 | tf_op jit(solution)/shard_map/ppermute | solution.py:35
  63.5 8.8 %collective-permute-done.2 = bf16[8,256,128]{2,1,0:T(8,128)(2,1)S(1)} collective-permute-done((bf16[8,256,128]{2,1,0:T(8,128)(2,1)S(1)}, bf16[8,256,128]{2,1,0:T(8,128)(2,1)S(1)}, u32[]{:S(2)}, u32[]{:S(2)}) %collective-permute-start.2) | collective-permute-done | bytes 524320 | tf_op jit(solution)/shard_map/ppermute | solution.py:35
  72.3 0.1 constant_dynamic-update-slice_fusion.2
  72.5 1.9 %collective-permute-start.5 = (bf16[24,256,128]{2,1,0:T(8,128)(2,1)S(1)}, bf16[24,256,128]{2,1,0:T(8,128)(2,1)}, u32[]{:S(2)}, u32[]{:S(2)}) collective-permute-start(bf16[24,256,128]{2,1,0:T(8,128)(2,1)S(1)} %constant_dynamic-update-slice_fusion.refs_2_), channel_id=1, source_target_pairs={{0,1},{1,0},{2,3},{3,2},{4,5},{5,4},{6,7},{7,6},{8,9},{9,8},{10,11... | collective-permute-start | bytes 4718600 | tf_op jit(solution)/shard_map/ppermute | solution.py:35
  74.4 2.4 %collective-permute-start = (bf16[8,256,128]{2,1,0:T(8,128)(2,1)S(1)}, bf16[8,256,128]{2,1,0:T(8,128)(2,1)S(1)}, u32[]{:S(2)}, u32[]{:S(2)}) collective-permute-start(bf16[8,256,128]{2,1,0:T(8,128)(2,1)S(1)} %bitcast.25), channel_id=1, source_target_pairs={{0,1},{1,0},{2,3},{3,2},{4,5},{5,4},{6,7},{7,6},{8,9},{9,8},{10,11... | collective-permute-start | bytes 1572872 | tf_op jit(solution)/shard_map/ppermute | solution.py:35
  76.9 0.1 stack.47.meta_ref
  77.0 1.5 collective-permute-done.refs_1_
  78.5 1.7 %collect.1.features_ref = bf16[8,8,256,128]{3,2,1,0:T(8,128)(2,1)S(1)} custom-call(s32[11]{0:T(128)S(1)} %stack.47.meta_ref, bf16[8,256,128]{2,1,0:T(8,128)(2,1)S(1)} %bitcast.26, bf16[8,256,128]{2,1,0:T(8,128)(2,1)S(1)} %collective-permute-done.refs_1_, bf16[24,256,128]{2,1,0:T(8,128)(2,1)S(1)} %constant_dynamic-update-slice_fusion.refs_2_, ...), custom_call_target="tpu_custom_call" | custom-call | tf_op jit(solution)/shard_map/collect/pallas_call | solution.py:200
  80.3 1.9 %copy-done = bf16[8,8,256,128]{3,2,1,0:T(8,128)(2,1)} copy-done((bf16[8,8,256,128]{3,2,1,0:T(8,128)(2,1)}, bf16[8,8,256,128]{3,2,1,0:T(8,128)(2,1)S(1)}, u32[]{:S(2)}) %copy-start) | copy-done | bytes 4194328
  82.2 15.6 %all-gather.7.cloned.1.call-done = bf16[64,2,128,256]{3,2,1,0:T(8,128)(2,1)} async-done(((bf16[8,2,128,256]{3,2,1,0:T(8,128)(2,1)}), bf16[64,2,128,256]{3,2,1,0:T(8,128)(2,1)}) %all-gather.7.cloned.1.call-update) | async-done | bytes 8388624 | tf_op jit(solution)/shard_map/all_gather | solution.py:187
  97.8 5.6 %drive.1 = (f32[2,384,128]{2,1,0:T(8,128)S(1)}, f32[16,256]{1,0:T(8,128)S(1)}) custom-call(bf16[8,8,256,128]{3,2,1,0:T(8,128)(2,1)} %copy-done, bf16[8,8,2,128,256]{4,3,2,1,0:T(8,128)(2,1)} %bitcast.27, f32[33,256]{1,0:T(8,128)S(1)} %pad_maximum_fusion.filter_ref), custom_call_target="tpu_custom_call" | custom-call | tf_op jit(solution)/shard_map/drive/pallas_call | solution.py:226
  103.5 0.7 broadcast_in_dim.39
  104.1 7.4 %all-to-all-start.1 = ((f32[8,16,256]{2,1,0:T(8,128)}), f32[8,16,256]{2,1,0:T(8,128)S(1)}, u32[]{:S(2)}, u32[]{:S(2)}) async-start(f32[8,16,256]{2,1,0:T(8,128)} %broadcast_in_dim.39), calls=%async_computation.1 | async-start | bytes 262144 | tf_op jit(solution)/shard_map/all_to_all | solution.py:40
  111.5 9.7 %all-to-all-done.1 = f32[8,16,256]{2,1,0:T(8,128)S(1)} async-done(((f32[8,16,256]{2,1,0:T(8,128)}), f32[8,16,256]{2,1,0:T(8,128)S(1)}, u32[]{:S(2)}, u32[]{:S(2)}) %all-to-all-start.1) | async-done | bytes 131104 | tf_op jit(solution)/shard_map/all_to_all | solution.py:40
  121.3 0.1 multiply_reduce_fusion
  121.4 14.0 %all_to_all.16.far_ref = f32[8,16,256]{2,1,0:T(8,128)S(1)} all-to-all(f32[8,16,256]{2,1,0:T(8,128)S(1)} %broadcast_in_dim.40), channel_id=1, replica_groups=mesh['y'=8,'z'=8,'x'=4,'k'=2] {'y'}, dimensions={0} | all-to-all | bytes 262144 | tf_op jit(solution)/shard_map/all_to_all | solution.py:40
  135.4 2.3 %convolve.1 = (f32[2,256,128]{2,1,0:T(8,128)S(1)}, f32[4,16]{1,0:T(4,128)}, f32[1,4]{1,0:T(1,128)}) custom-call(s32[11]{0:T(128)S(1)} %stack.47.meta_ref, f32[2,384,128]{2,1,0:T(8,128)S(1)} %get-tuple-element.8.local_ref, f32[16,256]{1,0:T(8,128)S(1)} %get-tuple-element.14.rows_in_ref, f32[8,16,256]{2,1,0:T(8,128)S(1)} %all_to_all.16.far_ref, ...), custom_call_target="tpu_custom_call" | custom-call | tf_op jit(solution)/shard_map/convolve/pallas_call | solution.py:244
  137.7 7.8 %all-gather.5.cloned.1.call-done = bf16[64,1,128,256]{3,2,1,0:T(8,128)(2,1)} async-done(((bf16[8,1,128,256]{3,2,1,0:T(8,128)(2,1)}), bf16[64,1,128,256]{3,2,1,0:T(8,128)(2,1)}) %all-gather.5.cloned.1.call-update) | async-done | bytes 4194320 | tf_op jit(solution)/shard_map/all_gather | solution.py:187
  145.5 4.7 %mix.1 = bf16[256,256]{1,0:T(8,128)(2,1)} custom-call(bf16[8,8,256,128]{3,2,1,0:T(8,128)(2,1)} %copy-done, bf16[8,8,1,128,256]{4,3,2,1,0:T(8,128)(2,1)} %bitcast.28, f32[2,256,128]{2,1,0:T(8,128)S(1)} %get-tuple-element.10.conv_ref), custom_call_target="tpu_custom_call" | custom-call | tf_op jit(solution)/shard_map/mix/pallas_call | solution.py:252
  (24 shorter events, 0.3 us)
Async XLA Ops:
  7.2 90.7 %all-gather.7.cloned.1.call-start = ((), (), s32[]{:S(2)}) async-start(), calls=%async_computation.4 | async-start | bytes 9437184 | tf_op jit(solution)/shard_map/all_gather | solution.py:187
  44.0 1.1 copy-start.1
  44.0 101.4 %all-gather.5.cloned.1.call-start = ((), (), s32[]{:S(2)}) async-start(), calls=%async_computation.3 | async-start | bytes 4718592 | tf_op jit(solution)/shard_map/all_gather | solution.py:187
  46.8 16.6 %collective-permute-start.1 = (bf16[8,256,128]{2,1,0:T(8,128)(2,1)S(1)}, bf16[8,256,128]{2,1,0:T(8,128)(2,1)S(1)}, u32[]{:S(2)}, u32[]{:S(2)}) collective-permute-start(bf16[8,256,128]{2,1,0:T(8,128)(2,1)S(1)} %bitcast.22), channel_id=1, source_target_pairs={{0,2},{2,4},{4,6},{6,0},{1,3},{3,5},{5,7},{7,1},{8,10},{10,12},{12... | collective-permute-start | bytes 1572872 | tf_op jit(solution)/shard_map/ppermute | solution.py:35
  49.2 23.1 %collective-permute-start.2 = (bf16[8,256,128]{2,1,0:T(8,128)(2,1)S(1)}, bf16[8,256,128]{2,1,0:T(8,128)(2,1)S(1)}, u32[]{:S(2)}, u32[]{:S(2)}) collective-permute-start(bf16[8,256,128]{2,1,0:T(8,128)(2,1)S(1)} %bitcast.23), channel_id=1, source_target_pairs={{0,6},{2,0},{4,2},{6,4},{1,7},{3,1},{5,3},{7,5},{8,14},{10,8},{12,... | collective-permute-start | bytes 1572872 | tf_op jit(solution)/shard_map/ppermute | solution.py:35
  52.7 19.6 %collective-permute-start.3 = (bf16[4,256,128]{2,1,0:T(8,128)(2,1)S(1)}, bf16[4,256,128]{2,1,0:T(8,128)(2,1)S(1)}, u32[]{:S(2)}, u32[]{:S(2)}) collective-permute-start(bf16[4,256,128]{2,1,0:T(8,128)(2,1)S(1)} %get-tuple-element.16), channel_id=1, source_target_pairs={{0,4},{2,6},{4,0},{6,2},{1,5},{3,7},{5,1},{7,3},{8,12},{10,14},{12... | collective-permute-start | bytes 786440 | tf_op jit(solution)/shard_map/ppermute | solution.py:35
  56.0 20.9 %copy-start.2 = (f32[256,16]{0,1:T(8,128)S(1)}, f32[256,16]{0,1:T(8,128)}, u32[]{:S(2)}) copy-start(f32[256,16]{0,1:T(8,128)} %param.7) | copy-start | bytes 49156
  56.1 20.9 %copy-start.3 = (f32[256,16]{0,1:T(8,128)S(1)}, f32[256,16]{0,1:T(8,128)}, u32[]{:S(2)}) copy-start(f32[256,16]{0,1:T(8,128)} %param.8) | copy-start | bytes 49156
  56.1 20.9 %copy-start.4 = (f32[256]{0:T(256)S(1)}, f32[256]{0:T(256)}, u32[]{:S(2)}) copy-start(f32[256]{0:T(256)} %param.9) | copy-start | bytes 3076
  56.1 16.3 %collective-permute-start.4 = (bf16[4,256,128]{2,1,0:T(8,128)(2,1)S(1)}, bf16[4,256,128]{2,1,0:T(8,128)(2,1)S(1)}, u32[]{:S(2)}, u32[]{:S(2)}) collective-permute-start(bf16[4,256,128]{2,1,0:T(8,128)(2,1)S(1)} %get-tuple-element.15), channel_id=1, source_target_pairs={{0,4},{2,6},{4,0},{6,2},{1,5},{3,7},{5,1},{7,3},{8,12},{10,14},{12... | collective-permute-start | bytes 786440 | tf_op jit(solution)/shard_map/ppermute | solution.py:35
  72.5 6.1 %collective-permute-start.5 = (bf16[24,256,128]{2,1,0:T(8,128)(2,1)S(1)}, bf16[24,256,128]{2,1,0:T(8,128)(2,1)}, u32[]{:S(2)}, u32[]{:S(2)}) collective-permute-start(bf16[24,256,128]{2,1,0:T(8,128)(2,1)S(1)} %constant_dynamic-update-slice_fusion.refs_2_), channel_id=1, source_target_pairs={{0,1},{1,0},{2,3},{3,2},{4,5},{5,4},{6,7},{7,6},{8,9},{9,8},{10,11... | collective-permute-start | bytes 4718600 | tf_op jit(solution)/shard_map/ppermute | solution.py:35
  74.4 4.1 %collective-permute-start = (bf16[8,256,128]{2,1,0:T(8,128)(2,1)S(1)}, bf16[8,256,128]{2,1,0:T(8,128)(2,1)S(1)}, u32[]{:S(2)}, u32[]{:S(2)}) collective-permute-start(bf16[8,256,128]{2,1,0:T(8,128)(2,1)S(1)} %bitcast.25), channel_id=1, source_target_pairs={{0,1},{1,0},{2,3},{3,2},{4,5},{5,4},{6,7},{7,6},{8,9},{9,8},{10,11... | collective-permute-start | bytes 1572872 | tf_op jit(solution)/shard_map/ppermute | solution.py:35
  80.3 1.9 %copy-start = (bf16[8,8,256,128]{3,2,1,0:T(8,128)(2,1)}, bf16[8,8,256,128]{3,2,1,0:T(8,128)(2,1)S(1)}, u32[]{:S(2)}) copy-start(bf16[8,8,256,128]{3,2,1,0:T(8,128)(2,1)S(1)} %collect.1.features_ref) | copy-start | bytes 12582916
  104.1 17.1 %all-to-all-start.1 = ((f32[8,16,256]{2,1,0:T(8,128)}), f32[8,16,256]{2,1,0:T(8,128)S(1)}, u32[]{:S(2)}, u32[]{:S(2)}) async-start(f32[8,16,256]{2,1,0:T(8,128)} %broadcast_in_dim.39), calls=%async_computation.1 | async-start | bytes 262144 | tf_op jit(solution)/shard_map/all_to_all | solution.py:40
Sparse Core Ops, SparseCore 0:
  44.1 53.6 all-gather.6
  99.9 45.4 all-gather.4

commit v3 on v2

v3 whole, which is shorter than its diff:
```python
import functools

import jax
import jax.numpy as jnp
from jax import lax
from jax.experimental import pallas as pl
from jax.experimental.pallas import tpu as pltpu
from jax.sharding import Mesh
from jax.sharding import PartitionSpec as P

Y, Z, X, K = 8, 8, 4, 2
LINE = 8
AXES = ("y", "z", "x", "k")
SUB = 8
LANES = 128
EARLY, LATE = (0, 1, -1, 2, -2, 3, -3), (4,)
EXACT = lax.Precision.HIGHEST


def number(y, z, x, k):
    return ((y * Z + z) * X + x) * K + k


def lines(first):
    groups = []
    for k in range(K):
        along_z = (k == 0) == first
        for x in range(X):
            for o in range(LINE):
                groups.append([number(o, i, x, k) if along_z else number(i, o, x, k) for i in range(LINE)])
    return groups


def shifted(array, axis, step):
    size = lax.axis_size(axis)
    return lax.ppermute(array, axis, [(i, (i + step) % size) for i in range(size)])


def to_all(array, axis):
    copies = jnp.broadcast_to(array[None], (lax.psum(1, axis),) + array.shape)
    return lax.all_to_all(copies, axis, 0, 0, tiled=True)


def turned(array, step):
    pairs = [(g[i], g[(i + step) % LINE]) for g in lines(False) for i in range(LINE)]
    return lax.ppermute(array, AXES, pairs)


def collect_kernel(meta_ref, pieces_ref, features_ref, tokens, sems):
    k = meta_ref[0]
    copies = [pltpu.make_async_copy(pieces_ref.at[piece], tokens.at[piece], sems.at[piece]) for piece in range(X * K)]
    for copy in copies:
        copy.start()
    for piece, copy in enumerate(copies):
        copy.wait()
        for block in range(LINE):
            chunk, part = jnp.where(k == 0, piece, block), jnp.where(k == 0, block, piece)
            features_ref[chunk, part] = tokens[piece, :, block * LANES : (block + 1) * LANES]


def multiply(steps, first, meta_ref, features_ref, weight_refs, total, weights, sems):
    streams, _, width = total.shape
    copies = []
    for i in range(len(steps)):
        halves = [ref.at[:, first : first + streams] for ref in (weight_refs[i], weight_refs[len(steps) + i])]
        copies.append([pltpu.make_async_copy(half, weights.at[i, j], sems.at[j, i]) for j, half in enumerate(halves)])
    for group in copies:
        for copy in group:
            copy.start()
    for i, step in enumerate(steps):
        chunk = lax.rem(meta_ref[1] - step + LINE, LINE)
        rows = jnp.concatenate([features_ref[chunk, part] for part in range(LINE)], axis=1)
        for copy in copies[i]:
            copy.wait()
        for stream in range(streams):
            block = weights[i, :, :, stream].reshape(-1, width)
            total[stream] += jnp.dot(rows, block, preferred_element_type=jnp.float32)


def begin_kernel(meta_ref, features_ref, *refs):
    count = 2 * len(EARLY)
    total_ref = refs[count]
    total_ref[...] = jnp.zeros_like(total_ref)
    multiply(EARLY, 1, meta_ref, features_ref, refs[:count], total_ref, *refs[count + 1 :])


def query_kernel(meta_ref, features_ref, *refs):
    steps = EARLY + LATE
    count = 2 * len(steps)
    query_ref, total = refs[count : count + 2]
    total[...] = jnp.zeros_like(total)
    multiply(steps, 0, meta_ref, features_ref, refs[:count], total, *refs[count + 2 :])
    query_ref[...] = total[0].astype(jnp.bfloat16)


def drive_kernel(meta_ref, features_ref, *refs):
    count = 2 * len(LATE)
    total_ref, filter_ref, local_ref, own_ref, ends, total = refs[count : count + 6]
    poles, width = own_ref.shape
    halves, rows = width // LANES, total.shape[1]
    span = rows // SUB
    total[...] = total_ref[...]
    multiply(LATE, 1, meta_ref, features_ref, refs[:count], total, *refs[count + 6 :])
    key, value = (total[stream].astype(jnp.bfloat16).astype(jnp.float32) for stream in range(2))
    for half in range(halves):
        here = slice(half * LANES, half * LANES + LANES)
        local_ref[half, :rows] = key[:, here] * value[:, here]
    for half in range(halves):
        here = slice(half * LANES, half * LANES + LANES)
        keep = [jnp.broadcast_to(jnp.exp(-filter_ref[n : n + 1, here]), (SUB, LANES)) for n in range(poles)]

        def advance(i, states):
            drive = local_ref[half, pl.ds(i, SUB, stride=span), :]
            return [s * a + drive for s, a in zip(states, keep)]

        states = lax.fori_loop(0, span, advance, [jnp.zeros((SUB, LANES), jnp.float32)] * poles, unroll=8)
        for n in range(poles):
            ends[half, n * SUB : (n + 1) * SUB, :] = states[n]
        across = jnp.exp(-filter_ref[:poles, here] * span)
        before = jnp.zeros((poles, LANES), jnp.float32)
        for b in range(SUB):
            local_ref[half, pl.ds(rows + b, poles, stride=SUB), :] = before
            before = before * across + ends[half, pl.ds(b, poles, stride=SUB), :]
        own_ref[:, here] = before


def finish_kernel(meta_ref, query_ref, local_ref, rows_in_ref, far_ref, filter_ref, mixed_ref, unit_ref, scale_ref, conv):
    halves, rows, _ = conv.shape
    poles, width = rows_in_ref.shape
    span = rows // SUB
    y, z = meta_ref[2], meta_ref[3]
    rate = filter_ref[:poles]
    incoming = jnp.zeros_like(rate)
    last = jnp.zeros_like(rate)
    hop = jnp.exp(-rate * (rows * Z))
    for other in range(Y):
        incoming = jnp.where(other < y, incoming * hop + far_ref[other], incoming)
        last = last * hop + far_ref[other]
    incoming = rows_in_ref[...] + incoming * jnp.exp(-rate * (rows * z).astype(jnp.float32))

    block = lax.broadcasted_iota(jnp.int32, (SUB, LANES), 0).astype(jnp.float32) * span
    for half in range(halves):
        here = slice(half * LANES, half * LANES + LANES)
        keep = [jnp.broadcast_to(jnp.exp(-rate[n : n + 1, here]), (SUB, LANES)) for n in range(poles)]
        gain = [jnp.broadcast_to(filter_ref[poles + n : poles + n + 1, here], (SUB, LANES)) for n in range(poles)]
        skip = jnp.broadcast_to(filter_ref[2 * poles : 2 * poles + 1, here], (SUB, LANES))
        states = [
            local_ref[half, rows + n * SUB : rows + (n + 1) * SUB, :] + incoming[n : n + 1, here] * jnp.exp(-rate[n : n + 1, here] * block)
            for n in range(poles)
        ]

        def advance(i, states):
            drive = local_ref[half, pl.ds(i, SUB, stride=span), :]
            states = [s * a + drive for s, a in zip(states, keep)]
            terms = [s * g for s, g in zip(states, gain)]
            while len(terms) > 1:
                terms = [a + b for a, b in zip(terms[::2], terms[1::2])]
            conv[half, pl.ds(i, SUB, stride=span), :] = terms[0] + skip * drive
            return states

        lax.fori_loop(0, span, advance, states, unroll=8)

    query = query_ref[...].astype(jnp.float32)
    for half in range(halves):
        here = slice(half * LANES, half * LANES + LANES)
        mixed_ref[:, here] = (query[:, here] * conv[half]).astype(jnp.bfloat16)

    owned = (y * Z + z) * 4
    pick = lax.broadcasted_iota(jnp.int32, (8, width), 1) == lax.broadcasted_iota(jnp.int32, (8, width), 0) + owned
    pick = pick.astype(jnp.float32)
    contract = (((1,), (1,)), ((), ()))
    state = lax.dot_general(pick, last, contract, precision=EXACT, preferred_element_type=jnp.float32)
    flipped = lax.dot_general(last, pick, contract, precision=EXACT, preferred_element_type=jnp.float32)
    top = jnp.maximum(jnp.max(jnp.abs(state), axis=1, keepdims=True), 1.0)
    unit_ref[...] = (state / top)[:4]
    scale_ref[...] = (jnp.maximum(jnp.max(jnp.abs(flipped), axis=0, keepdims=True), 1.0) / 127.0)[:, :4]


def vmem():
    return pl.BlockSpec(memory_space=pltpu.VMEM)


def in_hbm(array):
    return pltpu.with_memory_space_constraint(array, pltpu.HBM)


def smem():
    return pl.BlockSpec(memory_space=pltpu.SMEM)


def shards(tokens, in_weight, rate, residue, skip_gain):
    rows, depth = tokens.shape
    width, poles = rate.shape
    y, z, x, k = (lax.axis_index(a) for a in AXES)
    f32 = functools.partial(jax.ShapeDtypeStruct, dtype=jnp.float32)
    bf16 = functools.partial(jax.ShapeDtypeStruct, dtype=jnp.bfloat16)

    weights = in_weight.transpose(1, 0, 2)
    copies = jnp.broadcast_to(weights[None], (LINE,) + weights.shape)
    near = lax.all_to_all(copies, AXES, 0, 0, tiled=True, axis_index_groups=lines(True))

    half = LINE // 2
    front, back = near[:half], near[half:]

    lefts, rights = {0: front}, {0: back}
    for sign in (1, -1):
        for line in (lefts, rights):
            for step in (1, 2, 3):
                line[sign * step] = turned(line[sign * (step - 1)], sign)
    lefts[4], rights[4] = turned(lefts[3], 1), turned(rights[-3], -1)

    pieces = to_all(tokens, ("x", "k"))
    meta = jnp.stack([k, jnp.where(k == 0, y, z), y, z]).astype(jnp.int32)
    filters = jnp.concatenate([rate.T, residue.T, skip_gain[None]])
    params = pltpu.CompilerParams(vmem_limit_bytes=20 * 2**20)
    hbm = pl.BlockSpec(memory_space=pltpu.HBM)
    features = pl.pallas_call(
        collect_kernel,
        in_specs=[smem(), hbm],
        out_specs=vmem(),
        out_shape=bf16((LINE, LINE, rows, LANES)),
        scratch_shapes=[pltpu.VMEM((X * K,) + tokens.shape, jnp.bfloat16), pltpu.SemaphoreType.DMA((X * K,))],
        compiler_params=params,
        name="collect",
    )(meta, in_hbm(pieces))

    def chunks(steps):
        return [in_hbm(line[step]) for line in (lefts, rights) for step in steps]

    def buffers(steps, streams):
        return [
            pltpu.VMEM((len(steps), 2, half, streams) + near.shape[2:], jnp.bfloat16),
            pltpu.SemaphoreType.DMA((2, len(steps))),
        ]

    total = pl.pallas_call(
        begin_kernel,
        in_specs=[smem(), vmem()] + [hbm] * (2 * len(EARLY)),
        out_specs=vmem(),
        out_shape=f32((2, rows, width)),
        scratch_shapes=buffers(EARLY, 2),
        compiler_params=params,
        name="begin",
    )(meta, features, *chunks(EARLY))
    local_shape = (width // LANES, rows + poles * SUB, LANES)
    local, own = pl.pallas_call(
        drive_kernel,
        in_specs=[smem(), vmem()] + [hbm] * (2 * len(LATE)) + [vmem()] * 2,
        out_specs=[vmem()] * 2,
        out_shape=[f32(local_shape), f32((poles, width))],
        scratch_shapes=[
            pltpu.VMEM((width // LANES, poles * SUB, LANES), jnp.float32),
            pltpu.VMEM((2, rows, width), jnp.float32),
        ]
        + buffers(LATE, 2),
        compiler_params=params,
        name="drive",
    )(meta, features, *chunks(LATE), total, filters)

    beside = to_all(own, "z")
    at = jnp.arange(Z, dtype=jnp.float32)[:, None, None]
    gap = z.astype(jnp.float32) - 1.0 - at
    row_rate = rate.T[None] * rows
    rows_in = jnp.sum(jnp.where(gap >= 0, jnp.exp(-row_rate * jnp.maximum(gap, 0.0)), 0.0) * beside, axis=0)
    row_sum = jnp.sum(jnp.exp(-row_rate * (Z - 1.0 - at)) * beside, axis=0)
    far = to_all(row_sum, "y")

    query = pl.pallas_call(
        query_kernel,
        in_specs=[smem(), vmem()] + [hbm] * (2 * len(EARLY + LATE)),
        out_specs=vmem(),
        out_shape=bf16((rows, width)),
        scratch_shapes=[pltpu.VMEM((1, rows, width), jnp.float32)] + buffers(EARLY + LATE, 1),
        compiler_params=params,
        name="query",
    )(meta, features, *chunks(EARLY + LATE))
    mixed, unit, scale = pl.pallas_call(
        finish_kernel,
        in_specs=[smem()] + [vmem()] * 5,
        out_specs=[vmem()] * 3,
        out_shape=[bf16((rows, width)), f32((4, poles)), f32((1, 4))],
        scratch_shapes=[pltpu.VMEM((width // LANES, rows, LANES), jnp.float32)],
        compiler_params=params,
        name="finish",
    )(meta, query, local, rows_in, far, filters)
    return mixed, unit, scale.reshape(4)


def solution(mesh):
    fine = Mesh(mesh.devices.reshape(Y, Z, X, K), AXES)
    seq, chan = ("y", "z"), ("x", "k")
    in_specs = (P(seq, chan), P(seq, None, chan), P(chan, None), P(chan, None), P(chan))
    out_specs = (P(seq, chan), P(chan + seq, None), P(chan + seq))
    return jax.shard_map(shards, mesh=fine, in_specs=in_specs, out_specs=out_specs, check_vma=False)
```

time: 158 us -> 152 us (0.962)
  starting transfers between devices: 25.1 us -> 64.1 us
  waiting for transfers between devices: 46.7 us -> 26.3 us
  blocking collectives: 48.6 us -> 34.6 us
  between operations: 15 us -> 1.02 us
  Pallas kernels: 14.4 us -> 17.7 us
    ppermute x6 -> x14, starting transfers between devices: 17.6 us -> 48.1 us  [turned(): return lax.ppermute(array, AXES, pairs)]
    all_gather x2 -> x0, waiting for transfers between devices: 23.4 us -> none  [far_line(): return lax.all_gather(array, AXES, axis=0, axis_index_groups=lines(False))]
    all_to_all x2 -> x1, blocking collectives: 48.6 us -> 34.6 us  [shards(): lax.all_to_all(copies, AXES, 0, 0, tiled=True, axis_index_groups=lines(Tr...]
    all_to_all x1 -> x3, starting transfers between devices: 7.38 us -> 15.9 us  [to_all(): return lax.all_to_all(copies, axis, 0, 0, tiled=True)]
    pallas_call x4 -> x5, Pallas kernels: 14.4 us -> 17.7 us  [the longest x1 5.31 us: shards(): pl.pallas_call(begin_kernel, in_specs=[smem(), vmem()] + [hbm] * (2 * len...]
    broadcast_in_dim x3 -> x4, local copies, waits for them, and re-layouts: 1.76 us -> 5.04 us  [the longest x3 3.89 us: to_all(): copies = jnp.broadcast_to(array[None], (lax.psum(1, axis),) + array.shape)]
    slice x4 -> x1, local copies, waits for them, and re-layouts: 2.46 us -> 0.1 us  [shards(): front, back = (near[:half], near[half:])]
    all_to_all x1 -> x3, waiting for transfers between devices: 9.72 us -> 11.4 us  [to_all(): return lax.all_to_all(copies, axis, 0, 0, tiled=True)]
  transfers between devices with their start and end apart: 9 -> 17, of which waited for: 6 -> 8; matrix products, arithmetic and copies ran while one was open for 2% -> 0% of each run, Pallas kernels for 6% -> 8%
where the time goes in v3:
time: 152 us; the launch traced here: 151 us
  starting transfers between devices  64.1 us (42%)
  blocking collectives  34.6 us (23%)
  waiting for transfers between devices  26.3 us (17%)
  Pallas kernels  17.7 us (12%)
  local copies, waits for them, and re-layouts  7.38 us (5%)
    ppermute x14, starting transfers between devices, turned(): return lax.ppermute(array, AXES, pairs)  48.1 us
    all_to_all x1, blocking collectives, shards(): lax.all_to_all(copies, AXES, 0, 0, tiled=True, axis_index_groups=lines(Tr...  34.6 us
    all_to_all x3, starting transfers between devices, to_all(): return lax.all_to_all(copies, axis, 0, 0, tiled=True)  15.9 us
    ppermute x14, waiting for transfers between devices, turned(): return lax.ppermute(array, AXES, pairs)  14.9 us
    all_to_all x3, waiting for transfers between devices, to_all(): return lax.all_to_all(copies, axis, 0, 0, tiled=True)  11.4 us
    pallas_call x1, Pallas kernels, shards(): pl.pallas_call(begin_kernel, in_specs=[smem(), vmem()] + [hbm] * (2 * len...  5.31 us
    pallas_call x1, Pallas kernels, shards(): pl.pallas_call(query_kernel, in_specs=[smem(), vmem()] + [hbm] * (2 * len...  4.57 us
    broadcast_in_dim x3, local copies, waits for them, and re-layouts, to_all(): copies = jnp.broadcast_to(array[None], (lax.psum(1, axis),) + array.shape)  3.89 us
  transfers between devices with their start and end apart: 17, of which 8 were waited for; matrix products, arithmetic and copies ran while one was open for 0% of the time, Pallas kernels for 8%

profile of v3, /device:TPU:6, one launch (start us, length us, event | category | flops | bytes accessed | tf_op | source)
XLA Modules:
  0.0 151.3 jit_solution(424029694858473664)
XLA Ops:
  1.8 34.6 %all_to_all.20 = bf16[8,3,128,256]{3,2,1,0:T(8,128)(2,1)S(1)} all-to-all(bf16[8,3,128,256]{3,2,1,0:T(8,128)(2,1)S(1)} %broadcast_in_dim.23), channel_id=1, replica_groups={{0,8,16,24,32,40,48,56},{64,72,80,88,96,104,112,120},{128,136,144,152,1..., dimensions={0} | all-to-all | bytes 3145728 | tf_op jit(solution)/shard_map/all_to_all | solution.py:200
  36.4 2.6 %broadcast_in_dim.18 = bf16[8,256,1024]{2,1,0:T(8,128)(2,1)} broadcast(bf16[256,1024]{1,0:T(8,128)(2,1)S(1)} %copy-done.10), dimensions={1,2} | broadcast | bytes 4718592 | tf_op jit(solution)/shard_map/broadcast_in_dim | solution.py:40
  39.0 5.1 %all-to-all-start = ((bf16[8,256,1024]{2,1,0:T(8,128)(2,1)}), bf16[8,256,1024]{2,1,0:T(8,128)(2,1)}, u32[]{:S(2)}, u32[]{:S(2)}) async-start(bf16[8,256,1024]{2,1,0:T(8,128)(2,1)} %broadcast_in_dim.18), calls=%async_computation | async-start | bytes 8388608 | tf_op jit(solution)/shard_map/all_to_all | solution.py:41
  44.2 3.5 %collective-permute-start = (bf16[4,3,128,256]{3,2,1,0:T(8,128)(2,1)S(1)}, bf16[4,3,128,256]{3,2,1,0:T(8,128)(2,1)S(1)}, u32[]{:S(2)}, u32[]{:S(2)}) collective-permute-start(bf16[4,3,128,256]{3,2,1,0:T(8,128)(2,1)S(1)} %get-tuple-element.16.refs_0_), channel_id=1, source_target_pairs={{0,64},{64,128},{128,192},{192,256},{256,320},{320,384},{384,448},... | collective-permute-start | bytes 2359304 | tf_op jit(solution)/shard_map/ppermute | solution.py:46
  47.7 3.8 %collective-permute-start.8 = (bf16[4,3,128,256]{3,2,1,0:T(8,128)(2,1)S(1)}, bf16[4,3,128,256]{3,2,1,0:T(8,128)(2,1)S(1)}, u32[]{:S(2)}, u32[]{:S(2)}) collective-permute-start(bf16[4,3,128,256]{3,2,1,0:T(8,128)(2,1)S(1)} %get-tuple-element.15.refs_8_.refs_7_), channel_id=1, source_target_pairs={{0,448},{64,0},{128,64},{192,128},{256,192},{320,256},{384,320},{4... | collective-permute-start | bytes 2359304 | tf_op jit(solution)/shard_map/ppermute | solution.py:46
  51.5 3.9 %collective-permute-start.1 = (bf16[4,3,128,256]{3,2,1,0:T(8,128)(2,1)S(1)}, bf16[4,3,128,256]{3,2,1,0:T(8,128)(2,1)S(1)}, u32[]{:S(2)}, u32[]{:S(2)}) collective-permute-start(bf16[4,3,128,256]{3,2,1,0:T(8,128)(2,1)S(1)} %get-tuple-element.16.refs_0_), channel_id=1, source_target_pairs={{0,448},{64,0},{128,64},{192,128},{256,192},{320,256},{384,320},{4... | collective-permute-start | bytes 2359304 | tf_op jit(solution)/shard_map/ppermute | solution.py:46
  55.4 1.9 %collective-permute-start.7 = (bf16[4,3,128,256]{3,2,1,0:T(8,128)(2,1)S(1)}, bf16[4,3,128,256]{3,2,1,0:T(8,128)(2,1)S(1)}, u32[]{:S(2)}, u32[]{:S(2)}) collective-permute-start(bf16[4,3,128,256]{3,2,1,0:T(8,128)(2,1)S(1)} %get-tuple-element.15.refs_8_.refs_7_), channel_id=1, source_target_pairs={{0,64},{64,128},{128,192},{192,256},{256,320},{320,384},{384,448},... | collective-permute-start | bytes 2359304 | tf_op jit(solution)/shard_map/ppermute | solution.py:46
  57.4 2.2 %collective-permute-done.refs_1_ = bf16[4,3,128,256]{3,2,1,0:T(8,128)(2,1)S(1)} collective-permute-done((bf16[4,3,128,256]{3,2,1,0:T(8,128)(2,1)S(1)}, bf16[4,3,128,256]{3,2,1,0:T(8,128)(2,1)S(1)}, u32[]{:S(2)}, u32[]{:S(2)}) %collective-permute-start) | collective-permute-done | bytes 786464 | tf_op jit(solution)/shard_map/ppermute | solution.py:46
  59.5 2.0 %collective-permute-start.2 = (bf16[4,3,128,256]{3,2,1,0:T(8,128)(2,1)S(1)}, bf16[4,3,128,256]{3,2,1,0:T(8,128)(2,1)S(1)}, u32[]{:S(2)}, u32[]{:S(2)}) collective-permute-start(bf16[4,3,128,256]{3,2,1,0:T(8,128)(2,1)S(1)} %collective-permute-done.refs_1_), channel_id=1, source_target_pairs={{0,64},{64,128},{128,192},{192,256},{256,320},{320,384},{384,448},... | collective-permute-start | bytes 2359304 | tf_op jit(solution)/shard_map/ppermute | solution.py:46
  61.6 5.0 %collective-permute-start.10 = (bf16[4,3,128,256]{3,2,1,0:T(8,128)(2,1)S(1)}, bf16[4,3,128,256]{3,2,1,0:T(8,128)(2,1)S(1)}, u32[]{:S(2)}, u32[]{:S(2)}) collective-permute-start(bf16[4,3,128,256]{3,2,1,0:T(8,128)(2,1)S(1)} %collective-permute-done.8.refs_10_.refs_9_), channel_id=1, source_target_pairs={{0,448},{64,0},{128,64},{192,128},{256,192},{320,256},{384,320},{4... | collective-permute-start | bytes 2359304 | tf_op jit(solution)/shard_map/ppermute | solution.py:46
  66.6 3.4 %collective-permute-done.1.refs_2_ = bf16[4,3,128,256]{3,2,1,0:T(8,128)(2,1)S(1)} collective-permute-done((bf16[4,3,128,256]{3,2,1,0:T(8,128)(2,1)S(1)}, bf16[4,3,128,256]{3,2,1,0:T(8,128)(2,1)S(1)}, u32[]{:S(2)}, u32[]{:S(2)}) %collective-permute-start.1) | collective-permute-done | bytes 786464 | tf_op jit(solution)/shard_map/ppermute | solution.py:46
  70.0 5.0 %collective-permute-start.3 = (bf16[4,3,128,256]{3,2,1,0:T(8,128)(2,1)S(1)}, bf16[4,3,128,256]{3,2,1,0:T(8,128)(2,1)}, u32[]{:S(2)}, u32[]{:S(2)}) collective-permute-start(bf16[4,3,128,256]{3,2,1,0:T(8,128)(2,1)S(1)} %collective-permute-done.1.refs_2_), channel_id=1, source_target_pairs={{0,448},{64,0},{128,64},{192,128},{256,192},{320,256},{384,320},{4... | collective-permute-start | bytes 2359304 | tf_op jit(solution)/shard_map/ppermute | solution.py:46
  75.0 1.9 %collective-permute-start.9 = (bf16[4,3,128,256]{3,2,1,0:T(8,128)(2,1)S(1)}, bf16[4,3,128,256]{3,2,1,0:T(8,128)(2,1)}, u32[]{:S(2)}, u32[]{:S(2)}) collective-permute-start(bf16[4,3,128,256]{3,2,1,0:T(8,128)(2,1)S(1)} %collective-permute-done.7.refs_9_.refs_8_), channel_id=1, source_target_pairs={{0,64},{64,128},{128,192},{192,256},{256,320},{320,384},{384,448},... | collective-permute-start | bytes 2359304 | tf_op jit(solution)/shard_map/ppermute | solution.py:46
  77.0 2.0 %collective-permute-done.2.refs_3_ = bf16[4,3,128,256]{3,2,1,0:T(8,128)(2,1)S(1)} collective-permute-done((bf16[4,3,128,256]{3,2,1,0:T(8,128)(2,1)S(1)}, bf16[4,3,128,256]{3,2,1,0:T(8,128)(2,1)S(1)}, u32[]{:S(2)}, u32[]{:S(2)}) %collective-permute-start.2) | collective-permute-done | bytes 786464 | tf_op jit(solution)/shard_map/ppermute | solution.py:46
  79.0 1.9 %collective-permute-start.4 = (bf16[4,3,128,256]{3,2,1,0:T(8,128)(2,1)S(1)}, bf16[4,3,128,256]{3,2,1,0:T(8,128)(2,1)}, u32[]{:S(2)}, u32[]{:S(2)}) collective-permute-start(bf16[4,3,128,256]{3,2,1,0:T(8,128)(2,1)S(1)} %collective-permute-done.2.refs_3_), channel_id=1, source_target_pairs={{0,64},{64,128},{128,192},{192,256},{256,320},{320,384},{384,448},... | collective-permute-start | bytes 2359304 | tf_op jit(solution)/shard_map/ppermute | solution.py:46
  80.9 5.1 %collective-permute-start.12 = (bf16[4,3,128,256]{3,2,1,0:T(8,128)(2,1)S(1)}, bf16[4,3,128,256]{3,2,1,0:T(8,128)(2,1)}, u32[]{:S(2)}, u32[]{:S(2)}) collective-permute-start(bf16[4,3,128,256]{3,2,1,0:T(8,128)(2,1)S(1)} %collective-permute-done.10.refs_12_.refs_11_), channel_id=1, source_target_pairs={{0,448},{64,0},{128,64},{192,128},{256,192},{320,256},{384,320},{4... | collective-permute-start | bytes 2359304 | tf_op jit(solution)/shard_map/ppermute | solution.py:46
  87.0 5.0 %collective-permute-start.5 = (bf16[4,3,128,256]{3,2,1,0:T(8,128)(2,1)}, bf16[4,3,128,256]{3,2,1,0:T(8,128)(2,1)}, u32[]{:S(2)}, u32[]{:S(2)}) collective-permute-start(bf16[4,3,128,256]{3,2,1,0:T(8,128)(2,1)} %collective-permute-done.3.refs_4_), channel_id=1, source_target_pairs={{0,448},{64,0},{128,64},{192,128},{256,192},{320,256},{384,320},{4... | collective-permute-start | bytes 2359304 | tf_op jit(solution)/shard_map/ppermute | solution.py:46
  92.0 1.9 %collective-permute-start.11 = (bf16[4,3,128,256]{3,2,1,0:T(8,128)(2,1)}, bf16[4,3,128,256]{3,2,1,0:T(8,128)(2,1)}, u32[]{:S(2)}, u32[]{:S(2)}) collective-permute-start(bf16[4,3,128,256]{3,2,1,0:T(8,128)(2,1)} %collective-permute-done.9.refs_11_.refs_10_), channel_id=1, source_target_pairs={{0,64},{64,128},{128,192},{192,256},{256,320},{320,384},{384,448},... | collective-permute-start | bytes 2359304 | tf_op jit(solution)/shard_map/ppermute | solution.py:46
  93.9 4.7 %collective-permute-done.4.refs_5_ = bf16[4,3,128,256]{3,2,1,0:T(8,128)(2,1)} collective-permute-done((bf16[4,3,128,256]{3,2,1,0:T(8,128)(2,1)S(1)}, bf16[4,3,128,256]{3,2,1,0:T(8,128)(2,1)}, u32[]{:S(2)}, u32[]{:S(2)}) %collective-permute-start.4) | collective-permute-done | bytes 786464 | tf_op jit(solution)/shard_map/ppermute | solution.py:46
  98.7 1.9 %collective-permute-start.6 = (bf16[4,3,128,256]{3,2,1,0:T(8,128)(2,1)}, bf16[4,3,128,256]{3,2,1,0:T(8,128)(2,1)}, u32[]{:S(2)}, u32[]{:S(2)}) collective-permute-start(bf16[4,3,128,256]{3,2,1,0:T(8,128)(2,1)} %collective-permute-done.4.refs_5_), channel_id=1, source_target_pairs={{0,64},{64,128},{128,192},{192,256},{256,320},{320,384},{384,448},... | collective-permute-start | bytes 2359304 | tf_op jit(solution)/shard_map/ppermute | solution.py:46
  100.6 5.1 %collective-permute-start.13 = (bf16[4,3,128,256]{3,2,1,0:T(8,128)(2,1)}, bf16[4,3,128,256]{3,2,1,0:T(8,128)(2,1)}, u32[]{:S(2)}, u32[]{:S(2)}) collective-permute-start(bf16[4,3,128,256]{3,2,1,0:T(8,128)(2,1)} %collective-permute-done.12.refs_14_.refs_13_), channel_id=1, source_target_pairs={{0,448},{64,0},{128,64},{192,128},{256,192},{320,256},{384,320},{4... | collective-permute-start | bytes 2359304 | tf_op jit(solution)/shard_map/ppermute | solution.py:46
  105.9 2.9 %collect.1.features_ref = bf16[8,8,256,128]{3,2,1,0:T(8,128)(2,1)S(1)} custom-call(s32[4]{0:T(128)S(1)} %pad_add_fusion.meta_ref, bf16[8,256,1024]{2,1,0:T(8,128)(2,1)} %all-to-all-done.pieces_ref), custom_call_target="tpu_custom_call" | custom-call | tf_op jit(solution)/shard_map/collect/pallas_call | solution.py:217
  108.8 5.3 %begin.1.refs_2_ = f32[2,256,256]{2,1,0:T(8,128)S(1)} custom-call(s32[4]{0:T(128)S(1)} %pad_add_fusion.meta_ref, bf16[8,8,256,128]{3,2,1,0:T(8,128)(2,1)S(1)} %collect.1.features_ref, bf16[4,3,128,256]{3,2,1,0:T(8,128)(2,1)} %copy-done.3, bf16[4,3,128,256]{3,2,1,0:T(8,128)(2,1)} %copy-done.4, bf16[4,3,128,256]{3,2,1,0:T(8,128)(2,1)} %copy-done.6, ...), custom_call_target="tpu_custom_call" | custom-call | tf_op jit(solution)/shard_map/begin/pallas_call | solution.py:236
  114.1 1.7 %collective-permute-done.6.refs_7_.refs_0_ = bf16[4,3,128,256]{3,2,1,0:T(8,128)(2,1)} collective-permute-done((bf16[4,3,128,256]{3,2,1,0:T(8,128)(2,1)}, bf16[4,3,128,256]{3,2,1,0:T(8,128)(2,1)}, u32[]{:S(2)}, u32[]{:S(2)}) %collective-permute-start.6) | collective-permute-done | bytes 786464 | tf_op jit(solution)/shard_map/ppermute | solution.py:46
  115.8 2.7 %drive.1 = (f32[2,384,128]{2,1,0:T(8,128)S(1)}, f32[16,256]{1,0:T(8,128)S(1)}) custom-call(s32[4]{0:T(128)S(1)} %pad_add_fusion.meta_ref, bf16[8,8,256,128]{3,2,1,0:T(8,128)(2,1)S(1)} %collect.1.features_ref, bf16[4,3,128,256]{3,2,1,0:T(8,128)(2,1)} %collective-permute-done.6.refs_7_.refs_0_, ...), custom_call_target="tpu_custom_call" | custom-call | tf_op jit(solution)/shard_map/drive/pallas_call | solution.py:246
  119.2 4.7 %all-to-all-start.2 = ((f32[8,16,256]{2,1,0:T(8,128)}), f32[8,16,256]{2,1,0:T(8,128)S(1)}, u32[]{:S(2)}, u32[]{:S(2)}) async-start(f32[8,16,256]{2,1,0:T(8,128)} %broadcast_in_dim.46), calls=%async_computation.2 | async-start | bytes 262144 | tf_op jit(solution)/shard_map/all_to_all | solution.py:41
  123.9 9.1 %all-to-all-done.2 = f32[8,16,256]{2,1,0:T(8,128)S(1)} async-done(((f32[8,16,256]{2,1,0:T(8,128)}), f32[8,16,256]{2,1,0:T(8,128)S(1)}, u32[]{:S(2)}, u32[]{:S(2)}) %all-to-all-start.2) | async-done | bytes 131104 | tf_op jit(solution)/shard_map/all_to_all | solution.py:41
  133.8 6.2 %all-to-all-start.3 = ((f32[8,16,256]{2,1,0:T(8,128)}), f32[8,16,256]{2,1,0:T(8,128)S(1)}, u32[]{:S(2)}, u32[]{:S(2)}) async-start(f32[8,16,256]{2,1,0:T(8,128)} %broadcast_in_dim.47), calls=%async_computation.3 | async-start | bytes 262144 | tf_op jit(solution)/shard_map/all_to_all | solution.py:41
  139.9 2.2 %copy-done.1 = bf16[8,8,256,128]{3,2,1,0:T(8,128)(2,1)S(1)} copy-done((bf16[8,8,256,128]{3,2,1,0:T(8,128)(2,1)S(1)}, bf16[8,8,256,128]{3,2,1,0:T(8,128)(2,1)}, u32[]{:S(2)}) %copy-start.1) | copy-done | bytes 4194328
  142.1 4.6 %query.1.query_ref = bf16[256,256]{1,0:T(8,128)(2,1)S(1)} custom-call(s32[4]{0:T(128)S(1)} %pad_add_fusion.meta_ref, bf16[8,8,256,128]{3,2,1,0:T(8,128)(2,1)S(1)} %copy-done.1, bf16[4,3,128,256]{3,2,1,0:T(8,128)(2,1)} %copy-done.3, bf16[4,3,128,256]{3,2,1,0:T(8,128)(2,1)} %copy-done.4, bf16[4,3,128,256]{3,2,1,0:T(8,128)(2,1)} %copy-done.6, ...), custom_call_target="tpu_custom_call" | custom-call | tf_op jit(solution)/shard_map/query/pallas_call | solution.py:268
  146.7 2.3 %all-to-all-done.3.far_ref = f32[8,16,256]{2,1,0:T(8,128)S(1)} async-done(((f32[8,16,256]{2,1,0:T(8,128)}), f32[8,16,256]{2,1,0:T(8,128)S(1)}, u32[]{:S(2)}, u32[]{:S(2)}) %all-to-all-start.3) | async-done | bytes 131104 | tf_op jit(solution)/shard_map/all_to_all | solution.py:41
  149.0 2.3 %finish.1 = (bf16[256,256]{1,0:T(8,128)(2,1)}, f32[4,16]{1,0:T(4,128)}, f32[1,4]{1,0:T(1,128)}) custom-call(s32[4]{0:T(128)S(1)} %pad_add_fusion.meta_ref, bf16[256,256]{1,0:T(8,128)(2,1)S(1)} %query.1.query_ref, f32[2,384,128]{2,1,0:T(8,128)S(1)} %get-tuple-element.8.local_ref, f32[16,256]{1,0:T(8,128)S(1)} %get-tuple-element.14.rows_in_ref, ...), custom_call_target="tpu_custom_call" | custom-call | tf_op jit(solution)/shard_map/finish/pallas_call | solution.py:277
  (47 shorter events, 3.8 us)
Async XLA Ops:
  0.6 35.8 %copy-start.10 = (bf16[256,1024]{1,0:T(8,128)(2,1)S(1)}, bf16[256,1024]{1,0:T(8,128)(2,1)}, u32[]{:S(2)}) copy-start(bf16[256,1024]{1,0:T(8,128)(2,1)} %param.5) | copy-start | bytes 1572868
  39.0 66.8 %copy-start.11 = (f32[256,16]{0,1:T(8,128)S(1)}, f32[256,16]{0,1:T(8,128)}, u32[]{:S(2)}) copy-start(f32[256,16]{0,1:T(8,128)} %param.7) | copy-start | bytes 49156
  39.0 66.8 %copy-start.12 = (f32[256,16]{0,1:T(8,128)S(1)}, f32[256,16]{0,1:T(8,128)}, u32[]{:S(2)}) copy-start(f32[256,16]{0,1:T(8,128)} %param.8) | copy-start | bytes 49156
  39.0 66.9 %copy-start.13 = (f32[256]{0:T(256)S(1)}, f32[256]{0:T(256)}, u32[]{:S(2)}) copy-start(f32[256]{0:T(256)} %param.9) | copy-start | bytes 3076
  39.0 66.9 %all-to-all-start = ((bf16[8,256,1024]{2,1,0:T(8,128)(2,1)}), bf16[8,256,1024]{2,1,0:T(8,128)(2,1)}, u32[]{:S(2)}, u32[]{:S(2)}) async-start(bf16[8,256,1024]{2,1,0:T(8,128)(2,1)} %broadcast_in_dim.18), calls=%async_computation | async-start | bytes 8388608 | tf_op jit(solution)/shard_map/all_to_all | solution.py:41
  44.2 64.6 %copy-start.2 = (bf16[4,3,128,256]{3,2,1,0:T(8,128)(2,1)}, bf16[4,3,128,256]{3,2,1,0:T(8,128)(2,1)S(1)}, u32[]{:S(2)}) copy-start(bf16[4,3,128,256]{3,2,1,0:T(8,128)(2,1)S(1)} %get-tuple-element.15.refs_8_.refs_7_) | copy-start | bytes 2359300
  44.2 64.6 %copy-start.3 = (bf16[4,3,128,256]{3,2,1,0:T(8,128)(2,1)}, bf16[4,3,128,256]{3,2,1,0:T(8,128)(2,1)S(1)}, u32[]{:S(2)}) copy-start(bf16[4,3,128,256]{3,2,1,0:T(8,128)(2,1)S(1)} %get-tuple-element.16.refs_0_) | copy-start | bytes 2359300
  44.2 15.3 %collective-permute-start = (bf16[4,3,128,256]{3,2,1,0:T(8,128)(2,1)S(1)}, bf16[4,3,128,256]{3,2,1,0:T(8,128)(2,1)S(1)}, u32[]{:S(2)}, u32[]{:S(2)}) collective-permute-start(bf16[4,3,128,256]{3,2,1,0:T(8,128)(2,1)S(1)} %get-tuple-element.16.refs_0_), channel_id=1, source_target_pairs={{0,64},{64,128},{128,192},{192,256},{256,320},{320,384},{384,448},... | collective-permute-start | bytes 2359304 | tf_op jit(solution)/shard_map/ppermute | solution.py:46
  47.7 13.9 %collective-permute-start.8 = (bf16[4,3,128,256]{3,2,1,0:T(8,128)(2,1)S(1)}, bf16[4,3,128,256]{3,2,1,0:T(8,128)(2,1)S(1)}, u32[]{:S(2)}, u32[]{:S(2)}) collective-permute-start(bf16[4,3,128,256]{3,2,1,0:T(8,128)(2,1)S(1)} %get-tuple-element.15.refs_8_.refs_7_), channel_id=1, source_target_pairs={{0,448},{64,0},{128,64},{192,128},{256,192},{320,256},{384,320},{4... | collective-permute-start | bytes 2359304 | tf_op jit(solution)/shard_map/ppermute | solution.py:46
  51.5 18.5 %collective-permute-start.1 = (bf16[4,3,128,256]{3,2,1,0:T(8,128)(2,1)S(1)}, bf16[4,3,128,256]{3,2,1,0:T(8,128)(2,1)S(1)}, u32[]{:S(2)}, u32[]{:S(2)}) collective-permute-start(bf16[4,3,128,256]{3,2,1,0:T(8,128)(2,1)S(1)} %get-tuple-element.16.refs_0_), channel_id=1, source_target_pairs={{0,448},{64,0},{128,64},{192,128},{256,192},{320,256},{384,320},{4... | collective-permute-start | bytes 2359304 | tf_op jit(solution)/shard_map/ppermute | solution.py:46
  55.4 19.6 %collective-permute-start.7 = (bf16[4,3,128,256]{3,2,1,0:T(8,128)(2,1)S(1)}, bf16[4,3,128,256]{3,2,1,0:T(8,128)(2,1)S(1)}, u32[]{:S(2)}, u32[]{:S(2)}) collective-permute-start(bf16[4,3,128,256]{3,2,1,0:T(8,128)(2,1)S(1)} %get-tuple-element.15.refs_8_.refs_7_), channel_id=1, source_target_pairs={{0,64},{64,128},{128,192},{192,256},{256,320},{320,384},{384,448},... | collective-permute-start | bytes 2359304 | tf_op jit(solution)/shard_map/ppermute | solution.py:46
  59.5 49.2 %copy-start.4 = (bf16[4,3,128,256]{3,2,1,0:T(8,128)(2,1)}, bf16[4,3,128,256]{3,2,1,0:T(8,128)(2,1)S(1)}, u32[]{:S(2)}) copy-start(bf16[4,3,128,256]{3,2,1,0:T(8,128)(2,1)S(1)} %collective-permute-done.refs_1_) | copy-start | bytes 2359300
  59.5 19.4 %collective-permute-start.2 = (bf16[4,3,128,256]{3,2,1,0:T(8,128)(2,1)S(1)}, bf16[4,3,128,256]{3,2,1,0:T(8,128)(2,1)S(1)}, u32[]{:S(2)}, u32[]{:S(2)}) collective-permute-start(bf16[4,3,128,256]{3,2,1,0:T(8,128)(2,1)S(1)} %collective-permute-done.refs_1_), channel_id=1, source_target_pairs={{0,64},{64,128},{128,192},{192,256},{256,320},{320,384},{384,448},... | collective-permute-start | bytes 2359304 | tf_op jit(solution)/shard_map/ppermute | solution.py:46
  61.6 47.2 %copy-start.5 = (bf16[4,3,128,256]{3,2,1,0:T(8,128)(2,1)}, bf16[4,3,128,256]{3,2,1,0:T(8,128)(2,1)S(1)}, u32[]{:S(2)}) copy-start(bf16[4,3,128,256]{3,2,1,0:T(8,128)(2,1)S(1)} %collective-permute-done.8.refs_10_.refs_9_) | copy-start | bytes 2359300
  61.6 19.3 %collective-permute-start.10 = (bf16[4,3,128,256]{3,2,1,0:T(8,128)(2,1)S(1)}, bf16[4,3,128,256]{3,2,1,0:T(8,128)(2,1)S(1)}, u32[]{:S(2)}, u32[]{:S(2)}) collective-permute-start(bf16[4,3,128,256]{3,2,1,0:T(8,128)(2,1)S(1)} %collective-permute-done.8.refs_10_.refs_9_), channel_id=1, source_target_pairs={{0,448},{64,0},{128,64},{192,128},{256,192},{320,256},{384,320},{4... | collective-permute-start | bytes 2359304 | tf_op jit(solution)/shard_map/ppermute | solution.py:46
  70.0 10.9 %copy-start.6 = (bf16[4,3,128,256]{3,2,1,0:T(8,128)(2,1)}, bf16[4,3,128,256]{3,2,1,0:T(8,128)(2,1)S(1)}, u32[]{:S(2)}) copy-start(bf16[4,3,128,256]{3,2,1,0:T(8,128)(2,1)S(1)} %collective-permute-done.1.refs_2_) | copy-start | bytes 2359300
  70.0 17.0 %collective-permute-start.3 = (bf16[4,3,128,256]{3,2,1,0:T(8,128)(2,1)S(1)}, bf16[4,3,128,256]{3,2,1,0:T(8,128)(2,1)}, u32[]{:S(2)}, u32[]{:S(2)}) collective-permute-start(bf16[4,3,128,256]{3,2,1,0:T(8,128)(2,1)S(1)} %collective-permute-done.1.refs_2_), channel_id=1, source_target_pairs={{0,448},{64,0},{128,64},{192,128},{256,192},{320,256},{384,320},{4... | collective-permute-start | bytes 2359304 | tf_op jit(solution)/shard_map/ppermute | solution.py:46
  75.0 11.9 %copy-start.7 = (bf16[4,3,128,256]{3,2,1,0:T(8,128)(2,1)}, bf16[4,3,128,256]{3,2,1,0:T(8,128)(2,1)S(1)}, u32[]{:S(2)}) copy-start(bf16[4,3,128,256]{3,2,1,0:T(8,128)(2,1)S(1)} %collective-permute-done.7.refs_9_.refs_8_) | copy-start | bytes 2359300
  75.0 16.9 %collective-permute-start.9 = (bf16[4,3,128,256]{3,2,1,0:T(8,128)(2,1)S(1)}, bf16[4,3,128,256]{3,2,1,0:T(8,128)(2,1)}, u32[]{:S(2)}, u32[]{:S(2)}) collective-permute-start(bf16[4,3,128,256]{3,2,1,0:T(8,128)(2,1)S(1)} %collective-permute-done.7.refs_9_.refs_8_), channel_id=1, source_target_pairs={{0,64},{64,128},{128,192},{192,256},{256,320},{320,384},{384,448},... | collective-permute-start | bytes 2359304 | tf_op jit(solution)/shard_map/ppermute | solution.py:46
  79.0 13.0 %copy-start.8 = (bf16[4,3,128,256]{3,2,1,0:T(8,128)(2,1)}, bf16[4,3,128,256]{3,2,1,0:T(8,128)(2,1)S(1)}, u32[]{:S(2)}) copy-start(bf16[4,3,128,256]{3,2,1,0:T(8,128)(2,1)S(1)} %collective-permute-done.2.refs_3_) | copy-start | bytes 2359300
  79.0 19.7 %collective-permute-start.4 = (bf16[4,3,128,256]{3,2,1,0:T(8,128)(2,1)S(1)}, bf16[4,3,128,256]{3,2,1,0:T(8,128)(2,1)}, u32[]{:S(2)}, u32[]{:S(2)}) collective-permute-start(bf16[4,3,128,256]{3,2,1,0:T(8,128)(2,1)S(1)} %collective-permute-done.2.refs_3_), channel_id=1, source_target_pairs={{0,64},{64,128},{128,192},{192,256},{256,320},{320,384},{384,448},... | collective-permute-start | bytes 2359304 | tf_op jit(solution)/shard_map/ppermute | solution.py:46
  80.9 17.8 %copy-start.9 = (bf16[4,3,128,256]{3,2,1,0:T(8,128)(2,1)}, bf16[4,3,128,256]{3,2,1,0:T(8,128)(2,1)S(1)}, u32[]{:S(2)}) copy-start(bf16[4,3,128,256]{3,2,1,0:T(8,128)(2,1)S(1)} %collective-permute-done.10.refs_12_.refs_11_) | copy-start | bytes 2359300
  80.9 19.7 %collective-permute-start.12 = (bf16[4,3,128,256]{3,2,1,0:T(8,128)(2,1)S(1)}, bf16[4,3,128,256]{3,2,1,0:T(8,128)(2,1)}, u32[]{:S(2)}, u32[]{:S(2)}) collective-permute-start(bf16[4,3,128,256]{3,2,1,0:T(8,128)(2,1)S(1)} %collective-permute-done.10.refs_12_.refs_11_), channel_id=1, source_target_pairs={{0,448},{64,0},{128,64},{192,128},{256,192},{320,256},{384,320},{4... | collective-permute-start | bytes 2359304 | tf_op jit(solution)/shard_map/ppermute | solution.py:46
  87.0 21.8 %collective-permute-start.5 = (bf16[4,3,128,256]{3,2,1,0:T(8,128)(2,1)}, bf16[4,3,128,256]{3,2,1,0:T(8,128)(2,1)}, u32[]{:S(2)}, u32[]{:S(2)}) collective-permute-start(bf16[4,3,128,256]{3,2,1,0:T(8,128)(2,1)} %collective-permute-done.3.refs_4_), channel_id=1, source_target_pairs={{0,448},{64,0},{128,64},{192,128},{256,192},{320,256},{384,320},{4... | collective-permute-start | bytes 2359304 | tf_op jit(solution)/shard_map/ppermute | solution.py:46
  92.0 16.8 %collective-permute-start.11 = (bf16[4,3,128,256]{3,2,1,0:T(8,128)(2,1)}, bf16[4,3,128,256]{3,2,1,0:T(8,128)(2,1)}, u32[]{:S(2)}, u32[]{:S(2)}) collective-permute-start(bf16[4,3,128,256]{3,2,1,0:T(8,128)(2,1)} %collective-permute-done.9.refs_11_.refs_10_), channel_id=1, source_target_pairs={{0,64},{64,128},{128,192},{192,256},{256,320},{320,384},{384,448},... | collective-permute-start | bytes 2359304 | tf_op jit(solution)/shard_map/ppermute | solution.py:46
  98.7 17.2 %collective-permute-start.6 = (bf16[4,3,128,256]{3,2,1,0:T(8,128)(2,1)}, bf16[4,3,128,256]{3,2,1,0:T(8,128)(2,1)}, u32[]{:S(2)}, u32[]{:S(2)}) collective-permute-start(bf16[4,3,128,256]{3,2,1,0:T(8,128)(2,1)} %collective-permute-done.4.refs_5_), channel_id=1, source_target_pairs={{0,64},{64,128},{128,192},{192,256},{256,320},{320,384},{384,448},... | collective-permute-start | bytes 2359304 | tf_op jit(solution)/shard_map/ppermute | solution.py:46
  100.6 15.2 %collective-permute-start.13 = (bf16[4,3,128,256]{3,2,1,0:T(8,128)(2,1)}, bf16[4,3,128,256]{3,2,1,0:T(8,128)(2,1)}, u32[]{:S(2)}, u32[]{:S(2)}) collective-permute-start(bf16[4,3,128,256]{3,2,1,0:T(8,128)(2,1)} %collective-permute-done.12.refs_14_.refs_13_), channel_id=1, source_target_pairs={{0,448},{64,0},{128,64},{192,128},{256,192},{320,256},{384,320},{4... | collective-permute-start | bytes 2359304 | tf_op jit(solution)/shard_map/ppermute | solution.py:46
  108.8 7.1 %copy-start = (bf16[8,8,256,128]{3,2,1,0:T(8,128)(2,1)}, bf16[8,8,256,128]{3,2,1,0:T(8,128)(2,1)S(1)}, u32[]{:S(2)}) copy-start(bf16[8,8,256,128]{3,2,1,0:T(8,128)(2,1)S(1)} %collect.1.features_ref) | copy-start | bytes 12582916
  119.2 13.8 %all-to-all-start.2 = ((f32[8,16,256]{2,1,0:T(8,128)}), f32[8,16,256]{2,1,0:T(8,128)S(1)}, u32[]{:S(2)}, u32[]{:S(2)}) async-start(f32[8,16,256]{2,1,0:T(8,128)} %broadcast_in_dim.46), calls=%async_computation.2 | async-start | bytes 262144 | tf_op jit(solution)/shard_map/all_to_all | solution.py:41
  133.8 15.2 %all-to-all-start.3 = ((f32[8,16,256]{2,1,0:T(8,128)}), f32[8,16,256]{2,1,0:T(8,128)S(1)}, u32[]{:S(2)}, u32[]{:S(2)}) async-start(f32[8,16,256]{2,1,0:T(8,128)} %broadcast_in_dim.47), calls=%async_computation.3 | async-start | bytes 262144 | tf_op jit(solution)/shard_map/all_to_all | solution.py:41
  139.9 2.2 %copy-start.1 = (bf16[8,8,256,128]{3,2,1,0:T(8,128)(2,1)S(1)}, bf16[8,8,256,128]{3,2,1,0:T(8,128)(2,1)}, u32[]{:S(2)}) copy-start(bf16[8,8,256,128]{3,2,1,0:T(8,128)(2,1)} %copy-done) | copy-start | bytes 12582916

commit v4 on v3

--- a/solution.py
+++ b/solution.py
@@ -93,14 +93,16 @@
     query_ref[...] = total[0].astype(jnp.bfloat16)
 
 
-def drive_kernel(meta_ref, features_ref, *refs):
-    count = 2 * len(LATE)
-    total_ref, filter_ref, local_ref, own_ref, ends, total = refs[count : count + 6]
-    poles, width = own_ref.shape
-    halves, rows = width // LANES, total.shape[1]
+def drive_kernel(meta_ref, features_ref, front_ref, back_ref, total_ref, filter_ref, local_ref, own_ref, ends):
+    copies, poles, width = own_ref.shape
+    halves, rows = width // LANES, total_ref.shape[1]
     span = rows // SUB
-    total[...] = total_ref[...]
-    multiply(LATE, 1, meta_ref, features_ref, refs[:count], total, *refs[count + 6 :])
+    chunk = lax.rem(meta_ref[1] + LINE // 2, LINE)
+    left = jnp.concatenate([features_ref[chunk, part] for part in range(LINE)], axis=1)
+    total = []
+    for stream in range(2):
+        block = jnp.concatenate([ref[:, 1 + stream].reshape(-1, width) for ref in (front_ref, back_ref)], axis=0)
+        total.append(total_ref[stream] + jnp.dot(left, block, preferred_element_type=jnp.float32))
     key, value = (total[stream].astype(jnp.bfloat16).astype(jnp.float32) for stream in range(2))
     for half in range(halves):
         here = slice(half * LANES, half * LANES + LANES)
@@ -121,7 +123,8 @@
         for b in range(SUB):
             local_ref[half, pl.ds(rows + b, poles, stride=SUB), :] = before
             before = before * across + ends[half, pl.ds(b, poles, stride=SUB), :]
-        own_ref[:, here] = before
+        for copy in range(copies):
+            own_ref[copy, :, here] = before
 
 
 def finish_kernel(meta_ref, query_ref, local_ref, rows_in_ref, far_ref, filter_ref, mixed_ref, unit_ref, scale_ref, conv):
@@ -134,8 +137,9 @@
     last = jnp.zeros_like(rate)
     hop = jnp.exp(-rate * (rows * Z))
     for other in range(Y):
-        incoming = jnp.where(other < y, incoming * hop + far_ref[other], incoming)
-        last = last * hop + far_ref[other]
+        row = far_ref[other]
+        incoming = jnp.where(other < y, incoming * hop + row, incoming)
+        last = last * hop + row
     incoming = rows_in_ref[...] + incoming * jnp.exp(-rate * (rows * z).astype(jnp.float32))
 
     block = lax.broadcasted_iota(jnp.int32, (SUB, LANES), 0).astype(jnp.float32) * span
@@ -225,7 +229,7 @@
     )(meta, in_hbm(pieces))
 
     def chunks(steps):
-        return [in_hbm(line[step]) for line in (lefts, rights) for step in steps]
+        return [line[step] if step in LATE else in_hbm(line[step]) for line in (lefts, rights) for step in steps]
 
     def buffers(steps, streams):
         return [
@@ -245,19 +249,15 @@
     local_shape = (width // LANES, rows + poles * SUB, LANES)
     local, own = pl.pallas_call(
         drive_kernel,
-        in_specs=[smem(), vmem()] + [hbm] * (2 * len(LATE)) + [vmem()] * 2,
+        in_specs=[smem()] + [vmem()] * 5,
         out_specs=[vmem()] * 2,
-        out_shape=[f32(local_shape), f32((poles, width))],
-        scratch_shapes=[
-            pltpu.VMEM((width // LANES, poles * SUB, LANES), jnp.float32),
-            pltpu.VMEM((2, rows, width), jnp.float32),
-        ]
-        + buffers(LATE, 2),
+        out_shape=[f32(local_shape), f32((Z, poles, width))],
+        scratch_shapes=[pltpu.VMEM((width // LANES, poles * SUB, LANES), jnp.float32)],
         compiler_params=params,
         name="drive",
-    )(meta, features, *chunks(LATE), total, filters)
-
-    beside = to_all(own, "z")
+    )(meta, features, lefts[4], rights[4], total, filters)
+
+    beside = lax.all_to_all(own, "z", 0, 0, tiled=True)
     at = jnp.arange(Z, dtype=jnp.float32)[:, None, None]
     gap = z.astype(jnp.float32) - 1.0 - at
     row_rate = rate.T[None] * rows
@@ -267,7 +267,7 @@
 
     query = pl.pallas_call(
         query_kernel,
-        in_specs=[smem(), vmem()] + [hbm] * (2 * len(EARLY + LATE)),
+        in_specs=[smem(), vmem()] + ([hbm] * len(EARLY) + [vmem()]) * 2,
         out_specs=vmem(),
         out_shape=bf16((rows, width)),
         scratch_shapes=[pltpu.VMEM((1, rows, width), jnp.float32)] + buffers(EARLY + LATE, 1),

time: 152 us -> 152 us (level)
    all_to_all x3 -> x2, waiting for transfers between devices: 11.4 us -> 2.31 us  [to_all(): return lax.all_to_all(copies, axis, 0, 0, tiled=True)]
    all_to_all x0 -> x1, waiting for transfers between devices: none -> 9.06 us  [shards(): beside = lax.all_to_all(own, 'z', 0, 0, tiled=True)]
    all_to_all x0 -> x1, starting transfers between devices: none -> 4.71 us  [shards(): beside = lax.all_to_all(own, 'z', 0, 0, tiled=True)]
    all_to_all x3 -> x2, starting transfers between devices: 15.9 us -> 11.2 us  [to_all(): return lax.all_to_all(copies, axis, 0, 0, tiled=True)]
    broadcast_in_dim x3 -> x2, local copies, waits for them, and re-layouts: 3.89 us -> 3.23 us  [to_all(): copies = jnp.broadcast_to(array[None], (lax.psum(1, axis),) + array.shape)]
  transfers between devices with their start and end apart: 17 -> 17, of which waited for: 8 -> 8; matrix products, arithmetic and copies ran while one was open for 0% -> 1% of each run, Pallas kernels for 8% -> 8%
where the time goes in v4:
time: 152 us; the launch traced here: 151 us
  starting transfers between devices  64.1 us (42%)
  blocking collectives  34.7 us (23%)
  waiting for transfers between devices  26.1 us (17%)
  Pallas kernels  17.1 us (11%)
  local copies, waits for them, and re-layouts  8.12 us (5%)
    ppermute x14, starting transfers between devices, turned(): return lax.ppermute(array, AXES, pairs)  48.1 us
    all_to_all x1, blocking collectives, shards(): lax.all_to_all(copies, AXES, 0, 0, tiled=True, axis_index_groups=lines(Tr...  34.7 us
    ppermute x14, waiting for transfers between devices, turned(): return lax.ppermute(array, AXES, pairs)  14.8 us
    all_to_all x2, starting transfers between devices, to_all(): return lax.all_to_all(copies, axis, 0, 0, tiled=True)  11.2 us
    all_to_all x1, waiting for transfers between devices, shards(): beside = lax.all_to_all(own, 'z', 0, 0, tiled=True)  9.06 us
    pallas_call x1, Pallas kernels, shards(): pl.pallas_call(begin_kernel, in_specs=[smem(), vmem()] + [hbm] * (2 * len...  5.31 us
    all_to_all x1, starting transfers between devices, shards(): beside = lax.all_to_all(own, 'z', 0, 0, tiled=True)  4.71 us
    pallas_call x1, Pallas kernels, shards(): pl.pallas_call(query_kernel, in_specs=[smem(), vmem()] + ([hbm] * len(EAR...  4.58 us
  transfers between devices with their start and end apart: 17, of which 8 were waited for; matrix products, arithmetic and copies ran while one was open for 1% of the time, Pallas kernels for 8%

profile of v4, /device:TPU:6, one launch (start us, length us, event | category | flops | bytes accessed | tf_op | source)
XLA Modules:
  0.0 151.5 jit_solution(7616255401797774226)
XLA Ops:
  1.8 34.7 %all_to_all.20 = bf16[8,3,128,256]{3,2,1,0:T(8,128)(2,1)} all-to-all(bf16[8,3,128,256]{3,2,1,0:T(8,128)(2,1)S(1)} %broadcast_in_dim.21), channel_id=1, replica_groups={{0,8,16,24,32,40,48,56},{64,72,80,88,96,104,112,120},{128,136,144,152,1..., dimensions={0} | all-to-all | bytes 3145728 | tf_op jit(solution)/shard_map/all_to_all | solution.py:204
  36.5 2.6 %broadcast_in_dim.20 = bf16[8,256,1024]{2,1,0:T(8,128)(2,1)} broadcast(bf16[256,1024]{1,0:T(8,128)(2,1)S(1)} %copy-done.10), dimensions={1,2} | broadcast | bytes 4718592 | tf_op jit(solution)/shard_map/broadcast_in_dim | solution.py:40
  39.1 5.1 %all-to-all-start = ((bf16[8,256,1024]{2,1,0:T(8,128)(2,1)}), bf16[8,256,1024]{2,1,0:T(8,128)(2,1)}, u32[]{:S(2)}, u32[]{:S(2)}) async-start(bf16[8,256,1024]{2,1,0:T(8,128)(2,1)} %broadcast_in_dim.20), calls=%async_computation | async-start | bytes 8388608 | tf_op jit(solution)/shard_map/all_to_all | solution.py:41
  45.7 3.5 %collective-permute-start = (bf16[4,3,128,256]{3,2,1,0:T(8,128)(2,1)S(1)}, bf16[4,3,128,256]{3,2,1,0:T(8,128)(2,1)S(1)}, u32[]{:S(2)}, u32[]{:S(2)}) collective-permute-start(bf16[4,3,128,256]{3,2,1,0:T(8,128)(2,1)S(1)} %get-tuple-element.16.refs_0_), channel_id=1, source_target_pairs={{0,64},{64,128},{128,192},{192,256},{256,320},{320,384},{384,448},... | collective-permute-start | bytes 2359304 | tf_op jit(solution)/shard_map/ppermute | solution.py:46
  49.2 3.8 %collective-permute-start.8 = (bf16[4,3,128,256]{3,2,1,0:T(8,128)(2,1)S(1)}, bf16[4,3,128,256]{3,2,1,0:T(8,128)(2,1)S(1)}, u32[]{:S(2)}, u32[]{:S(2)}) collective-permute-start(bf16[4,3,128,256]{3,2,1,0:T(8,128)(2,1)S(1)} %get-tuple-element.15.refs_8_.refs_7_), channel_id=1, source_target_pairs={{0,448},{64,0},{128,64},{192,128},{256,192},{320,256},{384,320},{4... | collective-permute-start | bytes 2359304 | tf_op jit(solution)/shard_map/ppermute | solution.py:46
  53.0 3.9 %collective-permute-start.1 = (bf16[4,3,128,256]{3,2,1,0:T(8,128)(2,1)S(1)}, bf16[4,3,128,256]{3,2,1,0:T(8,128)(2,1)S(1)}, u32[]{:S(2)}, u32[]{:S(2)}) collective-permute-start(bf16[4,3,128,256]{3,2,1,0:T(8,128)(2,1)S(1)} %get-tuple-element.16.refs_0_), channel_id=1, source_target_pairs={{0,448},{64,0},{128,64},{192,128},{256,192},{320,256},{384,320},{4... | collective-permute-start | bytes 2359304 | tf_op jit(solution)/shard_map/ppermute | solution.py:46
  57.0 1.9 %collective-permute-start.7 = (bf16[4,3,128,256]{3,2,1,0:T(8,128)(2,1)S(1)}, bf16[4,3,128,256]{3,2,1,0:T(8,128)(2,1)S(1)}, u32[]{:S(2)}, u32[]{:S(2)}) collective-permute-start(bf16[4,3,128,256]{3,2,1,0:T(8,128)(2,1)S(1)} %get-tuple-element.15.refs_8_.refs_7_), channel_id=1, source_target_pairs={{0,64},{64,128},{128,192},{192,256},{256,320},{320,384},{384,448},... | collective-permute-start | bytes 2359304 | tf_op jit(solution)/shard_map/ppermute | solution.py:46
  58.9 2.2 %collective-permute-done.refs_1_ = bf16[4,3,128,256]{3,2,1,0:T(8,128)(2,1)S(1)} collective-permute-done((bf16[4,3,128,256]{3,2,1,0:T(8,128)(2,1)S(1)}, bf16[4,3,128,256]{3,2,1,0:T(8,128)(2,1)S(1)}, u32[]{:S(2)}, u32[]{:S(2)}) %collective-permute-start) | collective-permute-done | bytes 786464 | tf_op jit(solution)/shard_map/ppermute | solution.py:46
  61.1 2.0 %collective-permute-start.2 = (bf16[4,3,128,256]{3,2,1,0:T(8,128)(2,1)S(1)}, bf16[4,3,128,256]{3,2,1,0:T(8,128)(2,1)S(1)}, u32[]{:S(2)}, u32[]{:S(2)}) collective-permute-start(bf16[4,3,128,256]{3,2,1,0:T(8,128)(2,1)S(1)} %collective-permute-done.refs_1_), channel_id=1, source_target_pairs={{0,64},{64,128},{128,192},{192,256},{256,320},{320,384},{384,448},... | collective-permute-start | bytes 2359304 | tf_op jit(solution)/shard_map/ppermute | solution.py:46
  63.1 5.0 %collective-permute-start.10 = (bf16[4,3,128,256]{3,2,1,0:T(8,128)(2,1)S(1)}, bf16[4,3,128,256]{3,2,1,0:T(8,128)(2,1)S(1)}, u32[]{:S(2)}, u32[]{:S(2)}) collective-permute-start(bf16[4,3,128,256]{3,2,1,0:T(8,128)(2,1)S(1)} %collective-permute-done.8.refs_10_.refs_9_), channel_id=1, source_target_pairs={{0,448},{64,0},{128,64},{192,128},{256,192},{320,256},{384,320},{4... | collective-permute-start | bytes 2359304 | tf_op jit(solution)/shard_map/ppermute | solution.py:46
  68.1 3.4 %collective-permute-done.1.refs_2_ = bf16[4,3,128,256]{3,2,1,0:T(8,128)(2,1)S(1)} collective-permute-done((bf16[4,3,128,256]{3,2,1,0:T(8,128)(2,1)S(1)}, bf16[4,3,128,256]{3,2,1,0:T(8,128)(2,1)S(1)}, u32[]{:S(2)}, u32[]{:S(2)}) %collective-permute-start.1) | collective-permute-done | bytes 786464 | tf_op jit(solution)/shard_map/ppermute | solution.py:46
  71.5 5.0 %collective-permute-start.3 = (bf16[4,3,128,256]{3,2,1,0:T(8,128)(2,1)S(1)}, bf16[4,3,128,256]{3,2,1,0:T(8,128)(2,1)}, u32[]{:S(2)}, u32[]{:S(2)}) collective-permute-start(bf16[4,3,128,256]{3,2,1,0:T(8,128)(2,1)S(1)} %collective-permute-done.1.refs_2_), channel_id=1, source_target_pairs={{0,448},{64,0},{128,64},{192,128},{256,192},{320,256},{384,320},{4... | collective-permute-start | bytes 2359304 | tf_op jit(solution)/shard_map/ppermute | solution.py:46
  76.6 1.9 %collective-permute-start.9 = (bf16[4,3,128,256]{3,2,1,0:T(8,128)(2,1)S(1)}, bf16[4,3,128,256]{3,2,1,0:T(8,128)(2,1)}, u32[]{:S(2)}, u32[]{:S(2)}) collective-permute-start(bf16[4,3,128,256]{3,2,1,0:T(8,128)(2,1)S(1)} %collective-permute-done.7.refs_9_.refs_8_), channel_id=1, source_target_pairs={{0,64},{64,128},{128,192},{192,256},{256,320},{320,384},{384,448},... | collective-permute-start | bytes 2359304 | tf_op jit(solution)/shard_map/ppermute | solution.py:46
  78.5 2.0 %collective-permute-done.2.refs_3_ = bf16[4,3,128,256]{3,2,1,0:T(8,128)(2,1)S(1)} collective-permute-done((bf16[4,3,128,256]{3,2,1,0:T(8,128)(2,1)S(1)}, bf16[4,3,128,256]{3,2,1,0:T(8,128)(2,1)S(1)}, u32[]{:S(2)}, u32[]{:S(2)}) %collective-permute-start.2) | collective-permute-done | bytes 786464 | tf_op jit(solution)/shard_map/ppermute | solution.py:46
  80.5 1.9 %collective-permute-start.4 = (bf16[4,3,128,256]{3,2,1,0:T(8,128)(2,1)S(1)}, bf16[4,3,128,256]{3,2,1,0:T(8,128)(2,1)}, u32[]{:S(2)}, u32[]{:S(2)}) collective-permute-start(bf16[4,3,128,256]{3,2,1,0:T(8,128)(2,1)S(1)} %collective-permute-done.2.refs_3_), channel_id=1, source_target_pairs={{0,64},{64,128},{128,192},{192,256},{256,320},{320,384},{384,448},... | collective-permute-start | bytes 2359304 | tf_op jit(solution)/shard_map/ppermute | solution.py:46
  82.4 5.1 %collective-permute-start.12 = (bf16[4,3,128,256]{3,2,1,0:T(8,128)(2,1)S(1)}, bf16[4,3,128,256]{3,2,1,0:T(8,128)(2,1)}, u32[]{:S(2)}, u32[]{:S(2)}) collective-permute-start(bf16[4,3,128,256]{3,2,1,0:T(8,128)(2,1)S(1)} %collective-permute-done.10.refs_12_.refs_11_), channel_id=1, source_target_pairs={{0,448},{64,0},{128,64},{192,128},{256,192},{320,256},{384,320},{4... | collective-permute-start | bytes 2359304 | tf_op jit(solution)/shard_map/ppermute | solution.py:46
  88.5 5.0 %collective-permute-start.5 = (bf16[4,3,128,256]{3,2,1,0:T(8,128)(2,1)}, bf16[4,3,128,256]{3,2,1,0:T(8,128)(2,1)}, u32[]{:S(2)}, u32[]{:S(2)}) collective-permute-start(bf16[4,3,128,256]{3,2,1,0:T(8,128)(2,1)} %collective-permute-done.3.refs_4_), channel_id=1, source_target_pairs={{0,448},{64,0},{128,64},{192,128},{256,192},{320,256},{384,320},{4... | collective-permute-start | bytes 2359304 | tf_op jit(solution)/shard_map/ppermute | solution.py:46
  93.5 1.9 %collective-permute-start.11 = (bf16[4,3,128,256]{3,2,1,0:T(8,128)(2,1)}, bf16[4,3,128,256]{3,2,1,0:T(8,128)(2,1)}, u32[]{:S(2)}, u32[]{:S(2)}) collective-permute-start(bf16[4,3,128,256]{3,2,1,0:T(8,128)(2,1)} %collective-permute-done.9.refs_11_.refs_10_), channel_id=1, source_target_pairs={{0,64},{64,128},{128,192},{192,256},{256,320},{320,384},{384,448},... | collective-permute-start | bytes 2359304 | tf_op jit(solution)/shard_map/ppermute | solution.py:46
  95.4 4.7 %collective-permute-done.4.refs_5_ = bf16[4,3,128,256]{3,2,1,0:T(8,128)(2,1)} collective-permute-done((bf16[4,3,128,256]{3,2,1,0:T(8,128)(2,1)S(1)}, bf16[4,3,128,256]{3,2,1,0:T(8,128)(2,1)}, u32[]{:S(2)}, u32[]{:S(2)}) %collective-permute-start.4) | collective-permute-done | bytes 786464 | tf_op jit(solution)/shard_map/ppermute | solution.py:46
  100.2 1.9 %collective-permute-start.6 = (bf16[4,3,128,256]{3,2,1,0:T(8,128)(2,1)}, bf16[4,3,128,256]{3,2,1,0:T(8,128)(2,1)S(1)}, u32[]{:S(2)}, u32[]{:S(2)}) collective-permute-start(bf16[4,3,128,256]{3,2,1,0:T(8,128)(2,1)} %collective-permute-done.4.refs_5_), channel_id=1, source_target_pairs={{0,64},{64,128},{128,192},{192,256},{256,320},{320,384},{384,448},... | collective-permute-start | bytes 2359304 | tf_op jit(solution)/shard_map/ppermute | solution.py:46
  102.1 5.1 %collective-permute-start.13 = (bf16[4,3,128,256]{3,2,1,0:T(8,128)(2,1)}, bf16[4,3,128,256]{3,2,1,0:T(8,128)(2,1)S(1)}, u32[]{:S(2)}, u32[]{:S(2)}) collective-permute-start(bf16[4,3,128,256]{3,2,1,0:T(8,128)(2,1)} %collective-permute-done.12.refs_14_.refs_13_), channel_id=1, source_target_pairs={{0,448},{64,0},{128,64},{192,128},{256,192},{320,256},{384,320},{4... | collective-permute-start | bytes 2359304 | tf_op jit(solution)/shard_map/ppermute | solution.py:46
  107.4 2.9 %collect.1.features_ref = bf16[8,8,256,128]{3,2,1,0:T(8,128)(2,1)S(1)} custom-call(s32[4]{0:T(128)S(1)} %pad_add_fusion.meta_ref, bf16[8,256,1024]{2,1,0:T(8,128)(2,1)} %all-to-all-done.pieces_ref), custom_call_target="tpu_custom_call" | custom-call | tf_op jit(solution)/shard_map/collect/pallas_call | solution.py:221
  110.4 5.3 %begin.1.total_ref = f32[2,256,256]{2,1,0:T(8,128)S(1)} custom-call(s32[4]{0:T(128)S(1)} %pad_add_fusion.meta_ref, bf16[8,8,256,128]{3,2,1,0:T(8,128)(2,1)S(1)} %collect.1.features_ref, bf16[4,3,128,256]{3,2,1,0:T(8,128)(2,1)} %copy-done.3, bf16[4,3,128,256]{3,2,1,0:T(8,128)(2,1)} %copy-done.4, bf16[4,3,128,256]{3,2,1,0:T(8,128)(2,1)} %copy-done.6, ...), custom_call_target="tpu_custom_call" | custom-call | tf_op jit(solution)/shard_map/begin/pallas_call | solution.py:240
  115.7 1.6 %collective-permute-done.6.refs_7_.front_ref = bf16[4,3,128,256]{3,2,1,0:T(8,128)(2,1)S(1)} collective-permute-done((bf16[4,3,128,256]{3,2,1,0:T(8,128)(2,1)}, bf16[4,3,128,256]{3,2,1,0:T(8,128)(2,1)S(1)}, u32[]{:S(2)}, u32[]{:S(2)}) %collective-permute-start.6) | collective-permute-done | bytes 786464 | tf_op jit(solution)/shard_map/ppermute | solution.py:46
  117.2 2.1 %drive.1 = (f32[2,384,128]{2,1,0:T(8,128)S(1)}, f32[8,16,256]{2,1,0:T(8,128)}) custom-call(s32[4]{0:T(128)S(1)} %pad_add_fusion.meta_ref, bf16[8,8,256,128]{3,2,1,0:T(8,128)(2,1)S(1)} %collect.1.features_ref, bf16[4,3,128,256]{3,2,1,0:T(8,128)(2,1)S(1)} %collective-permute-done.6.refs_7_.front_ref, ...), custom_call_target="tpu_custom_call" | custom-call | tf_op jit(solution)/shard_map/drive/pallas_call | solution.py:250
  119.3 4.7 %all-to-all-start.2 = ((f32[8,16,256]{2,1,0:T(8,128)}), f32[8,16,256]{2,1,0:T(8,128)S(1)}, u32[]{:S(2)}, u32[]{:S(2)}) async-start(f32[8,16,256]{2,1,0:T(8,128)} %get-tuple-element.9), calls=%async_computation.2 | async-start | bytes 262144 | tf_op jit(solution)/shard_map/all_to_all | solution.py:260
  124.1 9.1 %all-to-all-done.2 = f32[8,16,256]{2,1,0:T(8,128)S(1)} async-done(((f32[8,16,256]{2,1,0:T(8,128)}), f32[8,16,256]{2,1,0:T(8,128)S(1)}, u32[]{:S(2)}, u32[]{:S(2)}) %all-to-all-start.2) | async-done | bytes 131104 | tf_op jit(solution)/shard_map/all_to_all | solution.py:260
  133.9 6.2 %all-to-all-start.3 = ((f32[8,16,256]{2,1,0:T(8,128)}), f32[8,16,256]{2,1,0:T(8,128)S(1)}, u32[]{:S(2)}, u32[]{:S(2)}) async-start(f32[8,16,256]{2,1,0:T(8,128)} %broadcast_in_dim.40), calls=%async_computation.3 | async-start | bytes 262144 | tf_op jit(solution)/shard_map/all_to_all | solution.py:41
  140.1 2.2 %copy-done.1 = bf16[8,8,256,128]{3,2,1,0:T(8,128)(2,1)S(1)} copy-done((bf16[8,8,256,128]{3,2,1,0:T(8,128)(2,1)S(1)}, bf16[8,8,256,128]{3,2,1,0:T(8,128)(2,1)}, u32[]{:S(2)}) %copy-start.1) | copy-done | bytes 4194328
  142.3 4.6 %query.1.query_ref = bf16[256,256]{1,0:T(8,128)(2,1)S(1)} custom-call(s32[4]{0:T(128)S(1)} %pad_add_fusion.meta_ref, bf16[8,8,256,128]{3,2,1,0:T(8,128)(2,1)S(1)} %copy-done.1, bf16[4,3,128,256]{3,2,1,0:T(8,128)(2,1)} %copy-done.3, bf16[4,3,128,256]{3,2,1,0:T(8,128)(2,1)} %copy-done.4, bf16[4,3,128,256]{3,2,1,0:T(8,128)(2,1)} %copy-done.6, ...), custom_call_target="tpu_custom_call" | custom-call | tf_op jit(solution)/shard_map/query/pallas_call | solution.py:268
  146.9 2.3 %all-to-all-done.3.far_ref = f32[8,16,256]{2,1,0:T(8,128)S(1)} async-done(((f32[8,16,256]{2,1,0:T(8,128)}), f32[8,16,256]{2,1,0:T(8,128)S(1)}, u32[]{:S(2)}, u32[]{:S(2)}) %all-to-all-start.3) | async-done | bytes 131104 | tf_op jit(solution)/shard_map/all_to_all | solution.py:41
  149.2 2.3 %finish.1 = (bf16[256,256]{1,0:T(8,128)(2,1)}, f32[4,16]{1,0:T(4,128)}, f32[1,4]{1,0:T(1,128)}) custom-call(s32[4]{0:T(128)S(1)} %pad_add_fusion.meta_ref, bf16[256,256]{1,0:T(8,128)(2,1)S(1)} %query.1.query_ref, f32[2,384,128]{2,1,0:T(8,128)S(1)} %get-tuple-element.8.local_ref, f32[16,256]{1,0:T(8,128)S(1)} %get-tuple-element.14.rows_in_ref, ...), custom_call_target="tpu_custom_call" | custom-call | tf_op jit(solution)/shard_map/finish/pallas_call | solution.py:277
  (46 shorter events, 4.5 us)
Async XLA Ops:
  0.6 35.9 %copy-start.10 = (bf16[256,1024]{1,0:T(8,128)(2,1)S(1)}, bf16[256,1024]{1,0:T(8,128)(2,1)}, u32[]{:S(2)}) copy-start(bf16[256,1024]{1,0:T(8,128)(2,1)} %param.5) | copy-start | bytes 1572868
  39.1 68.3 %copy-start.11 = (f32[256,16]{0,1:T(8,128)S(1)}, f32[256,16]{0,1:T(8,128)}, u32[]{:S(2)}) copy-start(f32[256,16]{0,1:T(8,128)} %param.7) | copy-start | bytes 49156
  39.1 68.3 %copy-start.12 = (f32[256,16]{0,1:T(8,128)S(1)}, f32[256,16]{0,1:T(8,128)}, u32[]{:S(2)}) copy-start(f32[256,16]{0,1:T(8,128)} %param.8) | copy-start | bytes 49156
  39.1 68.3 %copy-start.13 = (f32[256]{0:T(256)S(1)}, f32[256]{0:T(256)}, u32[]{:S(2)}) copy-start(f32[256]{0:T(256)} %param.9) | copy-start | bytes 3076
  39.1 68.3 %all-to-all-start = ((bf16[8,256,1024]{2,1,0:T(8,128)(2,1)}), bf16[8,256,1024]{2,1,0:T(8,128)(2,1)}, u32[]{:S(2)}, u32[]{:S(2)}) async-start(bf16[8,256,1024]{2,1,0:T(8,128)(2,1)} %broadcast_in_dim.20), calls=%async_computation | async-start | bytes 8388608 | tf_op jit(solution)/shard_map/all_to_all | solution.py:41
  45.7 49.7 %copy-start.3 = (bf16[4,3,128,256]{3,2,1,0:T(8,128)(2,1)}, bf16[4,3,128,256]{3,2,1,0:T(8,128)(2,1)S(1)}, u32[]{:S(2)}) copy-start(bf16[4,3,128,256]{3,2,1,0:T(8,128)(2,1)S(1)} %get-tuple-element.16.refs_0_) | copy-start | bytes 2359300
  45.7 64.6 %copy-start.2 = (bf16[4,3,128,256]{3,2,1,0:T(8,128)(2,1)}, bf16[4,3,128,256]{3,2,1,0:T(8,128)(2,1)S(1)}, u32[]{:S(2)}) copy-start(bf16[4,3,128,256]{3,2,1,0:T(8,128)(2,1)S(1)} %get-tuple-element.15.refs_8_.refs_7_) | copy-start | bytes 2359300
  45.7 15.3 %collective-permute-start = (bf16[4,3,128,256]{3,2,1,0:T(8,128)(2,1)S(1)}, bf16[4,3,128,256]{3,2,1,0:T(8,128)(2,1)S(1)}, u32[]{:S(2)}, u32[]{:S(2)}) collective-permute-start(bf16[4,3,128,256]{3,2,1,0:T(8,128)(2,1)S(1)} %get-tuple-element.16.refs_0_), channel_id=1, source_target_pairs={{0,64},{64,128},{128,192},{192,256},{256,320},{320,384},{384,448},... | collective-permute-start | bytes 2359304 | tf_op jit(solution)/shard_map/ppermute | solution.py:46
  49.2 13.9 %collective-permute-start.8 = (bf16[4,3,128,256]{3,2,1,0:T(8,128)(2,1)S(1)}, bf16[4,3,128,256]{3,2,1,0:T(8,128)(2,1)S(1)}, u32[]{:S(2)}, u32[]{:S(2)}) collective-permute-start(bf16[4,3,128,256]{3,2,1,0:T(8,128)(2,1)S(1)} %get-tuple-element.15.refs_8_.refs_7_), channel_id=1, source_target_pairs={{0,448},{64,0},{128,64},{192,128},{256,192},{320,256},{384,320},{4... | collective-permute-start | bytes 2359304 | tf_op jit(solution)/shard_map/ppermute | solution.py:46
  53.0 18.5 %collective-permute-start.1 = (bf16[4,3,128,256]{3,2,1,0:T(8,128)(2,1)S(1)}, bf16[4,3,128,256]{3,2,1,0:T(8,128)(2,1)S(1)}, u32[]{:S(2)}, u32[]{:S(2)}) collective-permute-start(bf16[4,3,128,256]{3,2,1,0:T(8,128)(2,1)S(1)} %get-tuple-element.16.refs_0_), channel_id=1, source_target_pairs={{0,448},{64,0},{128,64},{192,128},{256,192},{320,256},{384,320},{4... | collective-permute-start | bytes 2359304 | tf_op jit(solution)/shard_map/ppermute | solution.py:46
  57.0 19.6 %collective-permute-start.7 = (bf16[4,3,128,256]{3,2,1,0:T(8,128)(2,1)S(1)}, bf16[4,3,128,256]{3,2,1,0:T(8,128)(2,1)S(1)}, u32[]{:S(2)}, u32[]{:S(2)}) collective-permute-start(bf16[4,3,128,256]{3,2,1,0:T(8,128)(2,1)S(1)} %get-tuple-element.15.refs_8_.refs_7_), channel_id=1, source_target_pairs={{0,64},{64,128},{128,192},{192,256},{256,320},{320,384},{384,448},... | collective-permute-start | bytes 2359304 | tf_op jit(solution)/shard_map/ppermute | solution.py:46
  61.1 49.3 %copy-start.4 = (bf16[4,3,128,256]{3,2,1,0:T(8,128)(2,1)}, bf16[4,3,128,256]{3,2,1,0:T(8,128)(2,1)S(1)}, u32[]{:S(2)}) copy-start(bf16[4,3,128,256]{3,2,1,0:T(8,128)(2,1)S(1)} %collective-permute-done.refs_1_) | copy-start | bytes 2359300
  61.1 19.4 %collective-permute-start.2 = (bf16[4,3,128,256]{3,2,1,0:T(8,128)(2,1)S(1)}, bf16[4,3,128,256]{3,2,1,0:T(8,128)(2,1)S(1)}, u32[]{:S(2)}, u32[]{:S(2)}) collective-permute-start(bf16[4,3,128,256]{3,2,1,0:T(8,128)(2,1)S(1)} %collective-permute-done.refs_1_), channel_id=1, source_target_pairs={{0,64},{64,128},{128,192},{192,256},{256,320},{320,384},{384,448},... | collective-permute-start | bytes 2359304 | tf_op jit(solution)/shard_map/ppermute | solution.py:46
  63.1 39.0 %copy-start.5 = (bf16[4,3,128,256]{3,2,1,0:T(8,128)(2,1)}, bf16[4,3,128,256]{3,2,1,0:T(8,128)(2,1)S(1)}, u32[]{:S(2)}) copy-start(bf16[4,3,128,256]{3,2,1,0:T(8,128)(2,1)S(1)} %collective-permute-done.8.refs_10_.refs_9_) | copy-start | bytes 2359300
  63.1 19.3 %collective-permute-start.10 = (bf16[4,3,128,256]{3,2,1,0:T(8,128)(2,1)S(1)}, bf16[4,3,128,256]{3,2,1,0:T(8,128)(2,1)S(1)}, u32[]{:S(2)}, u32[]{:S(2)}) collective-permute-start(bf16[4,3,128,256]{3,2,1,0:T(8,128)(2,1)S(1)} %collective-permute-done.8.refs_10_.refs_9_), channel_id=1, source_target_pairs={{0,448},{64,0},{128,64},{192,128},{256,192},{320,256},{384,320},{4... | collective-permute-start | bytes 2359304 | tf_op jit(solution)/shard_map/ppermute | solution.py:46
  71.5 30.6 %copy-start.6 = (bf16[4,3,128,256]{3,2,1,0:T(8,128)(2,1)}, bf16[4,3,128,256]{3,2,1,0:T(8,128)(2,1)S(1)}, u32[]{:S(2)}) copy-start(bf16[4,3,128,256]{3,2,1,0:T(8,128)(2,1)S(1)} %collective-permute-done.1.refs_2_) | copy-start | bytes 2359300
  71.5 17.0 %collective-permute-start.3 = (bf16[4,3,128,256]{3,2,1,0:T(8,128)(2,1)S(1)}, bf16[4,3,128,256]{3,2,1,0:T(8,128)(2,1)}, u32[]{:S(2)}, u32[]{:S(2)}) collective-permute-start(bf16[4,3,128,256]{3,2,1,0:T(8,128)(2,1)S(1)} %collective-permute-done.1.refs_2_), channel_id=1, source_target_pairs={{0,448},{64,0},{128,64},{192,128},{256,192},{320,256},{384,320},{4... | collective-permute-start | bytes 2359304 | tf_op jit(solution)/shard_map/ppermute | solution.py:46
  76.5 30.7 %copy-start.7 = (bf16[4,3,128,256]{3,2,1,0:T(8,128)(2,1)}, bf16[4,3,128,256]{3,2,1,0:T(8,128)(2,1)S(1)}, u32[]{:S(2)}) copy-start(bf16[4,3,128,256]{3,2,1,0:T(8,128)(2,1)S(1)} %collective-permute-done.7.refs_9_.refs_8_) | copy-start | bytes 2359300
  76.6 16.9 %collective-permute-start.9 = (bf16[4,3,128,256]{3,2,1,0:T(8,128)(2,1)S(1)}, bf16[4,3,128,256]{3,2,1,0:T(8,128)(2,1)}, u32[]{:S(2)}, u32[]{:S(2)}) collective-permute-start(bf16[4,3,128,256]{3,2,1,0:T(8,128)(2,1)S(1)} %collective-permute-done.7.refs_9_.refs_8_), channel_id=1, source_target_pairs={{0,64},{64,128},{128,192},{192,256},{256,320},{320,384},{384,448},... | collective-permute-start | bytes 2359304 | tf_op jit(solution)/shard_map/ppermute | solution.py:46
  80.5 26.8 %copy-start.8 = (bf16[4,3,128,256]{3,2,1,0:T(8,128)(2,1)}, bf16[4,3,128,256]{3,2,1,0:T(8,128)(2,1)S(1)}, u32[]{:S(2)}) copy-start(bf16[4,3,128,256]{3,2,1,0:T(8,128)(2,1)S(1)} %collective-permute-done.2.refs_3_) | copy-start | bytes 2359300
  80.5 19.7 %collective-permute-start.4 = (bf16[4,3,128,256]{3,2,1,0:T(8,128)(2,1)S(1)}, bf16[4,3,128,256]{3,2,1,0:T(8,128)(2,1)}, u32[]{:S(2)}, u32[]{:S(2)}) collective-permute-start(bf16[4,3,128,256]{3,2,1,0:T(8,128)(2,1)S(1)} %collective-permute-done.2.refs_3_), channel_id=1, source_target_pairs={{0,64},{64,128},{128,192},{192,256},{256,320},{320,384},{384,448},... | collective-permute-start | bytes 2359304 | tf_op jit(solution)/shard_map/ppermute | solution.py:46
  82.4 24.9 %copy-start.9 = (bf16[4,3,128,256]{3,2,1,0:T(8,128)(2,1)}, bf16[4,3,128,256]{3,2,1,0:T(8,128)(2,1)S(1)}, u32[]{:S(2)}) copy-start(bf16[4,3,128,256]{3,2,1,0:T(8,128)(2,1)S(1)} %collective-permute-done.10.refs_12_.refs_11_) | copy-start | bytes 2359300
  82.4 19.7 %collective-permute-start.12 = (bf16[4,3,128,256]{3,2,1,0:T(8,128)(2,1)S(1)}, bf16[4,3,128,256]{3,2,1,0:T(8,128)(2,1)}, u32[]{:S(2)}, u32[]{:S(2)}) collective-permute-start(bf16[4,3,128,256]{3,2,1,0:T(8,128)(2,1)S(1)} %collective-permute-done.10.refs_12_.refs_11_), channel_id=1, source_target_pairs={{0,448},{64,0},{128,64},{192,128},{256,192},{320,256},{384,320},{4... | collective-permute-start | bytes 2359304 | tf_op jit(solution)/shard_map/ppermute | solution.py:46
  88.5 21.9 %collective-permute-start.5 = (bf16[4,3,128,256]{3,2,1,0:T(8,128)(2,1)}, bf16[4,3,128,256]{3,2,1,0:T(8,128)(2,1)}, u32[]{:S(2)}, u32[]{:S(2)}) collective-permute-start(bf16[4,3,128,256]{3,2,1,0:T(8,128)(2,1)} %collective-permute-done.3.refs_4_), channel_id=1, source_target_pairs={{0,448},{64,0},{128,64},{192,128},{256,192},{320,256},{384,320},{4... | collective-permute-start | bytes 2359304 | tf_op jit(solution)/shard_map/ppermute | solution.py:46
  93.5 16.8 %collective-permute-start.11 = (bf16[4,3,128,256]{3,2,1,0:T(8,128)(2,1)}, bf16[4,3,128,256]{3,2,1,0:T(8,128)(2,1)}, u32[]{:S(2)}, u32[]{:S(2)}) collective-permute-start(bf16[4,3,128,256]{3,2,1,0:T(8,128)(2,1)} %collective-permute-done.9.refs_11_.refs_10_), channel_id=1, source_target_pairs={{0,64},{64,128},{128,192},{192,256},{256,320},{320,384},{384,448},... | collective-permute-start | bytes 2359304 | tf_op jit(solution)/shard_map/ppermute | solution.py:46
  100.2 17.1 %collective-permute-start.6 = (bf16[4,3,128,256]{3,2,1,0:T(8,128)(2,1)}, bf16[4,3,128,256]{3,2,1,0:T(8,128)(2,1)S(1)}, u32[]{:S(2)}, u32[]{:S(2)}) collective-permute-start(bf16[4,3,128,256]{3,2,1,0:T(8,128)(2,1)} %collective-permute-done.4.refs_5_), channel_id=1, source_target_pairs={{0,64},{64,128},{128,192},{192,256},{256,320},{320,384},{384,448},... | collective-permute-start | bytes 2359304 | tf_op jit(solution)/shard_map/ppermute | solution.py:46
  102.1 15.1 %collective-permute-start.13 = (bf16[4,3,128,256]{3,2,1,0:T(8,128)(2,1)}, bf16[4,3,128,256]{3,2,1,0:T(8,128)(2,1)S(1)}, u32[]{:S(2)}, u32[]{:S(2)}) collective-permute-start(bf16[4,3,128,256]{3,2,1,0:T(8,128)(2,1)} %collective-permute-done.12.refs_14_.refs_13_), channel_id=1, source_target_pairs={{0,448},{64,0},{128,64},{192,128},{256,192},{320,256},{384,320},{4... | collective-permute-start | bytes 2359304 | tf_op jit(solution)/shard_map/ppermute | solution.py:46
  110.3 6.9 %copy-start = (bf16[8,8,256,128]{3,2,1,0:T(8,128)(2,1)}, bf16[8,8,256,128]{3,2,1,0:T(8,128)(2,1)S(1)}, u32[]{:S(2)}) copy-start(bf16[8,8,256,128]{3,2,1,0:T(8,128)(2,1)S(1)} %collect.1.features_ref) | copy-start | bytes 12582916
  119.3 13.8 %all-to-all-start.2 = ((f32[8,16,256]{2,1,0:T(8,128)}), f32[8,16,256]{2,1,0:T(8,128)S(1)}, u32[]{:S(2)}, u32[]{:S(2)}) async-start(f32[8,16,256]{2,1,0:T(8,128)} %get-tuple-element.9), calls=%async_computation.2 | async-start | bytes 262144 | tf_op jit(solution)/shard_map/all_to_all | solution.py:260
  133.9 15.3 %all-to-all-start.3 = ((f32[8,16,256]{2,1,0:T(8,128)}), f32[8,16,256]{2,1,0:T(8,128)S(1)}, u32[]{:S(2)}, u32[]{:S(2)}) async-start(f32[8,16,256]{2,1,0:T(8,128)} %broadcast_in_dim.40), calls=%async_computation.3 | async-start | bytes 262144 | tf_op jit(solution)/shard_map/all_to_all | solution.py:41
  140.1 2.2 %copy-start.1 = (bf16[8,8,256,128]{3,2,1,0:T(8,128)(2,1)S(1)}, bf16[8,8,256,128]{3,2,1,0:T(8,128)(2,1)}, u32[]{:S(2)}) copy-start(bf16[8,8,256,128]{3,2,1,0:T(8,128)(2,1)} %copy-done) | copy-start | bytes 12582916

commit v5 on v3

--- a/solution.py
+++ b/solution.py
@@ -44,6 +44,17 @@
 def turned(array, step):
     pairs = [(g[i], g[(i + step) % LINE]) for g in lines(False) for i in range(LINE)]
     return lax.ppermute(array, AXES, pairs)
+
+
+def copies_kernel(array_ref, copies_ref, held, load_sem, sems):
+    load = pltpu.make_async_copy(array_ref, held, load_sem)
+    load.start()
+    load.wait()
+    stores = [pltpu.make_async_copy(held, copies_ref.at[i], sems.at[i]) for i in range(copies_ref.shape[0])]
+    for store in stores:
+        store.start()
+    for store in stores:
+        store.wait()
 
 
 def collect_kernel(meta_ref, pieces_ref, features_ref, tokens, sems):
@@ -209,7 +220,20 @@
                 line[sign * step] = turned(line[sign * (step - 1)], sign)
     lefts[4], rights[4] = turned(lefts[3], 1), turned(rights[-3], -1)
 
-    pieces = to_all(tokens, ("x", "k"))
+    hbm = pl.BlockSpec(memory_space=pltpu.HBM)
+    token_copies = pl.pallas_call(
+        copies_kernel,
+        in_specs=[hbm],
+        out_specs=hbm,
+        out_shape=bf16((X * K,) + tokens.shape),
+        scratch_shapes=[
+            pltpu.VMEM(tokens.shape, jnp.bfloat16),
+            pltpu.SemaphoreType.DMA(()),
+            pltpu.SemaphoreType.DMA((X * K,)),
+        ],
+        name="copies",
+    )(tokens)
+    pieces = lax.all_to_all(token_copies, ("x", "k"), 0, 0, tiled=True)
     meta = jnp.stack([k, jnp.where(k == 0, y, z), y, z]).astype(jnp.int32)
     filters = jnp.concatenate([rate.T, residue.T, skip_gain[None]])
     params = pltpu.CompilerParams(vmem_limit_bytes=20 * 2**20)

time: 152 us -> 151 us (level)
  blocking collectives: 34.6 us -> 0 us
  waiting for transfers between devices: 26.3 us -> 47.7 us
  starting transfers between devices: 64.1 us -> 74.3 us
  Pallas kernels: 17.7 us -> 20.8 us
    all_to_all x1 -> x0, blocking collectives: 34.6 us -> none  [shards(): lax.all_to_all(copies, AXES, 0, 0, tiled=True, axis_index_groups=lines(Tr...]
    all_to_all x0 -> x2, waiting for transfers between devices: none -> 21.4 us  [the longest x1 21.4 us: shards(): lax.all_to_all(copies, AXES, 0, 0, tiled=True, axis_index_groups=lines(Tr...]
    all_to_all x0 -> x2, starting transfers between devices: none -> 15.3 us  [the longest x1 10.3 us: shards(): lax.all_to_all(copies, AXES, 0, 0, tiled=True, axis_index_groups=lines(Tr...]
    all_to_all x3 -> x2, starting transfers between devices: 15.9 us -> 10.9 us  [to_all(): return lax.all_to_all(copies, axis, 0, 0, tiled=True)]
    pallas_call x0 -> x1, Pallas kernels: none -> 3.08 us  [shards(): pl.pallas_call(copies_kernel, in_specs=[hbm], out_specs=hbm, out_shape=bf...]
    broadcast_in_dim x3 -> x2, local copies, waits for them, and re-layouts: 3.89 us -> 1.33 us  [to_all(): copies = jnp.broadcast_to(array[None], (lax.psum(1, axis),) + array.shape)]
    all_to_all x3 -> x2, waiting for transfers between devices: 11.4 us -> 11.4 us  [to_all(): return lax.all_to_all(copies, axis, 0, 0, tiled=True)]
  transfers between devices with their start and end apart: 17 -> 18, of which waited for: 8 -> 9; matrix products, arithmetic and copies ran while one was open for 0% -> 0% of each run, Pallas kernels for 8% -> 11%
where the time goes in v5:
time: 151 us; the launch traced here: 150 us
  starting transfers between devices  74.3 us (49%)
  waiting for transfers between devices  47.7 us (32%)
  Pallas kernels  20.8 us (14%)
  local copies, waits for them, and re-layouts  5.93 us (4%)
    ppermute x14, starting transfers between devices, turned(): return lax.ppermute(array, AXES, pairs)  48.1 us
    all_to_all x1, waiting for transfers between devices, shards(): lax.all_to_all(copies, AXES, 0, 0, tiled=True, axis_index_groups=lines(Tr...  21.4 us
    ppermute x14, waiting for transfers between devices, turned(): return lax.ppermute(array, AXES, pairs)  14.9 us
    all_to_all x2, waiting for transfers between devices, to_all(): return lax.all_to_all(copies, axis, 0, 0, tiled=True)  11.4 us
    all_to_all x2, starting transfers between devices, to_all(): return lax.all_to_all(copies, axis, 0, 0, tiled=True)  10.9 us
    all_to_all x1, starting transfers between devices, shards(): lax.all_to_all(copies, AXES, 0, 0, tiled=True, axis_index_groups=lines(Tr...  10.3 us
    pallas_call x1, Pallas kernels, shards(): pl.pallas_call(begin_kernel, in_specs=[smem(), vmem()] + [hbm] * (2 * len...  5.31 us
    all_to_all x1, starting transfers between devices, shards(): pieces = lax.all_to_all(token_copies, ('x', 'k'), 0, 0, tiled=True)  4.96 us
  transfers between devices with their start and end apart: 18, of which 9 were waited for; matrix products, arithmetic and copies ran while one was open for 0% of the time, Pallas kernels for 11%

profile of v5, /device:TPU:6, one launch (start us, length us, event | category | flops | bytes accessed | tf_op | source)
XLA Modules:
  0.0 150.0 jit_solution(11312627373124152969)
XLA Ops:
  0.6 2.3 %broadcast_in_dim.20 = bf16[8,3,128,256]{3,2,1,0:T(8,128)(2,1)} broadcast(bf16[3,128,256]{2,1,0:T(8,128)(2,1)} %bitcast.10), dimensions={1,2,3} | broadcast | bytes 1769472 | tf_op jit(solution)/shard_map/broadcast_in_dim | solution.py:210
  2.9 10.3 %all-to-all-start.1 = ((bf16[8,3,128,256]{3,2,1,0:T(8,128)(2,1)}), bf16[8,3,128,256]{3,2,1,0:T(8,128)(2,1)S(1)}, u32[]{:S(2)}, u32[]{:S(2)}) async-start(bf16[8,3,128,256]{3,2,1,0:T(8,128)(2,1)} %broadcast_in_dim.20), calls=%async_computation.1 | async-start | bytes 3145728 | tf_op jit(solution)/shard_map/all_to_all | solution.py:211
  13.2 3.1 %copies.1 = bf16[8,256,1024]{2,1,0:T(8,128)(2,1)} custom-call(bf16[256,1024]{1,0:T(8,128)(2,1)} %array_ref.1), custom_call_target="tpu_custom_call" | custom-call | tf_op jit(solution)/shard_map/copies/pallas_call | solution.py:224
  16.3 21.4 %all-to-all-done.1 = bf16[8,3,128,256]{3,2,1,0:T(8,128)(2,1)S(1)} async-done(((bf16[8,3,128,256]{3,2,1,0:T(8,128)(2,1)}), bf16[8,3,128,256]{3,2,1,0:T(8,128)(2,1)S(1)}, u32[]{:S(2)}, u32[]{:S(2)}) %all-to-all-start.1) | async-done | bytes 1572896 | tf_op jit(solution)/shard_map/all_to_all | solution.py:211
  37.7 5.0 %all-to-all-start = ((bf16[8,256,1024]{2,1,0:T(8,128)(2,1)}), bf16[8,256,1024]{2,1,0:T(8,128)(2,1)}, u32[]{:S(2)}, u32[]{:S(2)}) async-start(bf16[8,256,1024]{2,1,0:T(8,128)(2,1)} %copies.1), calls=%async_computation | async-start | bytes 8388608 | tf_op jit(solution)/shard_map/all_to_all | solution.py:236
  42.8 3.5 %collective-permute-start = (bf16[4,3,128,256]{3,2,1,0:T(8,128)(2,1)S(1)}, bf16[4,3,128,256]{3,2,1,0:T(8,128)(2,1)S(1)}, u32[]{:S(2)}, u32[]{:S(2)}) collective-permute-start(bf16[4,3,128,256]{3,2,1,0:T(8,128)(2,1)S(1)} %get-tuple-element.16.refs_0_), channel_id=1, source_target_pairs={{0,64},{64,128},{128,192},{192,256},{256,320},{320,384},{384,448},... | collective-permute-start | bytes 2359304 | tf_op jit(solution)/shard_map/ppermute | solution.py:46
  46.3 3.8 %collective-permute-start.8 = (bf16[4,3,128,256]{3,2,1,0:T(8,128)(2,1)S(1)}, bf16[4,3,128,256]{3,2,1,0:T(8,128)(2,1)S(1)}, u32[]{:S(2)}, u32[]{:S(2)}) collective-permute-start(bf16[4,3,128,256]{3,2,1,0:T(8,128)(2,1)S(1)} %get-tuple-element.15.refs_8_.refs_7_), channel_id=1, source_target_pairs={{0,448},{64,0},{128,64},{192,128},{256,192},{320,256},{384,320},{4... | collective-permute-start | bytes 2359304 | tf_op jit(solution)/shard_map/ppermute | solution.py:46
  50.1 3.9 %collective-permute-start.1 = (bf16[4,3,128,256]{3,2,1,0:T(8,128)(2,1)S(1)}, bf16[4,3,128,256]{3,2,1,0:T(8,128)(2,1)S(1)}, u32[]{:S(2)}, u32[]{:S(2)}) collective-permute-start(bf16[4,3,128,256]{3,2,1,0:T(8,128)(2,1)S(1)} %get-tuple-element.16.refs_0_), channel_id=1, source_target_pairs={{0,448},{64,0},{128,64},{192,128},{256,192},{320,256},{384,320},{4... | collective-permute-start | bytes 2359304 | tf_op jit(solution)/shard_map/ppermute | solution.py:46
  54.1 1.9 %collective-permute-start.7 = (bf16[4,3,128,256]{3,2,1,0:T(8,128)(2,1)S(1)}, bf16[4,3,128,256]{3,2,1,0:T(8,128)(2,1)S(1)}, u32[]{:S(2)}, u32[]{:S(2)}) collective-permute-start(bf16[4,3,128,256]{3,2,1,0:T(8,128)(2,1)S(1)} %get-tuple-element.15.refs_8_.refs_7_), channel_id=1, source_target_pairs={{0,64},{64,128},{128,192},{192,256},{256,320},{320,384},{384,448},... | collective-permute-start | bytes 2359304 | tf_op jit(solution)/shard_map/ppermute | solution.py:46
  56.0 2.2 %collective-permute-done.refs_1_ = bf16[4,3,128,256]{3,2,1,0:T(8,128)(2,1)S(1)} collective-permute-done((bf16[4,3,128,256]{3,2,1,0:T(8,128)(2,1)S(1)}, bf16[4,3,128,256]{3,2,1,0:T(8,128)(2,1)S(1)}, u32[]{:S(2)}, u32[]{:S(2)}) %collective-permute-start) | collective-permute-done | bytes 786464 | tf_op jit(solution)/shard_map/ppermute | solution.py:46
  58.2 2.0 %collective-permute-start.2 = (bf16[4,3,128,256]{3,2,1,0:T(8,128)(2,1)S(1)}, bf16[4,3,128,256]{3,2,1,0:T(8,128)(2,1)S(1)}, u32[]{:S(2)}, u32[]{:S(2)}) collective-permute-start(bf16[4,3,128,256]{3,2,1,0:T(8,128)(2,1)S(1)} %collective-permute-done.refs_1_), channel_id=1, source_target_pairs={{0,64},{64,128},{128,192},{192,256},{256,320},{320,384},{384,448},... | collective-permute-start | bytes 2359304 | tf_op jit(solution)/shard_map/ppermute | solution.py:46
  60.2 5.0 %collective-permute-start.10 = (bf16[4,3,128,256]{3,2,1,0:T(8,128)(2,1)S(1)}, bf16[4,3,128,256]{3,2,1,0:T(8,128)(2,1)S(1)}, u32[]{:S(2)}, u32[]{:S(2)}) collective-permute-start(bf16[4,3,128,256]{3,2,1,0:T(8,128)(2,1)S(1)} %collective-permute-done.8.refs_10_.refs_9_), channel_id=1, source_target_pairs={{0,448},{64,0},{128,64},{192,128},{256,192},{320,256},{384,320},{4... | collective-permute-start | bytes 2359304 | tf_op jit(solution)/shard_map/ppermute | solution.py:46
  65.2 3.4 %collective-permute-done.1.refs_2_ = bf16[4,3,128,256]{3,2,1,0:T(8,128)(2,1)S(1)} collective-permute-done((bf16[4,3,128,256]{3,2,1,0:T(8,128)(2,1)S(1)}, bf16[4,3,128,256]{3,2,1,0:T(8,128)(2,1)S(1)}, u32[]{:S(2)}, u32[]{:S(2)}) %collective-permute-start.1) | collective-permute-done | bytes 786464 | tf_op jit(solution)/shard_map/ppermute | solution.py:46
  68.6 5.0 %collective-permute-start.3 = (bf16[4,3,128,256]{3,2,1,0:T(8,128)(2,1)S(1)}, bf16[4,3,128,256]{3,2,1,0:T(8,128)(2,1)}, u32[]{:S(2)}, u32[]{:S(2)}) collective-permute-start(bf16[4,3,128,256]{3,2,1,0:T(8,128)(2,1)S(1)} %collective-permute-done.1.refs_2_), channel_id=1, source_target_pairs={{0,448},{64,0},{128,64},{192,128},{256,192},{320,256},{384,320},{4... | collective-permute-start | bytes 2359304 | tf_op jit(solution)/shard_map/ppermute | solution.py:46
  73.7 1.9 %collective-permute-start.9 = (bf16[4,3,128,256]{3,2,1,0:T(8,128)(2,1)S(1)}, bf16[4,3,128,256]{3,2,1,0:T(8,128)(2,1)}, u32[]{:S(2)}, u32[]{:S(2)}) collective-permute-start(bf16[4,3,128,256]{3,2,1,0:T(8,128)(2,1)S(1)} %collective-permute-done.7.refs_9_.refs_8_), channel_id=1, source_target_pairs={{0,64},{64,128},{128,192},{192,256},{256,320},{320,384},{384,448},... | collective-permute-start | bytes 2359304 | tf_op jit(solution)/shard_map/ppermute | solution.py:46
  75.6 2.0 %collective-permute-done.2.refs_3_ = bf16[4,3,128,256]{3,2,1,0:T(8,128)(2,1)S(1)} collective-permute-done((bf16[4,3,128,256]{3,2,1,0:T(8,128)(2,1)S(1)}, bf16[4,3,128,256]{3,2,1,0:T(8,128)(2,1)S(1)}, u32[]{:S(2)}, u32[]{:S(2)}) %collective-permute-start.2) | collective-permute-done | bytes 786464 | tf_op jit(solution)/shard_map/ppermute | solution.py:46
  79.5 5.1 %collective-permute-start.12 = (bf16[4,3,128,256]{3,2,1,0:T(8,128)(2,1)S(1)}, bf16[4,3,128,256]{3,2,1,0:T(8,128)(2,1)}, u32[]{:S(2)}, u32[]{:S(2)}) collective-permute-start(bf16[4,3,128,256]{3,2,1,0:T(8,128)(2,1)S(1)} %collective-permute-done.10.refs_12_.refs_11_), channel_id=1, source_target_pairs={{0,448},{64,0},{128,64},{192,128},{256,192},{320,256},{384,320},{4... | collective-permute-start | bytes 2359304 | tf_op jit(solution)/shard_map/ppermute | solution.py:46
  85.6 5.0 %collective-permute-start.5 = (bf16[4,3,128,256]{3,2,1,0:T(8,128)(2,1)}, bf16[4,3,128,256]{3,2,1,0:T(8,128)(2,1)}, u32[]{:S(2)}, u32[]{:S(2)}) collective-permute-start(bf16[4,3,128,256]{3,2,1,0:T(8,128)(2,1)} %collective-permute-done.3.refs_4_), channel_id=1, source_target_pairs={{0,448},{64,0},{128,64},{192,128},{256,192},{320,256},{384,320},{4... | collective-permute-start | bytes 2359304 | tf_op jit(solution)/shard_map/ppermute | solution.py:46
  90.6 1.9 %collective-permute-start.11 = (bf16[4,3,128,256]{3,2,1,0:T(8,128)(2,1)}, bf16[4,3,128,256]{3,2,1,0:T(8,128)(2,1)}, u32[]{:S(2)}, u32[]{:S(2)}) collective-permute-start(bf16[4,3,128,256]{3,2,1,0:T(8,128)(2,1)} %collective-permute-done.9.refs_11_.refs_10_), channel_id=1, source_target_pairs={{0,64},{64,128},{128,192},{192,256},{256,320},{320,384},{384,448},... | collective-permute-start | bytes 2359304 | tf_op jit(solution)/shard_map/ppermute | solution.py:46
  92.6 4.7 %collective-permute-done.4.refs_5_ = bf16[4,3,128,256]{3,2,1,0:T(8,128)(2,1)} collective-permute-done((bf16[4,3,128,256]{3,2,1,0:T(8,128)(2,1)S(1)}, bf16[4,3,128,256]{3,2,1,0:T(8,128)(2,1)}, u32[]{:S(2)}, u32[]{:S(2)}) %collective-permute-start.4) | collective-permute-done | bytes 786464 | tf_op jit(solution)/shard_map/ppermute | solution.py:46
  97.3 1.9 %collective-permute-start.6 = (bf16[4,3,128,256]{3,2,1,0:T(8,128)(2,1)}, bf16[4,3,128,256]{3,2,1,0:T(8,128)(2,1)}, u32[]{:S(2)}, u32[]{:S(2)}) collective-permute-start(bf16[4,3,128,256]{3,2,1,0:T(8,128)(2,1)} %collective-permute-done.4.refs_5_), channel_id=1, source_target_pairs={{0,64},{64,128},{128,192},{192,256},{256,320},{320,384},{384,448},... | collective-permute-start | bytes 2359304 | tf_op jit(solution)/shard_map/ppermute | solution.py:46
  99.2 5.1 %collective-permute-start.13 = (bf16[4,3,128,256]{3,2,1,0:T(8,128)(2,1)}, bf16[4,3,128,256]{3,2,1,0:T(8,128)(2,1)}, u32[]{:S(2)}, u32[]{:S(2)}) collective-permute-start(bf16[4,3,128,256]{3,2,1,0:T(8,128)(2,1)} %collective-permute-done.12.refs_14_.refs_13_), channel_id=1, source_target_pairs={{0,448},{64,0},{128,64},{192,128},{256,192},{320,256},{384,320},{4... | collective-permute-start | bytes 2359304 | tf_op jit(solution)/shard_map/ppermute | solution.py:46
  104.5 2.9 %collect.1.features_ref = bf16[8,8,256,128]{3,2,1,0:T(8,128)(2,1)S(1)} custom-call(s32[4]{0:T(128)S(1)} %pad_add_fusion.meta_ref, bf16[8,256,1024]{2,1,0:T(8,128)(2,1)} %all-to-all-done.pieces_ref), custom_call_target="tpu_custom_call" | custom-call | tf_op jit(solution)/shard_map/collect/pallas_call | solution.py:241
  107.4 5.3 %begin.1.refs_2_ = f32[2,256,256]{2,1,0:T(8,128)S(1)} custom-call(s32[4]{0:T(128)S(1)} %pad_add_fusion.meta_ref, bf16[8,8,256,128]{3,2,1,0:T(8,128)(2,1)S(1)} %collect.1.features_ref, bf16[4,3,128,256]{3,2,1,0:T(8,128)(2,1)} %copy-done.3, bf16[4,3,128,256]{3,2,1,0:T(8,128)(2,1)} %copy-done.4, bf16[4,3,128,256]{3,2,1,0:T(8,128)(2,1)} %copy-done.6, ...), custom_call_target="tpu_custom_call" | custom-call | tf_op jit(solution)/shard_map/begin/pallas_call | solution.py:260
  114.5 2.7 %drive.1 = (f32[2,384,128]{2,1,0:T(8,128)S(1)}, f32[16,256]{1,0:T(8,128)S(1)}) custom-call(s32[4]{0:T(128)S(1)} %pad_add_fusion.meta_ref, bf16[8,8,256,128]{3,2,1,0:T(8,128)(2,1)S(1)} %collect.1.features_ref, bf16[4,3,128,256]{3,2,1,0:T(8,128)(2,1)} %collective-permute-done.6.refs_7_.refs_0_, ...), custom_call_target="tpu_custom_call" | custom-call | tf_op jit(solution)/shard_map/drive/pallas_call | solution.py:270
  117.8 4.7 %all-to-all-start.2 = ((f32[8,16,256]{2,1,0:T(8,128)}), f32[8,16,256]{2,1,0:T(8,128)S(1)}, u32[]{:S(2)}, u32[]{:S(2)}) async-start(f32[8,16,256]{2,1,0:T(8,128)} %broadcast_in_dim.39), calls=%async_computation.2 | async-start | bytes 262144 | tf_op jit(solution)/shard_map/all_to_all | solution.py:41
  122.6 9.1 %all-to-all-done.2 = f32[8,16,256]{2,1,0:T(8,128)S(1)} async-done(((f32[8,16,256]{2,1,0:T(8,128)}), f32[8,16,256]{2,1,0:T(8,128)S(1)}, u32[]{:S(2)}, u32[]{:S(2)}) %all-to-all-start.2) | async-done | bytes 131104 | tf_op jit(solution)/shard_map/all_to_all | solution.py:41
  132.4 6.1 %all-to-all-start.3 = ((f32[8,16,256]{2,1,0:T(8,128)}), f32[8,16,256]{2,1,0:T(8,128)S(1)}, u32[]{:S(2)}, u32[]{:S(2)}) async-start(f32[8,16,256]{2,1,0:T(8,128)} %broadcast_in_dim.40), calls=%async_computation.3 | async-start | bytes 262144 | tf_op jit(solution)/shard_map/all_to_all | solution.py:41
  138.6 2.2 %copy-done.1 = bf16[8,8,256,128]{3,2,1,0:T(8,128)(2,1)S(1)} copy-done((bf16[8,8,256,128]{3,2,1,0:T(8,128)(2,1)S(1)}, bf16[8,8,256,128]{3,2,1,0:T(8,128)(2,1)}, u32[]{:S(2)}) %copy-start.1) | copy-done | bytes 4194328
  140.8 4.6 %query.1.query_ref = bf16[256,256]{1,0:T(8,128)(2,1)S(1)} custom-call(s32[4]{0:T(128)S(1)} %pad_add_fusion.meta_ref, bf16[8,8,256,128]{3,2,1,0:T(8,128)(2,1)S(1)} %copy-done.1, bf16[4,3,128,256]{3,2,1,0:T(8,128)(2,1)} %copy-done.3, bf16[4,3,128,256]{3,2,1,0:T(8,128)(2,1)} %copy-done.4, bf16[4,3,128,256]{3,2,1,0:T(8,128)(2,1)} %copy-done.6, ...), custom_call_target="tpu_custom_call" | custom-call | tf_op jit(solution)/shard_map/query/pallas_call | solution.py:292
  145.3 2.3 %all-to-all-done.3.far_ref = f32[8,16,256]{2,1,0:T(8,128)S(1)} async-done(((f32[8,16,256]{2,1,0:T(8,128)}), f32[8,16,256]{2,1,0:T(8,128)S(1)}, u32[]{:S(2)}, u32[]{:S(2)}) %all-to-all-start.3) | async-done | bytes 131104 | tf_op jit(solution)/shard_map/all_to_all | solution.py:41
  147.6 2.3 %finish.1 = (bf16[256,256]{1,0:T(8,128)(2,1)}, f32[4,16]{1,0:T(4,128)}, f32[1,4]{1,0:T(1,128)}) custom-call(s32[4]{0:T(128)S(1)} %pad_add_fusion.meta_ref, bf16[256,256]{1,0:T(8,128)(2,1)S(1)} %query.1.query_ref, f32[2,384,128]{2,1,0:T(8,128)S(1)} %get-tuple-element.8.local_ref, f32[16,256]{1,0:T(8,128)S(1)} %get-tuple-element.14.rows_in_ref, ...), custom_call_target="tpu_custom_call" | custom-call | tf_op jit(solution)/shard_map/finish/pallas_call | solution.py:301
  (46 shorter events, 6.3 us)
Async XLA Ops:
  2.9 34.8 %all-to-all-start.1 = ((bf16[8,3,128,256]{3,2,1,0:T(8,128)(2,1)}), bf16[8,3,128,256]{3,2,1,0:T(8,128)(2,1)S(1)}, u32[]{:S(2)}, u32[]{:S(2)}) async-start(bf16[8,3,128,256]{3,2,1,0:T(8,128)(2,1)} %broadcast_in_dim.20), calls=%async_computation.1 | async-start | bytes 3145728 | tf_op jit(solution)/shard_map/all_to_all | solution.py:211
  16.3 88.2 %copy-start.10 = (f32[256,16]{0,1:T(8,128)S(1)}, f32[256,16]{0,1:T(8,128)}, u32[]{:S(2)}) copy-start(f32[256,16]{0,1:T(8,128)} %param.7) | copy-start | bytes 49156
  16.3 88.2 %copy-start.11 = (f32[256,16]{0,1:T(8,128)S(1)}, f32[256,16]{0,1:T(8,128)}, u32[]{:S(2)}) copy-start(f32[256,16]{0,1:T(8,128)} %param.8) | copy-start | bytes 49156
  16.3 88.2 %copy-start.12 = (f32[256]{0:T(256)S(1)}, f32[256]{0:T(256)}, u32[]{:S(2)}) copy-start(f32[256]{0:T(256)} %param.9) | copy-start | bytes 3076
  37.7 66.8 %all-to-all-start = ((bf16[8,256,1024]{2,1,0:T(8,128)(2,1)}), bf16[8,256,1024]{2,1,0:T(8,128)(2,1)}, u32[]{:S(2)}, u32[]{:S(2)}) async-start(bf16[8,256,1024]{2,1,0:T(8,128)(2,1)} %copies.1), calls=%async_computation | async-start | bytes 8388608 | tf_op jit(solution)/shard_map/all_to_all | solution.py:236
  42.8 64.6 %copy-start.2 = (bf16[4,3,128,256]{3,2,1,0:T(8,128)(2,1)}, bf16[4,3,128,256]{3,2,1,0:T(8,128)(2,1)S(1)}, u32[]{:S(2)}) copy-start(bf16[4,3,128,256]{3,2,1,0:T(8,128)(2,1)S(1)} %get-tuple-element.15.refs_8_.refs_7_) | copy-start | bytes 2359300
  42.8 64.6 %copy-start.3 = (bf16[4,3,128,256]{3,2,1,0:T(8,128)(2,1)}, bf16[4,3,128,256]{3,2,1,0:T(8,128)(2,1)S(1)}, u32[]{:S(2)}) copy-start(bf16[4,3,128,256]{3,2,1,0:T(8,128)(2,1)S(1)} %get-tuple-element.16.refs_0_) | copy-start | bytes 2359300
  42.8 15.3 %collective-permute-start = (bf16[4,3,128,256]{3,2,1,0:T(8,128)(2,1)S(1)}, bf16[4,3,128,256]{3,2,1,0:T(8,128)(2,1)S(1)}, u32[]{:S(2)}, u32[]{:S(2)}) collective-permute-start(bf16[4,3,128,256]{3,2,1,0:T(8,128)(2,1)S(1)} %get-tuple-element.16.refs_0_), channel_id=1, source_target_pairs={{0,64},{64,128},{128,192},{192,256},{256,320},{320,384},{384,448},... | collective-permute-start | bytes 2359304 | tf_op jit(solution)/shard_map/ppermute | solution.py:46
  46.3 13.9 %collective-permute-start.8 = (bf16[4,3,128,256]{3,2,1,0:T(8,128)(2,1)S(1)}, bf16[4,3,128,256]{3,2,1,0:T(8,128)(2,1)S(1)}, u32[]{:S(2)}, u32[]{:S(2)}) collective-permute-start(bf16[4,3,128,256]{3,2,1,0:T(8,128)(2,1)S(1)} %get-tuple-element.15.refs_8_.refs_7_), channel_id=1, source_target_pairs={{0,448},{64,0},{128,64},{192,128},{256,192},{320,256},{384,320},{4... | collective-permute-start | bytes 2359304 | tf_op jit(solution)/shard_map/ppermute | solution.py:46
  50.1 18.5 %collective-permute-start.1 = (bf16[4,3,128,256]{3,2,1,0:T(8,128)(2,1)S(1)}, bf16[4,3,128,256]{3,2,1,0:T(8,128)(2,1)S(1)}, u32[]{:S(2)}, u32[]{:S(2)}) collective-permute-start(bf16[4,3,128,256]{3,2,1,0:T(8,128)(2,1)S(1)} %get-tuple-element.16.refs_0_), channel_id=1, source_target_pairs={{0,448},{64,0},{128,64},{192,128},{256,192},{320,256},{384,320},{4... | collective-permute-start | bytes 2359304 | tf_op jit(solution)/shard_map/ppermute | solution.py:46
  54.1 19.6 %collective-permute-start.7 = (bf16[4,3,128,256]{3,2,1,0:T(8,128)(2,1)S(1)}, bf16[4,3,128,256]{3,2,1,0:T(8,128)(2,1)S(1)}, u32[]{:S(2)}, u32[]{:S(2)}) collective-permute-start(bf16[4,3,128,256]{3,2,1,0:T(8,128)(2,1)S(1)} %get-tuple-element.15.refs_8_.refs_7_), channel_id=1, source_target_pairs={{0,64},{64,128},{128,192},{192,256},{256,320},{320,384},{384,448},... | collective-permute-start | bytes 2359304 | tf_op jit(solution)/shard_map/ppermute | solution.py:46
  58.2 49.2 %copy-start.4 = (bf16[4,3,128,256]{3,2,1,0:T(8,128)(2,1)}, bf16[4,3,128,256]{3,2,1,0:T(8,128)(2,1)S(1)}, u32[]{:S(2)}) copy-start(bf16[4,3,128,256]{3,2,1,0:T(8,128)(2,1)S(1)} %collective-permute-done.refs_1_) | copy-start | bytes 2359300
  58.2 19.4 %collective-permute-start.2 = (bf16[4,3,128,256]{3,2,1,0:T(8,128)(2,1)S(1)}, bf16[4,3,128,256]{3,2,1,0:T(8,128)(2,1)S(1)}, u32[]{:S(2)}, u32[]{:S(2)}) collective-permute-start(bf16[4,3,128,256]{3,2,1,0:T(8,128)(2,1)S(1)} %collective-permute-done.refs_1_), channel_id=1, source_target_pairs={{0,64},{64,128},{128,192},{192,256},{256,320},{320,384},{384,448},... | collective-permute-start | bytes 2359304 | tf_op jit(solution)/shard_map/ppermute | solution.py:46
  60.2 47.2 %copy-start.5 = (bf16[4,3,128,256]{3,2,1,0:T(8,128)(2,1)}, bf16[4,3,128,256]{3,2,1,0:T(8,128)(2,1)S(1)}, u32[]{:S(2)}) copy-start(bf16[4,3,128,256]{3,2,1,0:T(8,128)(2,1)S(1)} %collective-permute-done.8.refs_10_.refs_9_) | copy-start | bytes 2359300
  60.2 19.3 %collective-permute-start.10 = (bf16[4,3,128,256]{3,2,1,0:T(8,128)(2,1)S(1)}, bf16[4,3,128,256]{3,2,1,0:T(8,128)(2,1)S(1)}, u32[]{:S(2)}, u32[]{:S(2)}) collective-permute-start(bf16[4,3,128,256]{3,2,1,0:T(8,128)(2,1)S(1)} %collective-permute-done.8.refs_10_.refs_9_), channel_id=1, source_target_pairs={{0,448},{64,0},{128,64},{192,128},{256,192},{320,256},{384,320},{4... | collective-permute-start | bytes 2359304 | tf_op jit(solution)/shard_map/ppermute | solution.py:46
  68.6 10.9 %copy-start.6 = (bf16[4,3,128,256]{3,2,1,0:T(8,128)(2,1)}, bf16[4,3,128,256]{3,2,1,0:T(8,128)(2,1)S(1)}, u32[]{:S(2)}) copy-start(bf16[4,3,128,256]{3,2,1,0:T(8,128)(2,1)S(1)} %collective-permute-done.1.refs_2_) | copy-start | bytes 2359300
  68.6 17.0 %collective-permute-start.3 = (bf16[4,3,128,256]{3,2,1,0:T(8,128)(2,1)S(1)}, bf16[4,3,128,256]{3,2,1,0:T(8,128)(2,1)}, u32[]{:S(2)}, u32[]{:S(2)}) collective-permute-start(bf16[4,3,128,256]{3,2,1,0:T(8,128)(2,1)S(1)} %collective-permute-done.1.refs_2_), channel_id=1, source_target_pairs={{0,448},{64,0},{128,64},{192,128},{256,192},{320,256},{384,320},{4... | collective-permute-start | bytes 2359304 | tf_op jit(solution)/shard_map/ppermute | solution.py:46
  73.7 11.9 %copy-start.7 = (bf16[4,3,128,256]{3,2,1,0:T(8,128)(2,1)}, bf16[4,3,128,256]{3,2,1,0:T(8,128)(2,1)S(1)}, u32[]{:S(2)}) copy-start(bf16[4,3,128,256]{3,2,1,0:T(8,128)(2,1)S(1)} %collective-permute-done.7.refs_9_.refs_8_) | copy-start | bytes 2359300
  73.7 16.9 %collective-permute-start.9 = (bf16[4,3,128,256]{3,2,1,0:T(8,128)(2,1)S(1)}, bf16[4,3,128,256]{3,2,1,0:T(8,128)(2,1)}, u32[]{:S(2)}, u32[]{:S(2)}) collective-permute-start(bf16[4,3,128,256]{3,2,1,0:T(8,128)(2,1)S(1)} %collective-permute-done.7.refs_9_.refs_8_), channel_id=1, source_target_pairs={{0,64},{64,128},{128,192},{192,256},{256,320},{320,384},{384,448},... | collective-permute-start | bytes 2359304 | tf_op jit(solution)/shard_map/ppermute | solution.py:46
  77.6 13.0 %copy-start.8 = (bf16[4,3,128,256]{3,2,1,0:T(8,128)(2,1)}, bf16[4,3,128,256]{3,2,1,0:T(8,128)(2,1)S(1)}, u32[]{:S(2)}) copy-start(bf16[4,3,128,256]{3,2,1,0:T(8,128)(2,1)S(1)} %collective-permute-done.2.refs_3_) | copy-start | bytes 2359300
  77.6 19.7 %collective-permute-start.4 = (bf16[4,3,128,256]{3,2,1,0:T(8,128)(2,1)S(1)}, bf16[4,3,128,256]{3,2,1,0:T(8,128)(2,1)}, u32[]{:S(2)}, u32[]{:S(2)}) collective-permute-start(bf16[4,3,128,256]{3,2,1,0:T(8,128)(2,1)S(1)} %collective-permute-done.2.refs_3_), channel_id=1, source_target_pairs={{0,64},{64,128},{128,192},{192,256},{256,320},{320,384},{384,448},... | collective-permute-start | bytes 2359304 | tf_op jit(solution)/shard_map/ppermute | solution.py:46
  79.5 17.8 %copy-start.9 = (bf16[4,3,128,256]{3,2,1,0:T(8,128)(2,1)}, bf16[4,3,128,256]{3,2,1,0:T(8,128)(2,1)S(1)}, u32[]{:S(2)}) copy-start(bf16[4,3,128,256]{3,2,1,0:T(8,128)(2,1)S(1)} %collective-permute-done.10.refs_12_.refs_11_) | copy-start | bytes 2359300
  79.5 19.7 %collective-permute-start.12 = (bf16[4,3,128,256]{3,2,1,0:T(8,128)(2,1)S(1)}, bf16[4,3,128,256]{3,2,1,0:T(8,128)(2,1)}, u32[]{:S(2)}, u32[]{:S(2)}) collective-permute-start(bf16[4,3,128,256]{3,2,1,0:T(8,128)(2,1)S(1)} %collective-permute-done.10.refs_12_.refs_11_), channel_id=1, source_target_pairs={{0,448},{64,0},{128,64},{192,128},{256,192},{320,256},{384,320},{4... | collective-permute-start | bytes 2359304 | tf_op jit(solution)/shard_map/ppermute | solution.py:46
  85.6 21.8 %collective-permute-start.5 = (bf16[4,3,128,256]{3,2,1,0:T(8,128)(2,1)}, bf16[4,3,128,256]{3,2,1,0:T(8,128)(2,1)}, u32[]{:S(2)}, u32[]{:S(2)}) collective-permute-start(bf16[4,3,128,256]{3,2,1,0:T(8,128)(2,1)} %collective-permute-done.3.refs_4_), channel_id=1, source_target_pairs={{0,448},{64,0},{128,64},{192,128},{256,192},{320,256},{384,320},{4... | collective-permute-start | bytes 2359304 | tf_op jit(solution)/shard_map/ppermute | solution.py:46
  90.6 16.8 %collective-permute-start.11 = (bf16[4,3,128,256]{3,2,1,0:T(8,128)(2,1)}, bf16[4,3,128,256]{3,2,1,0:T(8,128)(2,1)}, u32[]{:S(2)}, u32[]{:S(2)}) collective-permute-start(bf16[4,3,128,256]{3,2,1,0:T(8,128)(2,1)} %collective-permute-done.9.refs_11_.refs_10_), channel_id=1, source_target_pairs={{0,64},{64,128},{128,192},{192,256},{256,320},{320,384},{384,448},... | collective-permute-start | bytes 2359304 | tf_op jit(solution)/shard_map/ppermute | solution.py:46
  97.3 17.2 %collective-permute-start.6 = (bf16[4,3,128,256]{3,2,1,0:T(8,128)(2,1)}, bf16[4,3,128,256]{3,2,1,0:T(8,128)(2,1)}, u32[]{:S(2)}, u32[]{:S(2)}) collective-permute-start(bf16[4,3,128,256]{3,2,1,0:T(8,128)(2,1)} %collective-permute-done.4.refs_5_), channel_id=1, source_target_pairs={{0,64},{64,128},{128,192},{192,256},{256,320},{320,384},{384,448},... | collective-permute-start | bytes 2359304 | tf_op jit(solution)/shard_map/ppermute | solution.py:46
  99.2 15.2 %collective-permute-start.13 = (bf16[4,3,128,256]{3,2,1,0:T(8,128)(2,1)}, bf16[4,3,128,256]{3,2,1,0:T(8,128)(2,1)}, u32[]{:S(2)}, u32[]{:S(2)}) collective-permute-start(bf16[4,3,128,256]{3,2,1,0:T(8,128)(2,1)} %collective-permute-done.12.refs_14_.refs_13_), channel_id=1, source_target_pairs={{0,448},{64,0},{128,64},{192,128},{256,192},{320,256},{384,320},{4... | collective-permute-start | bytes 2359304 | tf_op jit(solution)/shard_map/ppermute | solution.py:46
  107.4 7.1 %copy-start = (bf16[8,8,256,128]{3,2,1,0:T(8,128)(2,1)}, bf16[8,8,256,128]{3,2,1,0:T(8,128)(2,1)S(1)}, u32[]{:S(2)}) copy-start(bf16[8,8,256,128]{3,2,1,0:T(8,128)(2,1)S(1)} %collect.1.features_ref) | copy-start | bytes 12582916
  117.8 13.8 %all-to-all-start.2 = ((f32[8,16,256]{2,1,0:T(8,128)}), f32[8,16,256]{2,1,0:T(8,128)S(1)}, u32[]{:S(2)}, u32[]{:S(2)}) async-start(f32[8,16,256]{2,1,0:T(8,128)} %broadcast_in_dim.39), calls=%async_computation.2 | async-start | bytes 262144 | tf_op jit(solution)/shard_map/all_to_all | solution.py:41
  132.4 15.2 %all-to-all-start.3 = ((f32[8,16,256]{2,1,0:T(8,128)}), f32[8,16,256]{2,1,0:T(8,128)S(1)}, u32[]{:S(2)}, u32[]{:S(2)}) async-start(f32[8,16,256]{2,1,0:T(8,128)} %broadcast_in_dim.40), calls=%async_computation.3 | async-start | bytes 262144 | tf_op jit(solution)/shard_map/all_to_all | solution.py:41
  138.6 2.2 %copy-start.1 = (bf16[8,8,256,128]{3,2,1,0:T(8,128)(2,1)S(1)}, bf16[8,8,256,128]{3,2,1,0:T(8,128)(2,1)}, u32[]{:S(2)}) copy-start(bf16[8,8,256,128]{3,2,1,0:T(8,128)(2,1)} %copy-done) | copy-start | bytes 12582916

commit v6 on v3

--- a/solution.py
+++ b/solution.py
@@ -44,6 +44,17 @@
 def turned(array, step):
     pairs = [(g[i], g[(i + step) % LINE]) for g in lines(False) for i in range(LINE)]
     return lax.ppermute(array, AXES, pairs)
+
+
+def copies_kernel(array_ref, copies_ref, held, load_sem, sems):
+    load = pltpu.make_async_copy(array_ref, held, load_sem)
+    load.start()
+    load.wait()
+    stores = [pltpu.make_async_copy(held, copies_ref.at[i], sems.at[i]) for i in range(copies_ref.shape[0])]
+    for store in stores:
+        store.start()
+    for store in stores:
+        store.wait()
 
 
 def collect_kernel(meta_ref, pieces_ref, features_ref, tokens, sems):
@@ -196,7 +207,23 @@
     bf16 = functools.partial(jax.ShapeDtypeStruct, dtype=jnp.bfloat16)
 
     weights = in_weight.transpose(1, 0, 2)
-    copies = jnp.broadcast_to(weights[None], (LINE,) + weights.shape)
+    hbm = pl.BlockSpec(memory_space=pltpu.HBM)
+
+    def eightfold(array):
+        return pl.pallas_call(
+            copies_kernel,
+            in_specs=[hbm],
+            out_specs=hbm,
+            out_shape=bf16((LINE,) + array.shape),
+            scratch_shapes=[
+                pltpu.VMEM(array.shape, jnp.bfloat16),
+                pltpu.SemaphoreType.DMA(()),
+                pltpu.SemaphoreType.DMA((LINE,)),
+            ],
+            name="copies",
+        )(array)
+
+    copies = eightfold(weights)
     near = lax.all_to_all(copies, AXES, 0, 0, tiled=True, axis_index_groups=lines(True))
 
     half = LINE // 2
@@ -209,7 +236,7 @@
                 line[sign * step] = turned(line[sign * (step - 1)], sign)
     lefts[4], rights[4] = turned(lefts[3], 1), turned(rights[-3], -1)
 
-    pieces = to_all(tokens, ("x", "k"))
+    pieces = lax.all_to_all(eightfold(tokens), ("x", "k"), 0, 0, tiled=True)
     meta = jnp.stack([k, jnp.where(k == 0, y, z), y, z]).astype(jnp.int32)
     filters = jnp.concatenate([rate.T, residue.T, skip_gain[None]])
     params = pltpu.CompilerParams(vmem_limit_bytes=20 * 2**20)

time: 152 us -> 151 us (level)
  blocking collectives: 34.6 us -> 0 us
  waiting for transfers between devices: 26.3 us -> 47.7 us
  starting transfers between devices: 64.1 us -> 74.3 us
  Pallas kernels: 17.7 us -> 23 us
  local copies, waits for them, and re-layouts: 7.38 us -> 3.67 us
    all_to_all x1 -> x0, blocking collectives: 34.6 us -> none  [shards(): lax.all_to_all(copies, AXES, 0, 0, tiled=True, axis_index_groups=lines(Tr...]
    all_to_all x0 -> x2, waiting for transfers between devices: none -> 21.4 us  [the longest x1 21.4 us: shards(): lax.all_to_all(copies, AXES, 0, 0, tiled=True, axis_index_groups=lines(Tr...]
    all_to_all x0 -> x2, starting transfers between devices: none -> 15.3 us  [the longest x1 10.3 us: shards(): lax.all_to_all(copies, AXES, 0, 0, tiled=True, axis_index_groups=lines(Tr...]
    pallas_call x0 -> x2, Pallas kernels: none -> 5.24 us  [eightfold(): pl.pallas_call(copies_kernel, in_specs=[hbm], out_specs=hbm, out_shape=bf...]
    all_to_all x3 -> x2, starting transfers between devices: 15.9 us -> 10.9 us  [to_all(): return lax.all_to_all(copies, axis, 0, 0, tiled=True)]
    broadcast_in_dim x3 -> x2, local copies, waits for them, and re-layouts: 3.89 us -> 1.33 us  [to_all(): copies = jnp.broadcast_to(array[None], (lax.psum(1, axis),) + array.shape)]
    all_to_all x3 -> x2, waiting for transfers between devices: 11.4 us -> 11.4 us  [to_all(): return lax.all_to_all(copies, axis, 0, 0, tiled=True)]
  transfers between devices with their start and end apart: 17 -> 18, of which waited for: 8 -> 9; matrix products, arithmetic and copies ran while one was open for 0% -> 0% of each run, Pallas kernels for 8% -> 11%
where the time goes in v6:
time: 151 us; the launch traced here: 150 us
  starting transfers between devices  74.3 us (49%)
  waiting for transfers between devices  47.7 us (32%)
  Pallas kernels  23 us (15%)
  local copies, waits for them, and re-layouts  3.67 us (2%)
    ppermute x14, starting transfers between devices, turned(): return lax.ppermute(array, AXES, pairs)  48.1 us
    all_to_all x1, waiting for transfers between devices, shards(): lax.all_to_all(copies, AXES, 0, 0, tiled=True, axis_index_groups=lines(Tr...  21.4 us
    ppermute x14, waiting for transfers between devices, turned(): return lax.ppermute(array, AXES, pairs)  14.9 us
    all_to_all x2, waiting for transfers between devices, to_all(): return lax.all_to_all(copies, axis, 0, 0, tiled=True)  11.4 us
    all_to_all x2, starting transfers between devices, to_all(): return lax.all_to_all(copies, axis, 0, 0, tiled=True)  10.9 us
    all_to_all x1, starting transfers between devices, shards(): lax.all_to_all(copies, AXES, 0, 0, tiled=True, axis_index_groups=lines(Tr...  10.3 us
    pallas_call x1, Pallas kernels, shards(): pl.pallas_call(begin_kernel, in_specs=[smem(), vmem()] + [hbm] * (2 * len...  5.31 us
    pallas_call x2, Pallas kernels, eightfold(): pl.pallas_call(copies_kernel, in_specs=[hbm], out_specs=hbm, out_shape=bf...  5.24 us
  transfers between devices with their start and end apart: 18, of which 9 were waited for; matrix products, arithmetic and copies ran while one was open for 0% of the time, Pallas kernels for 11%

profile of v6, /device:TPU:6, one launch (start us, length us, event | category | flops | bytes accessed | tf_op | source)
XLA Modules:
  0.0 149.9 jit_solution(1635281971843495566)
XLA Ops:
  0.6 2.2 %copies.3 = bf16[8,3,128,256]{3,2,1,0:T(8,128)(2,1)} custom-call(bf16[3,128,256]{2,1,0:T(8,128)(2,1)} %bitcast.10), custom_call_target="tpu_custom_call" | custom-call | tf_op jit(solution)/shard_map/copies/pallas_call | solution.py:213
  2.8 10.3 %all-to-all-start.1 = ((bf16[8,3,128,256]{3,2,1,0:T(8,128)(2,1)}), bf16[8,3,128,256]{3,2,1,0:T(8,128)(2,1)S(1)}, u32[]{:S(2)}, u32[]{:S(2)}) async-start(bf16[8,3,128,256]{3,2,1,0:T(8,128)(2,1)} %copies.3), calls=%async_computation.1 | async-start | bytes 3145728 | tf_op jit(solution)/shard_map/all_to_all | solution.py:227
  13.1 3.1 %copies.2 = bf16[8,256,1024]{2,1,0:T(8,128)(2,1)} custom-call(bf16[256,1024]{1,0:T(8,128)(2,1)} %array_ref.1), custom_call_target="tpu_custom_call" | custom-call | tf_op jit(solution)/shard_map/copies/pallas_call | solution.py:213
  16.3 21.4 %all-to-all-done.1 = bf16[8,3,128,256]{3,2,1,0:T(8,128)(2,1)S(1)} async-done(((bf16[8,3,128,256]{3,2,1,0:T(8,128)(2,1)}), bf16[8,3,128,256]{3,2,1,0:T(8,128)(2,1)S(1)}, u32[]{:S(2)}, u32[]{:S(2)}) %all-to-all-start.1) | async-done | bytes 1572896 | tf_op jit(solution)/shard_map/all_to_all | solution.py:227
  37.7 5.0 %all-to-all-start = ((bf16[8,256,1024]{2,1,0:T(8,128)(2,1)}), bf16[8,256,1024]{2,1,0:T(8,128)(2,1)}, u32[]{:S(2)}, u32[]{:S(2)}) async-start(bf16[8,256,1024]{2,1,0:T(8,128)(2,1)} %copies.2), calls=%async_computation | async-start | bytes 8388608 | tf_op jit(solution)/shard_map/all_to_all | solution.py:239
  42.7 3.5 %collective-permute-start = (bf16[4,3,128,256]{3,2,1,0:T(8,128)(2,1)S(1)}, bf16[4,3,128,256]{3,2,1,0:T(8,128)(2,1)S(1)}, u32[]{:S(2)}, u32[]{:S(2)}) collective-permute-start(bf16[4,3,128,256]{3,2,1,0:T(8,128)(2,1)S(1)} %get-tuple-element.16.refs_0_), channel_id=1, source_target_pairs={{0,64},{64,128},{128,192},{192,256},{256,320},{320,384},{384,448},... | collective-permute-start | bytes 2359304 | tf_op jit(solution)/shard_map/ppermute | solution.py:46
  46.2 3.8 %collective-permute-start.8 = (bf16[4,3,128,256]{3,2,1,0:T(8,128)(2,1)S(1)}, bf16[4,3,128,256]{3,2,1,0:T(8,128)(2,1)S(1)}, u32[]{:S(2)}, u32[]{:S(2)}) collective-permute-start(bf16[4,3,128,256]{3,2,1,0:T(8,128)(2,1)S(1)} %get-tuple-element.15.refs_8_.refs_7_), channel_id=1, source_target_pairs={{0,448},{64,0},{128,64},{192,128},{256,192},{320,256},{384,320},{4... | collective-permute-start | bytes 2359304 | tf_op jit(solution)/shard_map/ppermute | solution.py:46
  50.1 3.9 %collective-permute-start.1 = (bf16[4,3,128,256]{3,2,1,0:T(8,128)(2,1)S(1)}, bf16[4,3,128,256]{3,2,1,0:T(8,128)(2,1)S(1)}, u32[]{:S(2)}, u32[]{:S(2)}) collective-permute-start(bf16[4,3,128,256]{3,2,1,0:T(8,128)(2,1)S(1)} %get-tuple-element.16.refs_0_), channel_id=1, source_target_pairs={{0,448},{64,0},{128,64},{192,128},{256,192},{320,256},{384,320},{4... | collective-permute-start | bytes 2359304 | tf_op jit(solution)/shard_map/ppermute | solution.py:46
  54.0 1.9 %collective-permute-start.7 = (bf16[4,3,128,256]{3,2,1,0:T(8,128)(2,1)S(1)}, bf16[4,3,128,256]{3,2,1,0:T(8,128)(2,1)S(1)}, u32[]{:S(2)}, u32[]{:S(2)}) collective-permute-start(bf16[4,3,128,256]{3,2,1,0:T(8,128)(2,1)S(1)} %get-tuple-element.15.refs_8_.refs_7_), channel_id=1, source_target_pairs={{0,64},{64,128},{128,192},{192,256},{256,320},{320,384},{384,448},... | collective-permute-start | bytes 2359304 | tf_op jit(solution)/shard_map/ppermute | solution.py:46
  55.9 2.2 %collective-permute-done.refs_1_ = bf16[4,3,128,256]{3,2,1,0:T(8,128)(2,1)S(1)} collective-permute-done((bf16[4,3,128,256]{3,2,1,0:T(8,128)(2,1)S(1)}, bf16[4,3,128,256]{3,2,1,0:T(8,128)(2,1)S(1)}, u32[]{:S(2)}, u32[]{:S(2)}) %collective-permute-start) | collective-permute-done | bytes 786464 | tf_op jit(solution)/shard_map/ppermute | solution.py:46
  58.1 2.0 %collective-permute-start.2 = (bf16[4,3,128,256]{3,2,1,0:T(8,128)(2,1)S(1)}, bf16[4,3,128,256]{3,2,1,0:T(8,128)(2,1)S(1)}, u32[]{:S(2)}, u32[]{:S(2)}) collective-permute-start(bf16[4,3,128,256]{3,2,1,0:T(8,128)(2,1)S(1)} %collective-permute-done.refs_1_), channel_id=1, source_target_pairs={{0,64},{64,128},{128,192},{192,256},{256,320},{320,384},{384,448},... | collective-permute-start | bytes 2359304 | tf_op jit(solution)/shard_map/ppermute | solution.py:46
  60.1 5.0 %collective-permute-start.10 = (bf16[4,3,128,256]{3,2,1,0:T(8,128)(2,1)S(1)}, bf16[4,3,128,256]{3,2,1,0:T(8,128)(2,1)S(1)}, u32[]{:S(2)}, u32[]{:S(2)}) collective-permute-start(bf16[4,3,128,256]{3,2,1,0:T(8,128)(2,1)S(1)} %collective-permute-done.8.refs_10_.refs_9_), channel_id=1, source_target_pairs={{0,448},{64,0},{128,64},{192,128},{256,192},{320,256},{384,320},{4... | collective-permute-start | bytes 2359304 | tf_op jit(solution)/shard_map/ppermute | solution.py:46
  65.2 3.4 %collective-permute-done.1.refs_2_ = bf16[4,3,128,256]{3,2,1,0:T(8,128)(2,1)S(1)} collective-permute-done((bf16[4,3,128,256]{3,2,1,0:T(8,128)(2,1)S(1)}, bf16[4,3,128,256]{3,2,1,0:T(8,128)(2,1)S(1)}, u32[]{:S(2)}, u32[]{:S(2)}) %collective-permute-start.1) | collective-permute-done | bytes 786464 | tf_op jit(solution)/shard_map/ppermute | solution.py:46
  68.6 5.0 %collective-permute-start.3 = (bf16[4,3,128,256]{3,2,1,0:T(8,128)(2,1)S(1)}, bf16[4,3,128,256]{3,2,1,0:T(8,128)(2,1)}, u32[]{:S(2)}, u32[]{:S(2)}) collective-permute-start(bf16[4,3,128,256]{3,2,1,0:T(8,128)(2,1)S(1)} %collective-permute-done.1.refs_2_), channel_id=1, source_target_pairs={{0,448},{64,0},{128,64},{192,128},{256,192},{320,256},{384,320},{4... | collective-permute-start | bytes 2359304 | tf_op jit(solution)/shard_map/ppermute | solution.py:46
  73.6 1.9 %collective-permute-start.9 = (bf16[4,3,128,256]{3,2,1,0:T(8,128)(2,1)S(1)}, bf16[4,3,128,256]{3,2,1,0:T(8,128)(2,1)}, u32[]{:S(2)}, u32[]{:S(2)}) collective-permute-start(bf16[4,3,128,256]{3,2,1,0:T(8,128)(2,1)S(1)} %collective-permute-done.7.refs_9_.refs_8_), channel_id=1, source_target_pairs={{0,64},{64,128},{128,192},{192,256},{256,320},{320,384},{384,448},... | collective-permute-start | bytes 2359304 | tf_op jit(solution)/shard_map/ppermute | solution.py:46
  75.5 2.0 %collective-permute-done.2.refs_3_ = bf16[4,3,128,256]{3,2,1,0:T(8,128)(2,1)S(1)} collective-permute-done((bf16[4,3,128,256]{3,2,1,0:T(8,128)(2,1)S(1)}, bf16[4,3,128,256]{3,2,1,0:T(8,128)(2,1)S(1)}, u32[]{:S(2)}, u32[]{:S(2)}) %collective-permute-start.2) | collective-permute-done | bytes 786464 | tf_op jit(solution)/shard_map/ppermute | solution.py:46
  79.5 5.1 %collective-permute-start.12 = (bf16[4,3,128,256]{3,2,1,0:T(8,128)(2,1)S(1)}, bf16[4,3,128,256]{3,2,1,0:T(8,128)(2,1)}, u32[]{:S(2)}, u32[]{:S(2)}) collective-permute-start(bf16[4,3,128,256]{3,2,1,0:T(8,128)(2,1)S(1)} %collective-permute-done.10.refs_12_.refs_11_), channel_id=1, source_target_pairs={{0,448},{64,0},{128,64},{192,128},{256,192},{320,256},{384,320},{4... | collective-permute-start | bytes 2359304 | tf_op jit(solution)/shard_map/ppermute | solution.py:46
  85.5 5.0 %collective-permute-start.5 = (bf16[4,3,128,256]{3,2,1,0:T(8,128)(2,1)}, bf16[4,3,128,256]{3,2,1,0:T(8,128)(2,1)}, u32[]{:S(2)}, u32[]{:S(2)}) collective-permute-start(bf16[4,3,128,256]{3,2,1,0:T(8,128)(2,1)} %collective-permute-done.3.refs_4_), channel_id=1, source_target_pairs={{0,448},{64,0},{128,64},{192,128},{256,192},{320,256},{384,320},{4... | collective-permute-start | bytes 2359304 | tf_op jit(solution)/shard_map/ppermute | solution.py:46
  90.6 1.9 %collective-permute-start.11 = (bf16[4,3,128,256]{3,2,1,0:T(8,128)(2,1)}, bf16[4,3,128,256]{3,2,1,0:T(8,128)(2,1)}, u32[]{:S(2)}, u32[]{:S(2)}) collective-permute-start(bf16[4,3,128,256]{3,2,1,0:T(8,128)(2,1)} %collective-permute-done.9.refs_11_.refs_10_), channel_id=1, source_target_pairs={{0,64},{64,128},{128,192},{192,256},{256,320},{320,384},{384,448},... | collective-permute-start | bytes 2359304 | tf_op jit(solution)/shard_map/ppermute | solution.py:46
  92.5 4.7 %collective-permute-done.4.refs_5_ = bf16[4,3,128,256]{3,2,1,0:T(8,128)(2,1)} collective-permute-done((bf16[4,3,128,256]{3,2,1,0:T(8,128)(2,1)S(1)}, bf16[4,3,128,256]{3,2,1,0:T(8,128)(2,1)}, u32[]{:S(2)}, u32[]{:S(2)}) %collective-permute-start.4) | collective-permute-done | bytes 786464 | tf_op jit(solution)/shard_map/ppermute | solution.py:46
  97.2 1.9 %collective-permute-start.6 = (bf16[4,3,128,256]{3,2,1,0:T(8,128)(2,1)}, bf16[4,3,128,256]{3,2,1,0:T(8,128)(2,1)}, u32[]{:S(2)}, u32[]{:S(2)}) collective-permute-start(bf16[4,3,128,256]{3,2,1,0:T(8,128)(2,1)} %collective-permute-done.4.refs_5_), channel_id=1, source_target_pairs={{0,64},{64,128},{128,192},{192,256},{256,320},{320,384},{384,448},... | collective-permute-start | bytes 2359304 | tf_op jit(solution)/shard_map/ppermute | solution.py:46
  99.2 5.1 %collective-permute-start.13 = (bf16[4,3,128,256]{3,2,1,0:T(8,128)(2,1)}, bf16[4,3,128,256]{3,2,1,0:T(8,128)(2,1)}, u32[]{:S(2)}, u32[]{:S(2)}) collective-permute-start(bf16[4,3,128,256]{3,2,1,0:T(8,128)(2,1)} %collective-permute-done.12.refs_14_.refs_13_), channel_id=1, source_target_pairs={{0,448},{64,0},{128,64},{192,128},{256,192},{320,256},{384,320},{4... | collective-permute-start | bytes 2359304 | tf_op jit(solution)/shard_map/ppermute | solution.py:46
  104.4 2.9 %collect.1.features_ref = bf16[8,8,256,128]{3,2,1,0:T(8,128)(2,1)S(1)} custom-call(s32[4]{0:T(128)S(1)} %pad_add_fusion.meta_ref, bf16[8,256,1024]{2,1,0:T(8,128)(2,1)} %all-to-all-done.pieces_ref), custom_call_target="tpu_custom_call" | custom-call | tf_op jit(solution)/shard_map/collect/pallas_call | solution.py:244
  107.4 5.3 %begin.1.refs_2_ = f32[2,256,256]{2,1,0:T(8,128)S(1)} custom-call(s32[4]{0:T(128)S(1)} %pad_add_fusion.meta_ref, bf16[8,8,256,128]{3,2,1,0:T(8,128)(2,1)S(1)} %collect.1.features_ref, bf16[4,3,128,256]{3,2,1,0:T(8,128)(2,1)} %copy-done.3, bf16[4,3,128,256]{3,2,1,0:T(8,128)(2,1)} %copy-done.4, bf16[4,3,128,256]{3,2,1,0:T(8,128)(2,1)} %copy-done.6, ...), custom_call_target="tpu_custom_call" | custom-call | tf_op jit(solution)/shard_map/begin/pallas_call | solution.py:263
  114.4 2.7 %drive.1 = (f32[2,384,128]{2,1,0:T(8,128)S(1)}, f32[16,256]{1,0:T(8,128)S(1)}) custom-call(s32[4]{0:T(128)S(1)} %pad_add_fusion.meta_ref, bf16[8,8,256,128]{3,2,1,0:T(8,128)(2,1)S(1)} %collect.1.features_ref, bf16[4,3,128,256]{3,2,1,0:T(8,128)(2,1)} %collective-permute-done.6.refs_7_.refs_0_, ...), custom_call_target="tpu_custom_call" | custom-call | tf_op jit(solution)/shard_map/drive/pallas_call | solution.py:273
  117.8 4.7 %all-to-all-start.2 = ((f32[8,16,256]{2,1,0:T(8,128)}), f32[8,16,256]{2,1,0:T(8,128)S(1)}, u32[]{:S(2)}, u32[]{:S(2)}) async-start(f32[8,16,256]{2,1,0:T(8,128)} %broadcast_in_dim.32), calls=%async_computation.2 | async-start | bytes 262144 | tf_op jit(solution)/shard_map/all_to_all | solution.py:41
  122.5 9.1 %all-to-all-done.2 = f32[8,16,256]{2,1,0:T(8,128)S(1)} async-done(((f32[8,16,256]{2,1,0:T(8,128)}), f32[8,16,256]{2,1,0:T(8,128)S(1)}, u32[]{:S(2)}, u32[]{:S(2)}) %all-to-all-start.2) | async-done | bytes 131104 | tf_op jit(solution)/shard_map/all_to_all | solution.py:41
  132.3 6.1 %all-to-all-start.3 = ((f32[8,16,256]{2,1,0:T(8,128)}), f32[8,16,256]{2,1,0:T(8,128)S(1)}, u32[]{:S(2)}, u32[]{:S(2)}) async-start(f32[8,16,256]{2,1,0:T(8,128)} %broadcast_in_dim.33), calls=%async_computation.3 | async-start | bytes 262144 | tf_op jit(solution)/shard_map/all_to_all | solution.py:41
  138.5 2.2 %copy-done.1 = bf16[8,8,256,128]{3,2,1,0:T(8,128)(2,1)S(1)} copy-done((bf16[8,8,256,128]{3,2,1,0:T(8,128)(2,1)S(1)}, bf16[8,8,256,128]{3,2,1,0:T(8,128)(2,1)}, u32[]{:S(2)}) %copy-start.1) | copy-done | bytes 4194328
  140.7 4.6 %query.1.query_ref = bf16[256,256]{1,0:T(8,128)(2,1)S(1)} custom-call(s32[4]{0:T(128)S(1)} %pad_add_fusion.meta_ref, bf16[8,8,256,128]{3,2,1,0:T(8,128)(2,1)S(1)} %copy-done.1, bf16[4,3,128,256]{3,2,1,0:T(8,128)(2,1)} %copy-done.3, bf16[4,3,128,256]{3,2,1,0:T(8,128)(2,1)} %copy-done.4, bf16[4,3,128,256]{3,2,1,0:T(8,128)(2,1)} %copy-done.6, ...), custom_call_target="tpu_custom_call" | custom-call | tf_op jit(solution)/shard_map/query/pallas_call | solution.py:295
  145.3 2.3 %all-to-all-done.3.far_ref = f32[8,16,256]{2,1,0:T(8,128)S(1)} async-done(((f32[8,16,256]{2,1,0:T(8,128)}), f32[8,16,256]{2,1,0:T(8,128)S(1)}, u32[]{:S(2)}, u32[]{:S(2)}) %all-to-all-start.3) | async-done | bytes 131104 | tf_op jit(solution)/shard_map/all_to_all | solution.py:41
  147.6 2.3 %finish.1 = (bf16[256,256]{1,0:T(8,128)(2,1)}, f32[4,16]{1,0:T(4,128)}, f32[1,4]{1,0:T(1,128)}) custom-call(s32[4]{0:T(128)S(1)} %pad_add_fusion.meta_ref, bf16[256,256]{1,0:T(8,128)(2,1)S(1)} %query.1.query_ref, f32[2,384,128]{2,1,0:T(8,128)S(1)} %get-tuple-element.8.local_ref, f32[16,256]{1,0:T(8,128)S(1)} %get-tuple-element.14.rows_in_ref, ...), custom_call_target="tpu_custom_call" | custom-call | tf_op jit(solution)/shard_map/finish/pallas_call | solution.py:304
  (46 shorter events, 6.3 us)
Async XLA Ops:
  2.8 34.9 %all-to-all-start.1 = ((bf16[8,3,128,256]{3,2,1,0:T(8,128)(2,1)}), bf16[8,3,128,256]{3,2,1,0:T(8,128)(2,1)S(1)}, u32[]{:S(2)}, u32[]{:S(2)}) async-start(bf16[8,3,128,256]{3,2,1,0:T(8,128)(2,1)} %copies.3), calls=%async_computation.1 | async-start | bytes 3145728 | tf_op jit(solution)/shard_map/all_to_all | solution.py:227
  16.2 88.2 %copy-start.10 = (f32[256,16]{0,1:T(8,128)S(1)}, f32[256,16]{0,1:T(8,128)}, u32[]{:S(2)}) copy-start(f32[256,16]{0,1:T(8,128)} %param.7) | copy-start | bytes 49156
  16.2 88.2 %copy-start.11 = (f32[256,16]{0,1:T(8,128)S(1)}, f32[256,16]{0,1:T(8,128)}, u32[]{:S(2)}) copy-start(f32[256,16]{0,1:T(8,128)} %param.8) | copy-start | bytes 49156
  16.2 88.2 %copy-start.12 = (f32[256]{0:T(256)S(1)}, f32[256]{0:T(256)}, u32[]{:S(2)}) copy-start(f32[256]{0:T(256)} %param.9) | copy-start | bytes 3076
  37.7 66.8 %all-to-all-start = ((bf16[8,256,1024]{2,1,0:T(8,128)(2,1)}), bf16[8,256,1024]{2,1,0:T(8,128)(2,1)}, u32[]{:S(2)}, u32[]{:S(2)}) async-start(bf16[8,256,1024]{2,1,0:T(8,128)(2,1)} %copies.2), calls=%async_computation | async-start | bytes 8388608 | tf_op jit(solution)/shard_map/all_to_all | solution.py:239
  42.7 64.6 %copy-start.2 = (bf16[4,3,128,256]{3,2,1,0:T(8,128)(2,1)}, bf16[4,3,128,256]{3,2,1,0:T(8,128)(2,1)S(1)}, u32[]{:S(2)}) copy-start(bf16[4,3,128,256]{3,2,1,0:T(8,128)(2,1)S(1)} %get-tuple-element.15.refs_8_.refs_7_) | copy-start | bytes 2359300
  42.7 64.6 %copy-start.3 = (bf16[4,3,128,256]{3,2,1,0:T(8,128)(2,1)}, bf16[4,3,128,256]{3,2,1,0:T(8,128)(2,1)S(1)}, u32[]{:S(2)}) copy-start(bf16[4,3,128,256]{3,2,1,0:T(8,128)(2,1)S(1)} %get-tuple-element.16.refs_0_) | copy-start | bytes 2359300
  42.7 15.3 %collective-permute-start = (bf16[4,3,128,256]{3,2,1,0:T(8,128)(2,1)S(1)}, bf16[4,3,128,256]{3,2,1,0:T(8,128)(2,1)S(1)}, u32[]{:S(2)}, u32[]{:S(2)}) collective-permute-start(bf16[4,3,128,256]{3,2,1,0:T(8,128)(2,1)S(1)} %get-tuple-element.16.refs_0_), channel_id=1, source_target_pairs={{0,64},{64,128},{128,192},{192,256},{256,320},{320,384},{384,448},... | collective-permute-start | bytes 2359304 | tf_op jit(solution)/shard_map/ppermute | solution.py:46
  46.2 13.9 %collective-permute-start.8 = (bf16[4,3,128,256]{3,2,1,0:T(8,128)(2,1)S(1)}, bf16[4,3,128,256]{3,2,1,0:T(8,128)(2,1)S(1)}, u32[]{:S(2)}, u32[]{:S(2)}) collective-permute-start(bf16[4,3,128,256]{3,2,1,0:T(8,128)(2,1)S(1)} %get-tuple-element.15.refs_8_.refs_7_), channel_id=1, source_target_pairs={{0,448},{64,0},{128,64},{192,128},{256,192},{320,256},{384,320},{4... | collective-permute-start | bytes 2359304 | tf_op jit(solution)/shard_map/ppermute | solution.py:46
  50.1 18.5 %collective-permute-start.1 = (bf16[4,3,128,256]{3,2,1,0:T(8,128)(2,1)S(1)}, bf16[4,3,128,256]{3,2,1,0:T(8,128)(2,1)S(1)}, u32[]{:S(2)}, u32[]{:S(2)}) collective-permute-start(bf16[4,3,128,256]{3,2,1,0:T(8,128)(2,1)S(1)} %get-tuple-element.16.refs_0_), channel_id=1, source_target_pairs={{0,448},{64,0},{128,64},{192,128},{256,192},{320,256},{384,320},{4... | collective-permute-start | bytes 2359304 | tf_op jit(solution)/shard_map/ppermute | solution.py:46
  54.0 19.6 %collective-permute-start.7 = (bf16[4,3,128,256]{3,2,1,0:T(8,128)(2,1)S(1)}, bf16[4,3,128,256]{3,2,1,0:T(8,128)(2,1)S(1)}, u32[]{:S(2)}, u32[]{:S(2)}) collective-permute-start(bf16[4,3,128,256]{3,2,1,0:T(8,128)(2,1)S(1)} %get-tuple-element.15.refs_8_.refs_7_), channel_id=1, source_target_pairs={{0,64},{64,128},{128,192},{192,256},{256,320},{320,384},{384,448},... | collective-permute-start | bytes 2359304 | tf_op jit(solution)/shard_map/ppermute | solution.py:46
  58.1 49.2 %copy-start.4 = (bf16[4,3,128,256]{3,2,1,0:T(8,128)(2,1)}, bf16[4,3,128,256]{3,2,1,0:T(8,128)(2,1)S(1)}, u32[]{:S(2)}) copy-start(bf16[4,3,128,256]{3,2,1,0:T(8,128)(2,1)S(1)} %collective-permute-done.refs_1_) | copy-start | bytes 2359300
  58.1 19.4 %collective-permute-start.2 = (bf16[4,3,128,256]{3,2,1,0:T(8,128)(2,1)S(1)}, bf16[4,3,128,256]{3,2,1,0:T(8,128)(2,1)S(1)}, u32[]{:S(2)}, u32[]{:S(2)}) collective-permute-start(bf16[4,3,128,256]{3,2,1,0:T(8,128)(2,1)S(1)} %collective-permute-done.refs_1_), channel_id=1, source_target_pairs={{0,64},{64,128},{128,192},{192,256},{256,320},{320,384},{384,448},... | collective-permute-start | bytes 2359304 | tf_op jit(solution)/shard_map/ppermute | solution.py:46
  60.1 47.2 %copy-start.5 = (bf16[4,3,128,256]{3,2,1,0:T(8,128)(2,1)}, bf16[4,3,128,256]{3,2,1,0:T(8,128)(2,1)S(1)}, u32[]{:S(2)}) copy-start(bf16[4,3,128,256]{3,2,1,0:T(8,128)(2,1)S(1)} %collective-permute-done.8.refs_10_.refs_9_) | copy-start | bytes 2359300
  60.1 19.3 %collective-permute-start.10 = (bf16[4,3,128,256]{3,2,1,0:T(8,128)(2,1)S(1)}, bf16[4,3,128,256]{3,2,1,0:T(8,128)(2,1)S(1)}, u32[]{:S(2)}, u32[]{:S(2)}) collective-permute-start(bf16[4,3,128,256]{3,2,1,0:T(8,128)(2,1)S(1)} %collective-permute-done.8.refs_10_.refs_9_), channel_id=1, source_target_pairs={{0,448},{64,0},{128,64},{192,128},{256,192},{320,256},{384,320},{4... | collective-permute-start | bytes 2359304 | tf_op jit(solution)/shard_map/ppermute | solution.py:46
  68.6 10.9 %copy-start.6 = (bf16[4,3,128,256]{3,2,1,0:T(8,128)(2,1)}, bf16[4,3,128,256]{3,2,1,0:T(8,128)(2,1)S(1)}, u32[]{:S(2)}) copy-start(bf16[4,3,128,256]{3,2,1,0:T(8,128)(2,1)S(1)} %collective-permute-done.1.refs_2_) | copy-start | bytes 2359300
  68.6 17.0 %collective-permute-start.3 = (bf16[4,3,128,256]{3,2,1,0:T(8,128)(2,1)S(1)}, bf16[4,3,128,256]{3,2,1,0:T(8,128)(2,1)}, u32[]{:S(2)}, u32[]{:S(2)}) collective-permute-start(bf16[4,3,128,256]{3,2,1,0:T(8,128)(2,1)S(1)} %collective-permute-done.1.refs_2_), channel_id=1, source_target_pairs={{0,448},{64,0},{128,64},{192,128},{256,192},{320,256},{384,320},{4... | collective-permute-start | bytes 2359304 | tf_op jit(solution)/shard_map/ppermute | solution.py:46
  73.6 11.9 %copy-start.7 = (bf16[4,3,128,256]{3,2,1,0:T(8,128)(2,1)}, bf16[4,3,128,256]{3,2,1,0:T(8,128)(2,1)S(1)}, u32[]{:S(2)}) copy-start(bf16[4,3,128,256]{3,2,1,0:T(8,128)(2,1)S(1)} %collective-permute-done.7.refs_9_.refs_8_) | copy-start | bytes 2359300
  73.6 16.9 %collective-permute-start.9 = (bf16[4,3,128,256]{3,2,1,0:T(8,128)(2,1)S(1)}, bf16[4,3,128,256]{3,2,1,0:T(8,128)(2,1)}, u32[]{:S(2)}, u32[]{:S(2)}) collective-permute-start(bf16[4,3,128,256]{3,2,1,0:T(8,128)(2,1)S(1)} %collective-permute-done.7.refs_9_.refs_8_), channel_id=1, source_target_pairs={{0,64},{64,128},{128,192},{192,256},{256,320},{320,384},{384,448},... | collective-permute-start | bytes 2359304 | tf_op jit(solution)/shard_map/ppermute | solution.py:46
  77.5 13.0 %copy-start.8 = (bf16[4,3,128,256]{3,2,1,0:T(8,128)(2,1)}, bf16[4,3,128,256]{3,2,1,0:T(8,128)(2,1)S(1)}, u32[]{:S(2)}) copy-start(bf16[4,3,128,256]{3,2,1,0:T(8,128)(2,1)S(1)} %collective-permute-done.2.refs_3_) | copy-start | bytes 2359300
  77.5 19.7 %collective-permute-start.4 = (bf16[4,3,128,256]{3,2,1,0:T(8,128)(2,1)S(1)}, bf16[4,3,128,256]{3,2,1,0:T(8,128)(2,1)}, u32[]{:S(2)}, u32[]{:S(2)}) collective-permute-start(bf16[4,3,128,256]{3,2,1,0:T(8,128)(2,1)S(1)} %collective-permute-done.2.refs_3_), channel_id=1, source_target_pairs={{0,64},{64,128},{128,192},{192,256},{256,320},{320,384},{384,448},... | collective-permute-start | bytes 2359304 | tf_op jit(solution)/shard_map/ppermute | solution.py:46
  79.5 17.8 %copy-start.9 = (bf16[4,3,128,256]{3,2,1,0:T(8,128)(2,1)}, bf16[4,3,128,256]{3,2,1,0:T(8,128)(2,1)S(1)}, u32[]{:S(2)}) copy-start(bf16[4,3,128,256]{3,2,1,0:T(8,128)(2,1)S(1)} %collective-permute-done.10.refs_12_.refs_11_) | copy-start | bytes 2359300
  79.5 19.7 %collective-permute-start.12 = (bf16[4,3,128,256]{3,2,1,0:T(8,128)(2,1)S(1)}, bf16[4,3,128,256]{3,2,1,0:T(8,128)(2,1)}, u32[]{:S(2)}, u32[]{:S(2)}) collective-permute-start(bf16[4,3,128,256]{3,2,1,0:T(8,128)(2,1)S(1)} %collective-permute-done.10.refs_12_.refs_11_), channel_id=1, source_target_pairs={{0,448},{64,0},{128,64},{192,128},{256,192},{320,256},{384,320},{4... | collective-permute-start | bytes 2359304 | tf_op jit(solution)/shard_map/ppermute | solution.py:46
  85.5 21.8 %collective-permute-start.5 = (bf16[4,3,128,256]{3,2,1,0:T(8,128)(2,1)}, bf16[4,3,128,256]{3,2,1,0:T(8,128)(2,1)}, u32[]{:S(2)}, u32[]{:S(2)}) collective-permute-start(bf16[4,3,128,256]{3,2,1,0:T(8,128)(2,1)} %collective-permute-done.3.refs_4_), channel_id=1, source_target_pairs={{0,448},{64,0},{128,64},{192,128},{256,192},{320,256},{384,320},{4... | collective-permute-start | bytes 2359304 | tf_op jit(solution)/shard_map/ppermute | solution.py:46
  90.6 16.8 %collective-permute-start.11 = (bf16[4,3,128,256]{3,2,1,0:T(8,128)(2,1)}, bf16[4,3,128,256]{3,2,1,0:T(8,128)(2,1)}, u32[]{:S(2)}, u32[]{:S(2)}) collective-permute-start(bf16[4,3,128,256]{3,2,1,0:T(8,128)(2,1)} %collective-permute-done.9.refs_11_.refs_10_), channel_id=1, source_target_pairs={{0,64},{64,128},{128,192},{192,256},{256,320},{320,384},{384,448},... | collective-permute-start | bytes 2359304 | tf_op jit(solution)/shard_map/ppermute | solution.py:46
  97.2 17.2 %collective-permute-start.6 = (bf16[4,3,128,256]{3,2,1,0:T(8,128)(2,1)}, bf16[4,3,128,256]{3,2,1,0:T(8,128)(2,1)}, u32[]{:S(2)}, u32[]{:S(2)}) collective-permute-start(bf16[4,3,128,256]{3,2,1,0:T(8,128)(2,1)} %collective-permute-done.4.refs_5_), channel_id=1, source_target_pairs={{0,64},{64,128},{128,192},{192,256},{256,320},{320,384},{384,448},... | collective-permute-start | bytes 2359304 | tf_op jit(solution)/shard_map/ppermute | solution.py:46
  99.2 15.2 %collective-permute-start.13 = (bf16[4,3,128,256]{3,2,1,0:T(8,128)(2,1)}, bf16[4,3,128,256]{3,2,1,0:T(8,128)(2,1)}, u32[]{:S(2)}, u32[]{:S(2)}) collective-permute-start(bf16[4,3,128,256]{3,2,1,0:T(8,128)(2,1)} %collective-permute-done.12.refs_14_.refs_13_), channel_id=1, source_target_pairs={{0,448},{64,0},{128,64},{192,128},{256,192},{320,256},{384,320},{4... | collective-permute-start | bytes 2359304 | tf_op jit(solution)/shard_map/ppermute | solution.py:46
  107.3 7.1 %copy-start = (bf16[8,8,256,128]{3,2,1,0:T(8,128)(2,1)}, bf16[8,8,256,128]{3,2,1,0:T(8,128)(2,1)S(1)}, u32[]{:S(2)}) copy-start(bf16[8,8,256,128]{3,2,1,0:T(8,128)(2,1)S(1)} %collect.1.features_ref) | copy-start | bytes 12582916
  117.8 13.8 %all-to-all-start.2 = ((f32[8,16,256]{2,1,0:T(8,128)}), f32[8,16,256]{2,1,0:T(8,128)S(1)}, u32[]{:S(2)}, u32[]{:S(2)}) async-start(f32[8,16,256]{2,1,0:T(8,128)} %broadcast_in_dim.32), calls=%async_computation.2 | async-start | bytes 262144 | tf_op jit(solution)/shard_map/all_to_all | solution.py:41
  132.3 15.2 %all-to-all-start.3 = ((f32[8,16,256]{2,1,0:T(8,128)}), f32[8,16,256]{2,1,0:T(8,128)S(1)}, u32[]{:S(2)}, u32[]{:S(2)}) async-start(f32[8,16,256]{2,1,0:T(8,128)} %broadcast_in_dim.33), calls=%async_computation.3 | async-start | bytes 262144 | tf_op jit(solution)/shard_map/all_to_all | solution.py:41
  138.5 2.2 %copy-start.1 = (bf16[8,8,256,128]{3,2,1,0:T(8,128)(2,1)S(1)}, bf16[8,8,256,128]{3,2,1,0:T(8,128)(2,1)}, u32[]{:S(2)}) copy-start(bf16[8,8,256,128]{3,2,1,0:T(8,128)(2,1)} %copy-done) | copy-start | bytes 12582916
